TPU v7x, 32 devices: a whole 2x2x4 slice. The times are simulated.
32 devices in a mesh: row: 8 (over y, x, core), col: 4 (over z).
Axes of the slice: x: 2, y: 2, z: 4, core: 2. Of those that a mesh axis runs over, the one named last changes fastest.
Arguments:
- tokens: bfloat16 [512, 8192], P('col', 'row'), may hold values from -6 to 6
- w_packed: bfloat16 [8, 4, 448, 128, 128], P('row', 'col'), may hold values from -0.09375 to 0.09375
- kept_rows: int32 [8, 4, 448], P('row', 'col'), may hold values from 0 to 7, as said below
- kept_cols: int32 [8, 4, 448], P('row', 'col'), may hold values from 0 to 55, as said below
- kept_count: int32 [8, 4], P('row', 'col'), may hold values from 1 to 448, as said below
- grad_act: bfloat16 [512, 28672], P('row', 'col'), may hold values from -6 to 6
Outputs:
- activation: bfloat16 [512, 28672], P('row', 'col')
- input_grad: bfloat16 [512, 8192], P('col', 'row')
- weight_grad: bfloat16 [8, 4, 448, 128, 128], P('row', 'col')
Inputs may be any that keep to these rules, and one draw needn't show every extreme that they name: Within each tile, the 448 slots name every block of the tile once (kept_rows[r, c, s] * 56 + kept_cols[r, c, s] runs over all block places). `kept_cols`: see kept_rows. `kept_count`: some tile in every draw keeps all 448 blocks.
All inputs are finite; a program needn't handle non-finite values.
Results may differ from a plain program's by a relative error of at most 0.0049.
Values may be sent and summed in bfloat16 or wider, within the bound.
No kernel may reach another device: no remote copies, remote signals or barrier semaphores. Data moves between devices by JAX's collectives and lax.ppermute only.
A program may use at most 384 MiB of HBM per device.

v0:
```python
import functools

import jax
import jax.numpy as jnp
import numpy as np
from jax import lax
from jax.experimental import pallas as pl
from jax.experimental.pallas import tpu as pltpu
from jax.sharding import PartitionSpec as P

gelu_scale = 0.7978845608
gelu_cubic = 0.044715
token_split = (1, 1)
column_parts = 2
vmem_limit = 16 * 1024 * 1024
in_vmem = pl.BlockSpec(memory_space=pltpu.VMEM)
in_smem = pl.BlockSpec(memory_space=pltpu.SMEM)
anywhere = pl.BlockSpec(memory_space=pltpu.HBM)


def gelu_pair(hidden, cotangent):
    inner = gelu_scale * (hidden + gelu_cubic * hidden * hidden * hidden)
    tangent = jnp.tanh(inner)
    activation = (0.5 * hidden * (1.0 + tangent)).astype(jnp.bfloat16)
    slope = 0.5 * (1.0 + tangent) + 0.5 * hidden * (1.0 - tangent * tangent) * gelu_scale * (
        1.0 + 3.0 * gelu_cubic * hidden * hidden
    )
    slope_grad = (cotangent.astype(jnp.float32) * slope).astype(jnp.bfloat16)
    return (activation, slope_grad)


def group_of(blocks, goal):
    return max(n for n in range(1, goal + 1) if blocks % n == 0)


class Core:
    def __init__(self):
        self.turn = None

    def __call__(self, kernel, name, out_shape, out_specs, in_specs, operands, scratch=(), aliases=None):
        homes = {id(in_vmem): pltpu.VMEM, id(anywhere): pltpu.HBM}
        in_specs, operands = list(in_specs), list(operands)
        if self.turn is not None:
            in_specs.append(in_vmem)
            operands.append(self.turn)
        taken = len(operands)
        given = len(out_shape)
        extra = self.turn is not None

        def body(*refs):
            refs[taken + given][...] = jnp.zeros((8, 128), jnp.float32)
            kernel(*refs[: taken - extra], *refs[taken : taken + given], *refs[taken + given + 1 :])

        placed = [
            pltpu.with_memory_space_constraint(x, homes[id(spec)]) if id(spec) in homes else x
            for x, spec in zip(operands, in_specs)
        ]
        *out, self.turn = pl.pallas_call(
            body,
            out_shape=[*out_shape, pltpu.VMEM((8, 128), jnp.float32)],
            in_specs=in_specs,
            out_specs=[*out_specs, in_vmem],
            scratch_shapes=list(scratch),
            input_output_aliases=aliases or {},
            compiler_params=pltpu.CompilerParams(vmem_limit_bytes=vmem_limit),
            cost_estimate=pl.CostEstimate(flops=1, transcendentals=0, bytes_accessed=1),
            name=name,
        )(*placed)
        return out


def dense_kernel(row_blocks, col_blocks, code, w_ref, *refs):
    out_ref, empty, sem = refs[-3:]
    blk = w_ref.shape[-1]
    empty[...] = jnp.zeros_like(empty)

    def load(at, carry):
        for r in range(row_blocks):
            entry = code[r * col_blocks + at]
            start = pl.multiple_of(at * blk, blk)
            target = out_ref.at[pl.ds(r * blk, blk), pl.ds(start, blk)]

            @pl.when(lax.rem(entry, 2) == 1)
            def _():
                pltpu.make_async_copy(w_ref.at[0, 0, lax.div(entry, 2)], target, sem).start()

            @pl.when(lax.rem(entry, 2) == 0)
            def _():
                pltpu.make_async_copy(empty, target, sem).start()

        return carry

    lax.fori_loop(0, col_blocks, load, 0)
    pltpu.make_async_copy(out_ref, out_ref, sem).wait()


def dense_tile(core, w_packed, code, row_blocks, col_blocks, ready):
    blk = w_packed.shape[-1]
    [weight] = core(
        functools.partial(dense_kernel, row_blocks, col_blocks),
        "dense_tile",
        [pltpu.VMEM((row_blocks * blk, col_blocks * blk), w_packed.dtype)],
        [in_vmem],
        [in_smem, anywhere] + [in_smem] * len(ready),
        (code, w_packed, *ready),
        scratch=[pltpu.VMEM((blk, blk), w_packed.dtype), pltpu.SemaphoreType.DMA],
    )
    return weight


def arrange_kernel(groups, rows, pieces, pick, *refs):
    out_ref, turned_ref, all_ref = refs[pieces:]
    each = groups // pieces
    for m in range(pieces):
        for j in range(each):
            all_ref[m * each + j] = refs[m][j]
    for t in range(groups):
        out_ref[pl.ds(t * rows, rows), :] = all_ref[pick[t]]
    turned_ref[...] = out_ref[...].T


def arrange(core, pieces, pick):
    groups = pick.shape[0]
    rows, tall = pieces[0].shape[1:]
    kind = pieces[0].dtype
    return core(
        functools.partial(arrange_kernel, groups, rows, len(pieces)),
        "arrange",
        [pltpu.VMEM((groups * rows, tall), kind), pltpu.VMEM((tall, groups * rows), kind)],
        [in_vmem, in_vmem],
        [in_smem] + [in_vmem] * len(pieces),
        (pick, *pieces),
        scratch=[pltpu.VMEM((groups, rows, tall), kind)],
    )


def forward_kernel(first, wide, x_ref, w_ref, keep_ref, send_ref):
    half, width = keep_ref.shape
    for at in range(0, width, wide):
        product = jnp.dot(
            x_ref[...], w_ref[:, first + at : first + at + wide], preferred_element_type=jnp.float32
        )
        keep_ref[:, at : at + wide] = product[:half]
        send_ref[:, at : at + wide] = product[half:].astype(jnp.bfloat16)


def forward(core, features, weight, first, width):
    half = features.shape[0] // 2
    wide = 128 * group_of(width // 128, 4)
    return core(
        functools.partial(forward_kernel, first, wide),
        "forward",
        [pltpu.VMEM((half, width), jnp.float32), pltpu.VMEM((half, width), jnp.bfloat16)],
        [in_vmem, in_vmem],
        [in_vmem, in_vmem],
        (features, weight),
    )


def sides(left, bit):
    at = len(left) - 1 - left.index(bit)
    names = range(1 << len(left))
    return [g for g in names if not g >> at & 1], [g for g in names if g >> at & 1]


def add_kernel(rows, stay, leave, keep_ref, arrived_ref, next_ref, send_ref):
    for out_ref, groups in ((next_ref, stay), (send_ref, leave)):
        for at, g in enumerate(groups):
            here = slice(g * rows, (g + 1) * rows)
            total = keep_ref[here, :] + arrived_ref[here, :].astype(jnp.float32)
            out_ref[at * rows : (at + 1) * rows, :] = total.astype(out_ref.dtype)


def add_step(core, keep, arrived, left, bit):
    rows = keep.shape[0] >> len(left)
    half = (keep.shape[0] // 2, keep.shape[1])
    return core(
        functools.partial(add_kernel, rows, *sides(left, bit)),
        "add_step",
        [pltpu.VMEM(half, jnp.float32), pltpu.VMEM(half, jnp.bfloat16)],
        [in_vmem, in_vmem],
        [in_vmem, in_vmem],
        (keep, arrived),
    )


def join_kernel(rows, stay, come, near_ref, arrived_ref, out_ref):
    for in_ref, groups in ((near_ref, stay), (arrived_ref, come)):
        for at, g in enumerate(groups):
            out_ref[g * rows : (g + 1) * rows, :] = in_ref[at * rows : (at + 1) * rows, :]


def join_step(core, near, arrived, held, bit):
    rows = 2 * near.shape[0] >> len(held)
    [out] = core(
        functools.partial(join_kernel, rows, *sides(held, bit)),
        "join_step",
        [pltpu.VMEM((2 * near.shape[0], near.shape[1]), near.dtype)],
        [in_vmem],
        [in_vmem, in_vmem],
        (near, arrived),
    )
    return out


def gelu_kernel(top, first, keep_ref, arrived_ref, cotangent_ref, activation_ref, slope_ref):
    rows, width = keep_ref.shape
    hidden = keep_ref[...] + arrived_ref[...].astype(jnp.float32)
    cotangent = cotangent_ref[top : top + rows, first : first + width]
    activation_ref[...], slope_ref[...] = gelu_pair(hidden, cotangent)


def gelu(core, keep, arrived, cotangent, top, first):
    out = pltpu.VMEM(keep.shape, jnp.bfloat16)
    return core(
        functools.partial(gelu_kernel, top, first),
        "gelu",
        [out, out],
        [in_vmem, in_vmem],
        [in_vmem] * 3,
        (keep, arrived, cotangent),
    )


def input_kernel(first, groups, has_before, finished, given, place, near_ref, far_ref, w_ref, *refs):
    half, width = near_ref.shape
    rows = 2 * half // groups
    tall = w_ref.shape[0]
    before = refs[0] if has_before else None
    outs = refs[has_before : has_before + given]
    scratch = refs[has_before + given :]
    turned = scratch[0]
    total = scratch[1] if finished else outs[0]
    wide = 128 * group_of(width // 128, 4)
    for at in range(0, width, wide):
        here = slice(at, at + wide)
        grad = jnp.concatenate([near_ref[:, here], far_ref[:, here]], axis=0)
        turned[here, :] = grad.T
    high = 128 * group_of(tall // 128, 4)
    for at in range(0, tall, high):
        here = slice(at, at + high)
        product = jnp.dot(
            w_ref[here, first : first + width], turned[...], preferred_element_type=jnp.float32
        )
        total[here, :] = product + before[here, :] if has_before else product
    if finished:
        upright = scratch[2]
        upright[...] = total[...].T
        each = groups // given
        for i in range(groups):
            start = pl.multiple_of(place[i] * rows, rows)
            out_ref = outs[i // each]
            at = i % each * rows
            out_ref[at : at + rows, :] = upright[pl.ds(start, rows), :].astype(out_ref.dtype)


def input_partial(core, near, far, weight, first, place, before, pieces):
    half, width = near.shape
    tall = weight.shape[0]
    both = 2 * half
    if pieces:
        outs = [pltpu.VMEM((both // pieces, tall), jnp.float32)]
        outs += [pltpu.VMEM((both // pieces, tall), jnp.bfloat16)] * (pieces - 1)
    else:
        outs = [pltpu.VMEM((tall, both), jnp.float32)]
    has_before = before is not None
    scratch = [pltpu.VMEM((width, both), near.dtype)]
    if pieces:
        scratch += [pltpu.VMEM((tall, both), jnp.float32), pltpu.VMEM((both, tall), jnp.float32)]
    return core(
        functools.partial(
            input_kernel, first, place.shape[0], has_before, pieces > 0, len(outs)
        ),
        "input_partial",
        outs,
        [in_vmem] * len(outs),
        [in_smem] + [in_vmem] * (4 if has_before else 3),
        (place, near, far, weight) + ((before,) if has_before else ()),
        scratch=scratch,
    )


def weight_kernel(row_blocks, col_blocks, first, parts, has_before, code, *refs):
    turned = refs[:parts]
    grads = refs[parts : 3 * parts]
    out_ref, made, sem = refs[3 * parts + has_before :]
    blk = made.shape[-1]
    width = grads[0].shape[1]
    here = width // blk
    per_step = group_of(here, 2)
    wide = per_step * blk
    for j in range(here // per_step):
        features = jnp.concatenate([t[...] for t in turned], axis=1)
        grad = jnp.concatenate([g[:, j * wide : (j + 1) * wide] for g in grads], axis=0)
        product = jnp.dot(features, grad, preferred_element_type=jnp.float32)
        for r in range(row_blocks):
            for c in range(per_step):
                entry = code[r * col_blocks + first // blk + j * per_step + c]
                live = lax.rem(entry, 2).astype(jnp.float32)
                at = (j * row_blocks + r) * per_step + c
                block = product[r * blk : (r + 1) * blk, c * blk : (c + 1) * blk] * live
                made[at] = block.astype(made.dtype)
                pltpu.make_async_copy(
                    made.at[at], out_ref.at[0, 0, lax.div(entry, 2)], sem
                ).start(priority=at % 2)
    pltpu.make_async_copy(made, out_ref.at[0, 0, pl.ds(0, made.shape[0])], sem).wait()


def weight_gradient(core, turned, grads, code, first, row_blocks, col_blocks, blk, before):
    parts = len(turned)
    has_before = before is not None
    here = row_blocks * grads[0].shape[1] // blk
    arrays = [*turned, *grads]
    [out] = core(
        functools.partial(weight_kernel, row_blocks, col_blocks, first, parts, has_before),
        "weight_gradient",
        [jax.ShapeDtypeStruct((1, 1, row_blocks * col_blocks, blk, blk), jnp.bfloat16)],
        [anywhere],
        [in_smem] + [in_vmem] * len(arrays) + [anywhere] * has_before,
        (code, *arrays) + ((before,) if has_before else ()),
        scratch=[pltpu.VMEM((here, blk, blk), jnp.bfloat16), pltpu.SemaphoreType.DMA],
        aliases={1 + len(arrays): 0} if has_before else None,
    )
    return out


def place_kernel(spots, *refs):
    blocks = refs[: len(spots)]
    out_ref, sems = refs[len(spots) :]
    copies = []
    for at, (top, first) in enumerate(spots):
        rows, width = blocks[at].shape
        target = out_ref.at[pl.ds(top, rows), pl.ds(first, width)]
        copies.append(pltpu.make_async_copy(blocks[at], target, sems.at[at]))
        copies[-1].start()
    for copy in copies:
        copy.wait()


def place_activation(core, blocks, spots, shape):
    [out] = core(
        functools.partial(place_kernel, spots),
        "place_activation",
        [jax.ShapeDtypeStruct(shape, jnp.bfloat16)],
        [anywhere],
        [in_vmem] * len(blocks),
        blocks,
        scratch=[pltpu.SemaphoreType.DMA((len(blocks),))],
    )
    return out


def total_kernel(each, many, starts, sizes, *refs):
    out_ref = refs[-1]
    own = sum(sizes)
    for k, (start, rows) in enumerate(zip(starts, sizes)):
        found = refs[k * many : (k + 1) * many]
        for j in range(each):
            here = slice(j * rows, (j + 1) * rows)
            total = found[0][here, :]
            for piece in found[1:]:
                total = total + piece[here, :].astype(jnp.float32)
            top = j * own + start
            out_ref[top : top + rows, :] = total.astype(jnp.bfloat16)


def total_input(core, found, each, starts, sizes):
    arrays = [x for part in found for x in part]
    shape = (each * sum(sizes), arrays[0].shape[1])
    [out] = core(
        functools.partial(total_kernel, each, len(found[0]), starts, sizes),
        "total_input",
        [jax.ShapeDtypeStruct(shape, jnp.bfloat16)],
        [pl.BlockSpec(shape, lambda: (0, 0))],
        [in_vmem] * len(arrays),
        arrays,
    )
    return out


def swap(array, axis, size, bit):
    return lax.ppermute(array, axis, [(i, i ^ bit) for i in range(size)])


def on_device(tokens, w_packed, kept_rows, kept_cols, kept_count, grad_act):
    blk = w_packed.shape[-1]
    slot_count = w_packed.shape[2]
    tall = tokens.shape[1]
    row_tokens, hidden_here = grad_act.shape
    row_blocks = tall // blk
    col_blocks = hidden_here // blk
    n_row = lax.axis_size("row")
    n_col = lax.axis_size("col")
    row_me = lax.axis_index("row")
    col_me = lax.axis_index("col")
    col_groups = tokens.shape[0] // row_tokens
    tiles = row_tokens // 16
    shares = token_split if tiles % sum(token_split) == 0 else (1,)
    sizes = [16 * (tiles // sum(shares)) * share for share in shares]
    starts = [sum(sizes[:k]) for k in range(len(sizes))]
    parts = len(sizes)
    slabs = group_of(col_blocks, column_parts)
    width = hidden_here // slabs
    direct = n_col <= 8
    core = Core()

    places = kept_rows[0, 0] * col_blocks + kept_cols[0, 0]
    slots = jnp.arange(slot_count, dtype=jnp.int32)
    coded = slots * 2 + (slots < kept_count[0, 0]).astype(jnp.int32)
    code = jnp.sum(jnp.where(places[None, :] == slots[:, None], coded[None, :], 0), axis=1)

    apart = row_me ^ (col_me * col_groups) if direct else row_me
    everyone = np.arange(n_row)
    order = np.concatenate([everyone[::2], everyone[1::2]]).astype(np.int32)
    pick = (jnp.asarray(order) ^ apart).astype(jnp.int32)
    distance = jnp.asarray(everyone.astype(np.int32)) ^ apart
    place = ((distance & 1) * (n_row // 2) + (distance >> 1)).astype(jnp.int32)

    pieces = []
    for start, rows in zip(starts, sizes):
        mine = tokens.reshape(col_groups, row_tokens, tall)[:, start : start + rows]
        if direct:
            pieces.append([mine] + [swap(mine, "col", n_col, m) for m in range(1, n_col)])
        else:
            pieces.append([lax.all_gather(mine, "col", axis=0, tiled=True)])
    weight = dense_tile(core, w_packed, code, row_blocks, col_blocks, [pick, place])

    far_bits = [1 << b for b in range(1, n_row.bit_length() - 1)]
    units = [(k, c) for k in range(parts) for c in range(slabs)]
    paths = [far_bits if at % 2 == 0 else far_bits[::-1] for at in range(len(units))]
    state = {}
    full, turned = {}, {}
    activations, sums, input_grads = {}, {}, {}

    def begin(k, c, path):
        if c == 0:
            full[k], turned[k] = arrange(core, pieces[k], pick)
        keep, send = forward(core, full[k], weight, c * width, width)
        state[k, c] = (keep, swap(send, "row", n_row, 1))

    def add(at, k, c, path):
        left = sorted(path[at:], reverse=True)
        keep, send = add_step(core, *state[k, c], left, path[at])
        state[k, c] = (keep, swap(send, "row", n_row, path[at]))

    def bend(k, c, path):
        activations[k, c], near = gelu(core, *state[k, c], grad_act, starts[k], c * width)
        state[k, c] = (near, swap(near, "row", n_row, ([1] + path)[-1]))

    def join(at, k, c, path):
        held = sorted(path[at:], reverse=True)
        near = join_step(core, *state[k, c], held, path[at])
        state[k, c] = (near, swap(near, "row", n_row, ([1] + path)[at]))

    def finish(k, c, path):
        last = c + 1 == slabs
        cut = (n_col if direct else 1) * last
        found = input_partial(
            core, *state[k, c], weight, c * width, place, sums.get((k, c - 1)), cut
        )
        sums[k, c] = found[0]
        if last and direct:
            input_grads[k] = [found[0]]
            input_grads[k] += [swap(found[m], "col", n_col, m) for m in range(1, n_col)]
        elif last:
            total = found[0].reshape(n_col, col_groups * sizes[k], tall)
            total = lax.psum_scatter(total, "col", scatter_dimension=0, tiled=True)[0]
            input_grads[k] = [total]

    hops = len(far_bits)
    stages = [begin] + [functools.partial(add, at) for at in range(hops)] + [bend]
    stages += [functools.partial(join, at) for at in reversed(range(hops))] + [finish]
    plan = [(k, at) for at in range(len(stages)) for k in range(parts)]
    if parts == 2 and hops == 2:
        plan = [(0, 0), (0, 1), (0, 2), (1, 0), (1, 1), (0, 3), (0, 4), (1, 2), (0, 5), (1, 3), (1, 4), (0, 6), (1, 5), (1, 6)]
    for k, at in plan:
        for c in range(slabs):
            stages[at](k, c, paths[units.index((k, c))])
        if (k, at) == (parts - 1, len(stages) - 3):
            activation = place_activation(
                core,
                [activations[k, c] for k, c in units],
                [(starts[k], c * width) for k, c in units],
                grad_act.shape,
            )
    weight_grad = None
    for c in range(slabs):
        weight_grad = weight_gradient(
            core,
            [turned[k] for k in range(parts)],
            [g for k in range(parts) for g in state[k, c]],
            code,
            c * width,
            row_blocks,
            col_blocks,
            blk,
            weight_grad,
        )
    input_grad = total_input(
        core, [input_grads[k] for k in range(parts)], col_groups, starts, sizes
    )
    return (activation, input_grad, weight_grad)


def solution(mesh):
    placed = (
        P("col", "row"),
        P("row", "col", None, None, None),
        P("row", "col", None),
        P("row", "col", None),
        P("row", "col"),
        P("row", "col"),
    )
    return jax.shard_map(
        on_device,
        mesh=mesh,
        in_specs=placed,
        out_specs=(P("row", "col"), P("col", "row"), P("row", "col", None, None, None)),
        check_vma=False,
    )
```

profile of v0, /device:TPU:0, one launch (start us, length us, event | category | flops | bytes accessed | tf_op | source)
XLA Modules:
  0.0 132.8 jit_solution(2799783627746706704)
XLA Ops:
  1.6 5.1 %collective-permute-start.2 = (bf16[2,32,1024]{2,1,0:T(8,128)(2,1)S(1)}, bf16[2,32,1024]{2,1,0:T(8,128)(2,1)S(1)}, u32[]{:S(2)}, u32[]{:S(2)}) collective-permute-start(bf16[2,32,1024]{2,1,0:T(8,128)(2,1)S(1)} %get-tuple-element.190.refs_1_), channel_id=1, source_target_pairs={{0,3},{1,2},{2,1},{3,0},{4,7},{5,6},{6,5},{7,4},{8,11},{9,10},{10,... | collective-permute-start | bytes 393224 | tf_op jit(solution)/shard_map/ppermute | solution.py:382
  9.6 7.2 %dense_tile.1 = (bf16[1024,7168]{1,0:T(8,128)(2,1)S(1)}, f32[8,128]{1,0:T(8,128)S(1)}) custom-call(s32[448]{0:T(512)S(1)} %select_reduce_fusion.refs_0_, bf16[1,1,448,128,128]{4,3,2,1,0:T(8,128)(2,1)} %refs_1_.1, s32[8]{0:T(128)S(1)} %broadcast_xor_fusion.refs_2_.refs_0_, s32[8]{0:T(128)S(1)} %shift-right-arithmetic_add_fusion.refs_3_.refs_0_), custom_call_target="tpu_custom_call" | custom-call | flops 1 | bytes 1 | tf_op jit(solution)/shard_map/dense_tile/pallas_call | solution.py:58
  18.6 2.1 %forward.4 = (f32[128,3584]{1,0:T(8,128)S(1)}, bf16[128,3584]{1,0:T(8,128)(2,1)S(1)}, f32[8,128]{1,0:T(8,128)S(1)}) custom-call(bf16[256,1024]{1,0:T(8,128)(2,1)S(1)} %get-tuple-element.97.refs_0_, bf16[1024,7168]{1,0:T(8,128)(2,1)S(1)} %get-tuple-element.98.refs_1_.refs_3_, f32[8,128]{1,0:T(8,128)S(1)} %get-tuple-element.99.refs_2_), custom_call_target="tpu_custom_call" | custom-call | flops 1 | bytes 1 | tf_op jit(solution)/shard_map/forward/pallas_call | solution.py:58
  20.8 2.1 %forward.5 = (f32[128,3584]{1,0:T(8,128)S(1)}, bf16[128,3584]{1,0:T(8,128)(2,1)S(1)}, f32[8,128]{1,0:T(8,128)S(1)}) custom-call(bf16[256,1024]{1,0:T(8,128)(2,1)S(1)} %get-tuple-element.97.refs_0_, bf16[1024,7168]{1,0:T(8,128)(2,1)S(1)} %get-tuple-element.98.refs_1_.refs_3_, f32[8,128]{1,0:T(8,128)S(1)} %get-tuple-element.102.refs_2_), custom_call_target="tpu_custom_call" | custom-call | flops 1 | bytes 1 | tf_op jit(solution)/shard_map/forward/pallas_call | solution.py:58
  23.7 1.6 %collective-permute-start.4 = (bf16[64,3584]{1,0:T(8,128)(2,1)S(1)}, bf16[64,3584]{1,0:T(8,128)(2,1)S(1)}, u32[]{:S(2)}, u32[]{:S(2)}) collective-permute-start(bf16[64,3584]{1,0:T(8,128)(2,1)S(1)} %get-tuple-element.105), channel_id=1, source_target_pairs={{0,8},{4,12},{8,0},{12,4},{16,24},{20,28},{24,16},{28,20},{1,9},{5... | collective-permute-start | bytes 1376264 | tf_op jit(solution)/shard_map/ppermute | solution.py:382
  25.8 1.6 %collective-permute-start.10 = (bf16[64,3584]{1,0:T(8,128)(2,1)S(1)}, bf16[64,3584]{1,0:T(8,128)(2,1)S(1)}, u32[]{:S(2)}, u32[]{:S(2)}) collective-permute-start(bf16[64,3584]{1,0:T(8,128)(2,1)S(1)} %get-tuple-element.113), channel_id=1, source_target_pairs={{0,16},{4,20},{8,24},{12,28},{16,0},{20,4},{24,8},{28,12},{1,17},{... | collective-permute-start | bytes 1376264 | tf_op jit(solution)/shard_map/ppermute | solution.py:382
  27.4 3.2 %collective-permute-start.9 = (bf16[2,32,1024]{2,1,0:T(8,128)(2,1)S(1)}, bf16[2,32,1024]{2,1,0:T(8,128)(2,1)S(1)}, u32[]{:S(2)}, u32[]{:S(2)}) collective-permute-start(bf16[2,32,1024]{2,1,0:T(8,128)(2,1)S(1)} %get-tuple-element.189.refs_1_), channel_id=1, source_target_pairs={{0,3},{1,2},{2,1},{3,0},{4,7},{5,6},{6,5},{7,4},{8,11},{9,10},{10,... | collective-permute-start | bytes 393224 | tf_op jit(solution)/shard_map/ppermute | solution.py:382
  31.8 4.4 %collective-permute-done.4.refs_1_ = bf16[64,3584]{1,0:T(8,128)(2,1)S(1)} collective-permute-done((bf16[64,3584]{1,0:T(8,128)(2,1)S(1)}, bf16[64,3584]{1,0:T(8,128)(2,1)S(1)}, u32[]{:S(2)}, u32[]{:S(2)}) %collective-permute-start.4) | collective-permute-done | bytes 458784 | tf_op jit(solution)/shard_map/ppermute | solution.py:382
  36.3 2.3 %collective-permute-done.10.refs_1_ = bf16[64,3584]{1,0:T(8,128)(2,1)S(1)} collective-permute-done((bf16[64,3584]{1,0:T(8,128)(2,1)S(1)}, bf16[64,3584]{1,0:T(8,128)(2,1)S(1)}, u32[]{:S(2)}, u32[]{:S(2)}) %collective-permute-start.10) | collective-permute-done | bytes 458784 | tf_op jit(solution)/shard_map/ppermute | solution.py:382
  38.7 2.9 %collective-permute-done.8.refs_3_ = bf16[2,32,1024]{2,1,0:T(8,128)(2,1)S(1)} collective-permute-done((bf16[2,32,1024]{2,1,0:T(8,128)(2,1)S(1)}, bf16[2,32,1024]{2,1,0:T(8,128)(2,1)S(1)}, u32[]{:S(2)}, u32[]{:S(2)}) %collective-permute-start.8) | collective-permute-done | bytes 131104 | tf_op jit(solution)/shard_map/ppermute | solution.py:382
  42.4 2.1 %forward.6 = (f32[128,3584]{1,0:T(8,128)S(1)}, bf16[128,3584]{1,0:T(8,128)(2,1)S(1)}, f32[8,128]{1,0:T(8,128)S(1)}) custom-call(bf16[256,1024]{1,0:T(8,128)(2,1)S(1)} %get-tuple-element.116.refs_0_, bf16[1024,7168]{1,0:T(8,128)(2,1)S(1)} %get-tuple-element.98.refs_1_.refs_3_, f32[8,128]{1,0:T(8,128)S(1)} %get-tuple-element.117.refs_2_), custom_call_target="tpu_custom_call" | custom-call | flops 1 | bytes 1 | tf_op jit(solution)/shard_map/forward/pallas_call | solution.py:58
  44.6 2.1 %forward.7 = (f32[128,3584]{1,0:T(8,128)S(1)}, bf16[128,3584]{1,0:T(8,128)(2,1)S(1)}, f32[8,128]{1,0:T(8,128)S(1)}) custom-call(bf16[256,1024]{1,0:T(8,128)(2,1)S(1)} %get-tuple-element.116.refs_0_, bf16[1024,7168]{1,0:T(8,128)(2,1)S(1)} %get-tuple-element.98.refs_1_.refs_3_, f32[8,128]{1,0:T(8,128)S(1)} %get-tuple-element.118.refs_2_), custom_call_target="tpu_custom_call" | custom-call | flops 1 | bytes 1 | tf_op jit(solution)/shard_map/forward/pallas_call | solution.py:58
  47.7 1.6 %collective-permute-start.13 = (bf16[32,3584]{1,0:T(8,128)(2,1)S(1)}, bf16[32,3584]{1,0:T(8,128)(2,1)S(1)}, u32[]{:S(2)}, u32[]{:S(2)}) collective-permute-start(bf16[32,3584]{1,0:T(8,128)(2,1)S(1)} %get-tuple-element.128), channel_id=1, source_target_pairs={{0,8},{4,12},{8,0},{12,4},{16,24},{20,28},{24,16},{28,20},{1,9},{5... | collective-permute-start | bytes 688136 | tf_op jit(solution)/shard_map/ppermute | solution.py:382
  49.7 5.2 %collective-permute-done.6.refs_1_ = bf16[32,3584]{1,0:T(8,128)(2,1)S(1)} collective-permute-done((bf16[32,3584]{1,0:T(8,128)(2,1)S(1)}, bf16[32,3584]{1,0:T(8,128)(2,1)S(1)}, u32[]{:S(2)}, u32[]{:S(2)}) %collective-permute-start.6) | collective-permute-done | bytes 229408 | tf_op jit(solution)/shard_map/ppermute | solution.py:382
  56.1 1.6 %collective-permute-start.15 = (bf16[32,3584]{1,0:T(8,128)(2,1)S(1)}, bf16[32,3584]{1,0:T(8,128)(2,1)S(1)}, u32[]{:S(2)}, u32[]{:S(2)}) collective-permute-start(bf16[32,3584]{1,0:T(8,128)(2,1)S(1)} %get-tuple-element.133.refs_0_), channel_id=1, source_target_pairs={{0,8},{4,12},{8,0},{12,4},{16,24},{20,28},{24,16},{28,20},{1,9},{5... | collective-permute-start | bytes 688136 | tf_op jit(solution)/shard_map/ppermute | solution.py:382
  58.2 1.6 %collective-permute-start.20 = (bf16[64,3584]{1,0:T(8,128)(2,1)S(1)}, bf16[64,3584]{1,0:T(8,128)(2,1)S(1)}, u32[]{:S(2)}, u32[]{:S(2)}) collective-permute-start(bf16[64,3584]{1,0:T(8,128)(2,1)S(1)} %get-tuple-element.143), channel_id=1, source_target_pairs={{0,16},{4,20},{8,24},{12,28},{16,0},{20,4},{24,8},{28,12},{1,17},{... | collective-permute-start | bytes 1376264 | tf_op jit(solution)/shard_map/ppermute | solution.py:382
  59.8 4.0 %collective-permute-done.16.refs_1_ = bf16[32,3584]{1,0:T(8,128)(2,1)S(1)} collective-permute-done((bf16[32,3584]{1,0:T(8,128)(2,1)S(1)}, bf16[32,3584]{1,0:T(8,128)(2,1)S(1)}, u32[]{:S(2)}, u32[]{:S(2)}) %collective-permute-start.16) | collective-permute-done | bytes 229408 | tf_op jit(solution)/shard_map/ppermute | solution.py:382
  66.4 8.1 %collective-permute-done.14.refs_1_ = bf16[64,3584]{1,0:T(8,128)(2,1)S(1)} collective-permute-done((bf16[64,3584]{1,0:T(8,128)(2,1)S(1)}, bf16[64,3584]{1,0:T(8,128)(2,1)S(1)}, u32[]{:S(2)}, u32[]{:S(2)}) %collective-permute-start.14) | collective-permute-done | bytes 458784 | tf_op jit(solution)/shard_map/ppermute | solution.py:382
  74.7 1.7 %collective-permute-start.17 = (bf16[32,3584]{1,0:T(8,128)(2,1)S(1)}, bf16[32,3584]{1,0:T(8,128)(2,1)S(1)}, u32[]{:S(2)}, u32[]{:S(2)}) collective-permute-start(bf16[32,3584]{1,0:T(8,128)(2,1)S(1)} %get-tuple-element.139), channel_id=1, source_target_pairs={{0,16},{4,20},{8,24},{12,28},{16,0},{20,4},{24,8},{28,12},{1,17},{... | collective-permute-start | bytes 688136 | tf_op jit(solution)/shard_map/ppermute | solution.py:382
  77.8 6.6 %collective-permute-done.19.refs_1_ = bf16[64,3584]{1,0:T(8,128)(2,1)S(1)} collective-permute-done((bf16[64,3584]{1,0:T(8,128)(2,1)S(1)}, bf16[64,3584]{1,0:T(8,128)(2,1)S(1)}, u32[]{:S(2)}, u32[]{:S(2)}) %collective-permute-start.19) | collective-permute-done | bytes 458784 | tf_op jit(solution)/shard_map/ppermute | solution.py:382
  87.9 1.6 %collective-permute-start.22 = (bf16[32,3584]{1,0:T(8,128)(2,1)S(1)}, bf16[32,3584]{1,0:T(8,128)(2,1)S(1)}, u32[]{:S(2)}, u32[]{:S(2)}) collective-permute-start(bf16[32,3584]{1,0:T(8,128)(2,1)S(1)} %get-tuple-element.153.refs_0_), channel_id=1, source_target_pairs={{0,8},{4,12},{8,0},{12,4},{16,24},{20,28},{24,16},{28,20},{1,9},{5... | collective-permute-start | bytes 688136 | tf_op jit(solution)/shard_map/ppermute | solution.py:382
  89.6 3.6 %collective-permute-done.23.refs_1_ = bf16[32,3584]{1,0:T(8,128)(2,1)S(1)} collective-permute-done((bf16[32,3584]{1,0:T(8,128)(2,1)S(1)}, bf16[32,3584]{1,0:T(8,128)(2,1)S(1)}, u32[]{:S(2)}, u32[]{:S(2)}) %collective-permute-start.23) | collective-permute-done | bytes 229408 | tf_op jit(solution)/shard_map/ppermute | solution.py:382
  93.2 1.6 %collective-permute-start.30 = (bf16[64,3584]{1,0:T(8,128)(2,1)S(1)}, bf16[64,3584]{1,0:T(8,128)(2,1)S(1)}, u32[]{:S(2)}, u32[]{:S(2)}) collective-permute-start(bf16[64,3584]{1,0:T(8,128)(2,1)S(1)} %get-tuple-element.169.refs_0_), channel_id=1, source_target_pairs={{0,8},{4,12},{8,0},{12,4},{16,24},{20,28},{24,16},{28,20},{1,9},{5... | collective-permute-start | bytes 1376264 | tf_op jit(solution)/shard_map/ppermute | solution.py:382
  97.3 2.9 %input_partial.4 = (f32[1024,256]{1,0:T(8,128)S(1)}, f32[8,128]{1,0:T(8,128)S(1)}) custom-call(s32[8]{0:T(128)S(1)} %shift-right-arithmetic_add_fusion.refs_3_.refs_0_, bf16[128,3584]{1,0:T(8,128)(2,1)S(1)} %get-tuple-element.160.refs_1_.refs_3_, bf16[128,3584]{1,0:T(8,128)(2,1)S(1)} %collective-permute-done.25.refs_2_.refs_4_, ...), custom_call_target="tpu_custom_call" | custom-call | flops 1 | bytes 1 | tf_op jit(solution)/shard_map/input_partial/pallas_call | solution.py:58
  100.2 2.9 %input_partial.5 = (f32[64,1024]{1,0:T(8,128)S(1)}, bf16[64,1024]{1,0:T(8,128)(2,1)S(1)}, bf16[64,1024]{1,0:T(8,128)(2,1)S(1)}, bf16[64,1024]{1,0:T(8,128)(2,1)S(1)}, f32[8,128]{1,0:T(8,128)S(1)}) custom-call(s32[8]{0:T(128)S(1)} %shift-right-arithmetic_add_fusion.refs_3_.refs_0_, bf16[128,3584]{1,0:T(8,128)(2,1)S(1)} %get-tuple-element.159.refs_1_.refs_3_, ...), custom_call_target="tpu_custom_call" | custom-call | flops 1 | bytes 1 | tf_op jit(solution)/shard_map/input_partial/pallas_call | solution.py:58
  103.1 1.7 %collective-permute-done.30.refs_1_ = bf16[64,3584]{1,0:T(8,128)(2,1)S(1)} collective-permute-done((bf16[64,3584]{1,0:T(8,128)(2,1)S(1)}, bf16[64,3584]{1,0:T(8,128)(2,1)S(1)}, u32[]{:S(2)}, u32[]{:S(2)}) %collective-permute-start.30) | collective-permute-done | bytes 458784 | tf_op jit(solution)/shard_map/ppermute | solution.py:382
  106.5 2.7 %collective-permute-start.27 = (bf16[64,1024]{1,0:T(8,128)(2,1)S(1)}, bf16[64,1024]{1,0:T(8,128)(2,1)S(1)}, u32[]{:S(2)}, u32[]{:S(2)}) collective-permute-start(bf16[64,1024]{1,0:T(8,128)(2,1)S(1)} %get-tuple-element.166), channel_id=1, source_target_pairs={{0,2},{1,3},{2,0},{3,1},{4,6},{5,7},{6,4},{7,5},{8,10},{9,11},{10,... | collective-permute-start | bytes 393224 | tf_op jit(solution)/shard_map/ppermute | solution.py:382
  110.6 2.7 %input_partial.6 = (f32[1024,256]{1,0:T(8,128)S(1)}, f32[8,128]{1,0:T(8,128)S(1)}) custom-call(s32[8]{0:T(128)S(1)} %shift-right-arithmetic_add_fusion.refs_3_.refs_0_, bf16[128,3584]{1,0:T(8,128)(2,1)S(1)} %get-tuple-element.173.refs_1_.refs_5_, bf16[128,3584]{1,0:T(8,128)(2,1)S(1)} %collective-permute-done.32.refs_2_.refs_6_, ...), custom_call_target="tpu_custom_call" | custom-call | flops 1 | bytes 1 | tf_op jit(solution)/shard_map/input_partial/pallas_call | solution.py:58
  113.3 2.9 %input_partial.7 = (f32[64,1024]{1,0:T(8,128)S(1)}, bf16[64,1024]{1,0:T(8,128)(2,1)S(1)}, bf16[64,1024]{1,0:T(8,128)(2,1)S(1)}, bf16[64,1024]{1,0:T(8,128)(2,1)S(1)}, f32[8,128]{1,0:T(8,128)S(1)}) custom-call(s32[8]{0:T(128)S(1)} %shift-right-arithmetic_add_fusion.refs_3_.refs_0_, bf16[128,3584]{1,0:T(8,128)(2,1)S(1)} %get-tuple-element.172.refs_1_.refs_5_, ...), custom_call_target="tpu_custom_call" | custom-call | flops 1 | bytes 1 | tf_op jit(solution)/shard_map/input_partial/pallas_call | solution.py:58
  116.3 3.0 %collective-permute-start.34 = (bf16[64,1024]{1,0:T(8,128)(2,1)S(1)}, bf16[64,1024]{1,0:T(8,128)(2,1)S(1)}, u32[]{:S(2)}, u32[]{:S(2)}) collective-permute-start(bf16[64,1024]{1,0:T(8,128)(2,1)S(1)} %get-tuple-element.179), channel_id=1, source_target_pairs={{0,2},{1,3},{2,0},{3,1},{4,6},{5,7},{6,4},{7,5},{8,10},{9,11},{10,... | collective-permute-start | bytes 393224 | tf_op jit(solution)/shard_map/ppermute | solution.py:382
  120.7 5.6 %weight_gradient.2 = (bf16[1,1,448,128,128]{4,3,2,1,0:T(8,128)(2,1)}, f32[8,128]{1,0:T(8,128)S(1)}) custom-call(s32[448]{0:T(512)S(1)} %select_reduce_fusion.refs_0_, bf16[1024,256]{1,0:T(8,128)(2,1)S(1)} %get-tuple-element.181.refs_1_, bf16[1024,256]{1,0:T(8,128)(2,1)S(1)} %get-tuple-element.182.refs_2_, ...), custom_call_target="tpu_custom_call" | custom-call | flops 1 | bytes 1 | tf_op jit(solution)/shard_map/weight_gradient/pallas_call | solution.py:58
  126.3 5.6 %weight_gradient.3 = (bf16[1,1,448,128,128]{4,3,2,1,0:T(8,128)(2,1)}, f32[8,128]{1,0:T(8,128)S(1)}) custom-call(s32[448]{0:T(512)S(1)} %select_reduce_fusion.refs_0_, bf16[1024,256]{1,0:T(8,128)(2,1)S(1)} %get-tuple-element.181.refs_1_, bf16[1024,256]{1,0:T(8,128)(2,1)S(1)} %get-tuple-element.182.refs_2_, ...), custom_call_target="tpu_custom_call", output_to_operand_aliasing={{0}: (7, {})} | custom-call | flops 1 | bytes 1 | tf_op jit(solution)/shard_map/weight_gradient/pallas_call | solution.py:58
  (83 shorter events, 27.2 us)
Async XLA Ops:
  1.6 15.2 %collective-permute-start.2 = (bf16[2,32,1024]{2,1,0:T(8,128)(2,1)S(1)}, bf16[2,32,1024]{2,1,0:T(8,128)(2,1)S(1)}, u32[]{:S(2)}, u32[]{:S(2)}) collective-permute-start(bf16[2,32,1024]{2,1,0:T(8,128)(2,1)S(1)} %get-tuple-element.190.refs_1_), channel_id=1, source_target_pairs={{0,3},{1,2},{2,1},{3,0},{4,7},{5,6},{6,5},{7,4},{8,11},{9,10},{10,... | collective-permute-start | bytes 393224 | tf_op jit(solution)/shard_map/ppermute | solution.py:382
  6.7 11.1 %collective-permute-start.1 = (bf16[2,32,1024]{2,1,0:T(8,128)(2,1)S(1)}, bf16[2,32,1024]{2,1,0:T(8,128)(2,1)S(1)}, u32[]{:S(2)}, u32[]{:S(2)}) collective-permute-start(bf16[2,32,1024]{2,1,0:T(8,128)(2,1)S(1)} %get-tuple-element.190.refs_1_), channel_id=1, source_target_pairs={{0,2},{1,3},{2,0},{3,1},{4,6},{5,7},{6,4},{7,5},{8,10},{9,11},{10,... | collective-permute-start | bytes 393224 | tf_op jit(solution)/shard_map/ppermute | solution.py:382
  6.7 11.1 %collective-permute-start = (bf16[2,32,1024]{2,1,0:T(8,128)(2,1)S(1)}, bf16[2,32,1024]{2,1,0:T(8,128)(2,1)S(1)}, u32[]{:S(2)}, u32[]{:S(2)}) collective-permute-start(bf16[2,32,1024]{2,1,0:T(8,128)(2,1)S(1)} %get-tuple-element.190.refs_1_), channel_id=1, source_target_pairs={{0,1},{1,0},{2,3},{3,2},{4,5},{5,4},{6,7},{7,6},{8,9},{9,8},{10,11... | collective-permute-start | bytes 393224 | tf_op jit(solution)/shard_map/ppermute | solution.py:382
  23.7 12.5 %collective-permute-start.4 = (bf16[64,3584]{1,0:T(8,128)(2,1)S(1)}, bf16[64,3584]{1,0:T(8,128)(2,1)S(1)}, u32[]{:S(2)}, u32[]{:S(2)}) collective-permute-start(bf16[64,3584]{1,0:T(8,128)(2,1)S(1)} %get-tuple-element.105), channel_id=1, source_target_pairs={{0,8},{4,12},{8,0},{12,4},{16,24},{20,28},{24,16},{28,20},{1,9},{5... | collective-permute-start | bytes 1376264 | tf_op jit(solution)/shard_map/ppermute | solution.py:382
  25.8 12.9 %collective-permute-start.10 = (bf16[64,3584]{1,0:T(8,128)(2,1)S(1)}, bf16[64,3584]{1,0:T(8,128)(2,1)S(1)}, u32[]{:S(2)}, u32[]{:S(2)}) collective-permute-start(bf16[64,3584]{1,0:T(8,128)(2,1)S(1)} %get-tuple-element.113), channel_id=1, source_target_pairs={{0,16},{4,20},{8,24},{12,28},{16,0},{20,4},{24,8},{28,12},{1,17},{... | collective-permute-start | bytes 1376264 | tf_op jit(solution)/shard_map/ppermute | solution.py:382
  27.4 11.3 %collective-permute-start.9 = (bf16[2,32,1024]{2,1,0:T(8,128)(2,1)S(1)}, bf16[2,32,1024]{2,1,0:T(8,128)(2,1)S(1)}, u32[]{:S(2)}, u32[]{:S(2)}) collective-permute-start(bf16[2,32,1024]{2,1,0:T(8,128)(2,1)S(1)} %get-tuple-element.189.refs_1_), channel_id=1, source_target_pairs={{0,3},{1,2},{2,1},{3,0},{4,7},{5,6},{6,5},{7,4},{8,11},{9,10},{10,... | collective-permute-start | bytes 393224 | tf_op jit(solution)/shard_map/ppermute | solution.py:382
  30.6 11.0 %collective-permute-start.8 = (bf16[2,32,1024]{2,1,0:T(8,128)(2,1)S(1)}, bf16[2,32,1024]{2,1,0:T(8,128)(2,1)S(1)}, u32[]{:S(2)}, u32[]{:S(2)}) collective-permute-start(bf16[2,32,1024]{2,1,0:T(8,128)(2,1)S(1)} %get-tuple-element.189.refs_1_), channel_id=1, source_target_pairs={{0,2},{1,3},{2,0},{3,1},{4,6},{5,7},{6,4},{7,5},{8,10},{9,11},{10,... | collective-permute-start | bytes 393224 | tf_op jit(solution)/shard_map/ppermute | solution.py:382
  30.6 11.0 %collective-permute-start.7 = (bf16[2,32,1024]{2,1,0:T(8,128)(2,1)S(1)}, bf16[2,32,1024]{2,1,0:T(8,128)(2,1)S(1)}, u32[]{:S(2)}, u32[]{:S(2)}) collective-permute-start(bf16[2,32,1024]{2,1,0:T(8,128)(2,1)S(1)} %get-tuple-element.189.refs_1_), channel_id=1, source_target_pairs={{0,1},{1,0},{2,3},{3,2},{4,5},{5,4},{6,7},{7,6},{8,9},{9,8},{10,11... | collective-permute-start | bytes 393224 | tf_op jit(solution)/shard_map/ppermute | solution.py:382
  47.2 7.6 %collective-permute-start.6 = (bf16[32,3584]{1,0:T(8,128)(2,1)S(1)}, bf16[32,3584]{1,0:T(8,128)(2,1)S(1)}, u32[]{:S(2)}, u32[]{:S(2)}) collective-permute-start(bf16[32,3584]{1,0:T(8,128)(2,1)S(1)} %get-tuple-element.111), channel_id=1, source_target_pairs={{0,16},{4,20},{8,24},{12,28},{16,0},{20,4},{24,8},{28,12},{1,17},{... | collective-permute-start | bytes 688136 | tf_op jit(solution)/shard_map/ppermute | solution.py:382
  47.7 8.1 %collective-permute-start.13 = (bf16[32,3584]{1,0:T(8,128)(2,1)S(1)}, bf16[32,3584]{1,0:T(8,128)(2,1)S(1)}, u32[]{:S(2)}, u32[]{:S(2)}) collective-permute-start(bf16[32,3584]{1,0:T(8,128)(2,1)S(1)} %get-tuple-element.128), channel_id=1, source_target_pairs={{0,8},{4,12},{8,0},{12,4},{16,24},{20,28},{24,16},{28,20},{1,9},{5... | collective-permute-start | bytes 688136 | tf_op jit(solution)/shard_map/ppermute | solution.py:382
  55.2 8.6 %collective-permute-start.16 = (bf16[32,3584]{1,0:T(8,128)(2,1)S(1)}, bf16[32,3584]{1,0:T(8,128)(2,1)S(1)}, u32[]{:S(2)}, u32[]{:S(2)}) collective-permute-start(bf16[32,3584]{1,0:T(8,128)(2,1)S(1)} %get-tuple-element.134.refs_0_), channel_id=1, source_target_pairs={{0,16},{4,20},{8,24},{12,28},{16,0},{20,4},{24,8},{28,12},{1,17},{... | collective-permute-start | bytes 688136 | tf_op jit(solution)/shard_map/ppermute | solution.py:382
  56.1 9.2 %collective-permute-start.15 = (bf16[32,3584]{1,0:T(8,128)(2,1)S(1)}, bf16[32,3584]{1,0:T(8,128)(2,1)S(1)}, u32[]{:S(2)}, u32[]{:S(2)}) collective-permute-start(bf16[32,3584]{1,0:T(8,128)(2,1)S(1)} %get-tuple-element.133.refs_0_), channel_id=1, source_target_pairs={{0,8},{4,12},{8,0},{12,4},{16,24},{20,28},{24,16},{28,20},{1,9},{5... | collective-permute-start | bytes 688136 | tf_op jit(solution)/shard_map/ppermute | solution.py:382
  57.8 16.8 %collective-permute-start.14 = (bf16[64,3584]{1,0:T(8,128)(2,1)S(1)}, bf16[64,3584]{1,0:T(8,128)(2,1)S(1)}, u32[]{:S(2)}, u32[]{:S(2)}) collective-permute-start(bf16[64,3584]{1,0:T(8,128)(2,1)S(1)} %get-tuple-element.132), channel_id=1, source_target_pairs={{0,8},{4,12},{8,0},{12,4},{16,24},{20,28},{24,16},{28,20},{1,9},{5... | collective-permute-start | bytes 1376264 | tf_op jit(solution)/shard_map/ppermute | solution.py:382
  58.2 18.1 %collective-permute-start.20 = (bf16[64,3584]{1,0:T(8,128)(2,1)S(1)}, bf16[64,3584]{1,0:T(8,128)(2,1)S(1)}, u32[]{:S(2)}, u32[]{:S(2)}) collective-permute-start(bf16[64,3584]{1,0:T(8,128)(2,1)S(1)} %get-tuple-element.143), channel_id=1, source_target_pairs={{0,16},{4,20},{8,24},{12,28},{16,0},{20,4},{24,8},{28,12},{1,17},{... | collective-permute-start | bytes 1376264 | tf_op jit(solution)/shard_map/ppermute | solution.py:382
  63.9 20.5 %collective-permute-start.19 = (bf16[64,3584]{1,0:T(8,128)(2,1)S(1)}, bf16[64,3584]{1,0:T(8,128)(2,1)S(1)}, u32[]{:S(2)}, u32[]{:S(2)}) collective-permute-start(bf16[64,3584]{1,0:T(8,128)(2,1)S(1)} %get-tuple-element.141.refs_0_), channel_id=1, source_target_pairs={{0,8},{4,12},{8,0},{12,4},{16,24},{20,28},{24,16},{28,20},{1,9},{5... | collective-permute-start | bytes 1376264 | tf_op jit(solution)/shard_map/ppermute | solution.py:382
  65.3 19.2 %collective-permute-start.18 = (bf16[64,3584]{1,0:T(8,128)(2,1)S(1)}, bf16[64,3584]{1,0:T(8,128)(2,1)S(1)}, u32[]{:S(2)}, u32[]{:S(2)}) collective-permute-start(bf16[64,3584]{1,0:T(8,128)(2,1)S(1)} %get-tuple-element.140.refs_0_), channel_id=1, source_target_pairs={{0,16},{4,20},{8,24},{12,28},{16,0},{20,4},{24,8},{28,12},{1,17},{... | collective-permute-start | bytes 1376264 | tf_op jit(solution)/shard_map/ppermute | solution.py:382
  74.7 12.0 %collective-permute-start.17 = (bf16[32,3584]{1,0:T(8,128)(2,1)S(1)}, bf16[32,3584]{1,0:T(8,128)(2,1)S(1)}, u32[]{:S(2)}, u32[]{:S(2)}) collective-permute-start(bf16[32,3584]{1,0:T(8,128)(2,1)S(1)} %get-tuple-element.139), channel_id=1, source_target_pairs={{0,16},{4,20},{8,24},{12,28},{16,0},{20,4},{24,8},{28,12},{1,17},{... | collective-permute-start | bytes 688136 | tf_op jit(solution)/shard_map/ppermute | solution.py:382
  76.4 11.1 %collective-permute-start.21 = (bf16[32,3584]{1,0:T(8,128)(2,1)S(1)}, bf16[32,3584]{1,0:T(8,128)(2,1)S(1)}, u32[]{:S(2)}, u32[]{:S(2)}) collective-permute-start(bf16[32,3584]{1,0:T(8,128)(2,1)S(1)} %get-tuple-element.150), channel_id=1, source_target_pairs={{0,8},{4,12},{8,0},{12,4},{16,24},{20,28},{24,16},{28,20},{1,9},{5... | collective-permute-start | bytes 688136 | tf_op jit(solution)/shard_map/ppermute | solution.py:382
  84.5 12.8 %collective-permute-start.25 = (bf16[128,3584]{1,0:T(8,128)(2,1)S(1)}, bf16[128,3584]{1,0:T(8,128)(2,1)S(1)}, u32[]{:S(2)}, u32[]{:S(2)}) collective-permute-start(bf16[128,3584]{1,0:T(8,128)(2,1)S(1)} %get-tuple-element.160.refs_1_.refs_3_), channel_id=1, source_target_pairs={{0,4},{4,0},{8,12},{12,8},{16,20},{20,16},{24,28},{28,24},{1,5},{5... | collective-permute-start | bytes 2752520 | tf_op jit(solution)/shard_map/ppermute | solution.py:382
  84.6 15.5 %collective-permute-start.24 = (bf16[128,3584]{1,0:T(8,128)(2,1)S(1)}, bf16[128,3584]{1,0:T(8,128)(2,1)S(1)}, u32[]{:S(2)}, u32[]{:S(2)}) collective-permute-start(bf16[128,3584]{1,0:T(8,128)(2,1)S(1)} %get-tuple-element.159.refs_1_.refs_3_), channel_id=1, source_target_pairs={{0,4},{4,0},{8,12},{12,8},{16,20},{20,16},{24,28},{28,24},{1,5},{5... | collective-permute-start | bytes 2752520 | tf_op jit(solution)/shard_map/ppermute | solution.py:382
  87.0 6.2 %collective-permute-start.23 = (bf16[32,3584]{1,0:T(8,128)(2,1)S(1)}, bf16[32,3584]{1,0:T(8,128)(2,1)S(1)}, u32[]{:S(2)}, u32[]{:S(2)}) collective-permute-start(bf16[32,3584]{1,0:T(8,128)(2,1)S(1)} %get-tuple-element.154.refs_0_), channel_id=1, source_target_pairs={{0,16},{4,20},{8,24},{12,28},{16,0},{20,4},{24,8},{28,12},{1,17},{... | collective-permute-start | bytes 688136 | tf_op jit(solution)/shard_map/ppermute | solution.py:382
  87.9 8.1 %collective-permute-start.22 = (bf16[32,3584]{1,0:T(8,128)(2,1)S(1)}, bf16[32,3584]{1,0:T(8,128)(2,1)S(1)}, u32[]{:S(2)}, u32[]{:S(2)}) collective-permute-start(bf16[32,3584]{1,0:T(8,128)(2,1)S(1)} %get-tuple-element.153.refs_0_), channel_id=1, source_target_pairs={{0,8},{4,12},{8,0},{12,4},{16,24},{20,28},{24,16},{28,20},{1,9},{5... | collective-permute-start | bytes 688136 | tf_op jit(solution)/shard_map/ppermute | solution.py:382
  93.2 11.6 %collective-permute-start.30 = (bf16[64,3584]{1,0:T(8,128)(2,1)S(1)}, bf16[64,3584]{1,0:T(8,128)(2,1)S(1)}, u32[]{:S(2)}, u32[]{:S(2)}) collective-permute-start(bf16[64,3584]{1,0:T(8,128)(2,1)S(1)} %get-tuple-element.169.refs_0_), channel_id=1, source_target_pairs={{0,8},{4,12},{8,0},{12,4},{16,24},{20,28},{24,16},{28,20},{1,9},{5... | collective-permute-start | bytes 1376264 | tf_op jit(solution)/shard_map/ppermute | solution.py:382
  96.0 10.0 %collective-permute-start.29 = (bf16[64,3584]{1,0:T(8,128)(2,1)S(1)}, bf16[64,3584]{1,0:T(8,128)(2,1)S(1)}, u32[]{:S(2)}, u32[]{:S(2)}) collective-permute-start(bf16[64,3584]{1,0:T(8,128)(2,1)S(1)} %get-tuple-element.168.refs_0_), channel_id=1, source_target_pairs={{0,16},{4,20},{8,24},{12,28},{16,0},{20,4},{24,8},{28,12},{1,17},{... | collective-permute-start | bytes 1376264 | tf_op jit(solution)/shard_map/ppermute | solution.py:382
  104.9 5.8 %collective-permute-start.32 = (bf16[128,3584]{1,0:T(8,128)(2,1)S(1)}, bf16[128,3584]{1,0:T(8,128)(2,1)S(1)}, u32[]{:S(2)}, u32[]{:S(2)}) collective-permute-start(bf16[128,3584]{1,0:T(8,128)(2,1)S(1)} %get-tuple-element.173.refs_1_.refs_5_), channel_id=1, source_target_pairs={{0,4},{4,0},{8,12},{12,8},{16,20},{20,16},{24,28},{28,24},{1,5},{5... | collective-permute-start | bytes 2752520 | tf_op jit(solution)/shard_map/ppermute | solution.py:382
  106.1 7.2 %collective-permute-start.31 = (bf16[128,3584]{1,0:T(8,128)(2,1)S(1)}, bf16[128,3584]{1,0:T(8,128)(2,1)S(1)}, u32[]{:S(2)}, u32[]{:S(2)}) collective-permute-start(bf16[128,3584]{1,0:T(8,128)(2,1)S(1)} %get-tuple-element.172.refs_1_.refs_5_), channel_id=1, source_target_pairs={{0,4},{4,0},{8,12},{12,8},{16,20},{20,16},{24,28},{28,24},{1,5},{5... | collective-permute-start | bytes 2752520 | tf_op jit(solution)/shard_map/ppermute | solution.py:382
  106.2 13.1 %collective-permute-start.26 = (bf16[64,1024]{1,0:T(8,128)(2,1)S(1)}, bf16[64,1024]{1,0:T(8,128)(2,1)S(1)}, u32[]{:S(2)}, u32[]{:S(2)}) collective-permute-start(bf16[64,1024]{1,0:T(8,128)(2,1)S(1)} %get-tuple-element.165), channel_id=1, source_target_pairs={{0,1},{1,0},{2,3},{3,2},{4,5},{5,4},{6,7},{7,6},{8,9},{9,8},{10,11... | collective-permute-start | bytes 393224 | tf_op jit(solution)/shard_map/ppermute | solution.py:382
  106.5 25.4 %collective-permute-start.27 = (bf16[64,1024]{1,0:T(8,128)(2,1)S(1)}, bf16[64,1024]{1,0:T(8,128)(2,1)S(1)}, u32[]{:S(2)}, u32[]{:S(2)}) collective-permute-start(bf16[64,1024]{1,0:T(8,128)(2,1)S(1)} %get-tuple-element.166), channel_id=1, source_target_pairs={{0,2},{1,3},{2,0},{3,1},{4,6},{5,7},{6,4},{7,5},{8,10},{9,11},{10,... | collective-permute-start | bytes 393224 | tf_op jit(solution)/shard_map/ppermute | solution.py:382
  109.2 22.7 %collective-permute-start.28 = (bf16[64,1024]{1,0:T(8,128)(2,1)S(1)}, bf16[64,1024]{1,0:T(8,128)(2,1)S(1)}, u32[]{:S(2)}, u32[]{:S(2)}) collective-permute-start(bf16[64,1024]{1,0:T(8,128)(2,1)S(1)} %get-tuple-element.167), channel_id=1, source_target_pairs={{0,3},{1,2},{2,1},{3,0},{4,7},{5,6},{6,5},{7,4},{8,11},{9,10},{10,... | collective-permute-start | bytes 393224 | tf_op jit(solution)/shard_map/ppermute | solution.py:382
  116.2 15.7 %collective-permute-start.33 = (bf16[64,1024]{1,0:T(8,128)(2,1)S(1)}, bf16[64,1024]{1,0:T(8,128)(2,1)S(1)}, u32[]{:S(2)}, u32[]{:S(2)}) collective-permute-start(bf16[64,1024]{1,0:T(8,128)(2,1)S(1)} %get-tuple-element.178), channel_id=1, source_target_pairs={{0,1},{1,0},{2,3},{3,2},{4,5},{5,4},{6,7},{7,6},{8,9},{9,8},{10,11... | collective-permute-start | bytes 393224 | tf_op jit(solution)/shard_map/ppermute | solution.py:382
  116.3 15.7 %collective-permute-start.34 = (bf16[64,1024]{1,0:T(8,128)(2,1)S(1)}, bf16[64,1024]{1,0:T(8,128)(2,1)S(1)}, u32[]{:S(2)}, u32[]{:S(2)}) collective-permute-start(bf16[64,1024]{1,0:T(8,128)(2,1)S(1)} %get-tuple-element.179), channel_id=1, source_target_pairs={{0,2},{1,3},{2,0},{3,1},{4,6},{5,7},{6,4},{7,5},{8,10},{9,11},{10,... | collective-permute-start | bytes 393224 | tf_op jit(solution)/shard_map/ppermute | solution.py:382
  119.3 12.7 %collective-permute-start.35 = (bf16[64,1024]{1,0:T(8,128)(2,1)S(1)}, bf16[64,1024]{1,0:T(8,128)(2,1)S(1)}, u32[]{:S(2)}, u32[]{:S(2)}) collective-permute-start(bf16[64,1024]{1,0:T(8,128)(2,1)S(1)} %get-tuple-element.180), channel_id=1, source_target_pairs={{0,3},{1,2},{2,1},{3,0},{4,7},{5,6},{6,5},{7,4},{8,11},{9,10},{10,... | collective-permute-start | bytes 393224 | tf_op jit(solution)/shard_map/ppermute | solution.py:382
  (5 other events, 25.5 us)
where the time goes:
time: 133 us
  Pallas kernels  44.7 us (34%)
  waiting for transfers between devices  43.8 us (33%)
  starting transfers between devices  40.1 us (30%)
  between operations  1.65 us (1%)
  other arithmetic  1.56 us (1%)
    pallas_call x35, Pallas kernels, __call__(): pl.pallas_call(body, out_shape=[*out_shape, pltpu.VMEM((8, 128), jnp.floa...  44.7 us
    ppermute x36, waiting for transfers between devices, swap(): return lax.ppermute(array, axis, [(i, i ^ bit) for i in range(size)])  43.8 us
    ppermute x36, starting transfers between devices, swap(): return lax.ppermute(array, axis, [(i, i ^ bit) for i in range(size)])  40.1 us
  transfers between devices with their start and end apart: 36, of which 14 were waited for; matrix products, arithmetic and copies ran while one was open for 1% of the time, Pallas kernels for 29%

commit v1 on v0

--- a/solution.py
+++ b/solution.py
@@ -236,7 +236,7 @@
         here = slice(at, at + wide)
         grad = jnp.concatenate([near_ref[:, here], far_ref[:, here]], axis=0)
         turned[here, :] = grad.T
-    high = 128 * group_of(tall // 128, 4)
+    high = 128 * group_of(tall // 128, 2)
     for at in range(0, tall, high):
         here = slice(at, at + high)
         product = jnp.dot(
@@ -287,22 +287,25 @@
     blk = made.shape[-1]
     width = grads[0].shape[1]
     here = width // blk
-    per_step = group_of(here, 2)
+    per_step = group_of(here, 4)
     wide = per_step * blk
+    high = group_of(row_blocks, 2)
     for j in range(here // per_step):
-        features = jnp.concatenate([t[...] for t in turned], axis=1)
         grad = jnp.concatenate([g[:, j * wide : (j + 1) * wide] for g in grads], axis=0)
-        product = jnp.dot(features, grad, preferred_element_type=jnp.float32)
-        for r in range(row_blocks):
-            for c in range(per_step):
-                entry = code[r * col_blocks + first // blk + j * per_step + c]
-                live = lax.rem(entry, 2).astype(jnp.float32)
-                at = (j * row_blocks + r) * per_step + c
-                block = product[r * blk : (r + 1) * blk, c * blk : (c + 1) * blk] * live
-                made[at] = block.astype(made.dtype)
-                pltpu.make_async_copy(
-                    made.at[at], out_ref.at[0, 0, lax.div(entry, 2)], sem
-                ).start(priority=at % 2)
+        for r in range(0, row_blocks, high):
+            rows = slice(r * blk, (r + high) * blk)
+            features = jnp.concatenate([t[rows, :] for t in turned], axis=1)
+            product = jnp.dot(features, grad, preferred_element_type=jnp.float32)
+            for i in range(high):
+                for c in range(per_step):
+                    entry = code[(r + i) * col_blocks + first // blk + j * per_step + c]
+                    live = lax.rem(entry, 2).astype(jnp.float32)
+                    at = (j * row_blocks + r + i) * per_step + c
+                    block = product[i * blk : (i + 1) * blk, c * blk : (c + 1) * blk] * live
+                    made[at] = block.astype(made.dtype)
+                    pltpu.make_async_copy(
+                        made.at[at], out_ref.at[0, 0, lax.div(entry, 2)], sem
+                    ).start(priority=at % 2)
     pltpu.make_async_copy(made, out_ref.at[0, 0, pl.ds(0, made.shape[0])], sem).wait()
 
 

time: 133 us -> 132 us (level)
  waiting for transfers between devices: 43.8 us -> 41.9 us
    ppermute x36, waiting for transfers between devices: 43.8 us -> 41.9 us  [swap(): return lax.ppermute(array, axis, [(i, i ^ bit) for i in range(size)])]
where the time goes in v1:
time: 132 us
  Pallas kernels  45.1 us (34%)
  waiting for transfers between devices  41.9 us (32%)
  starting transfers between devices  41.2 us (31%)
  between operations  1.66 us (1%)
  other arithmetic  1.56 us (1%)
    pallas_call x35, Pallas kernels, __call__(): pl.pallas_call(body, out_shape=[*out_shape, pltpu.VMEM((8, 128), jnp.floa...  45.1 us
    ppermute x36, waiting for transfers between devices, swap(): return lax.ppermute(array, axis, [(i, i ^ bit) for i in range(size)])  41.9 us
    ppermute x36, starting transfers between devices, swap(): return lax.ppermute(array, axis, [(i, i ^ bit) for i in range(size)])  41.2 us
  transfers between devices with their start and end apart: 36, of which 14 were waited for; matrix products, arithmetic and copies ran while one was open for 1% of the time, Pallas kernels for 29%

profile of v1, /device:TPU:0, one launch (start us, length us, event | category | flops | bytes accessed | tf_op | source)
XLA Modules:
  0.0 132.4 jit_solution(16263331363228738028)
XLA Ops:
  1.6 5.1 %collective-permute-start.2 = (bf16[2,32,1024]{2,1,0:T(8,128)(2,1)S(1)}, bf16[2,32,1024]{2,1,0:T(8,128)(2,1)S(1)}, u32[]{:S(2)}, u32[]{:S(2)}) collective-permute-start(bf16[2,32,1024]{2,1,0:T(8,128)(2,1)S(1)} %get-tuple-element.190.refs_1_), channel_id=1, source_target_pairs={{0,3},{1,2},{2,1},{3,0},{4,7},{5,6},{6,5},{7,4},{8,11},{9,10},{10,... | collective-permute-start | bytes 393224 | tf_op jit(solution)/shard_map/ppermute | solution.py:385
  9.6 7.9 %dense_tile.1 = (bf16[1024,7168]{1,0:T(8,128)(2,1)S(1)}, f32[8,128]{1,0:T(8,128)S(1)}) custom-call(s32[448]{0:T(512)S(1)} %select_reduce_fusion.refs_0_, bf16[1,1,448,128,128]{4,3,2,1,0:T(8,128)(2,1)} %refs_1_.1, s32[8]{0:T(128)S(1)} %broadcast_xor_fusion.refs_2_.refs_0_, s32[8]{0:T(128)S(1)} %shift-right-arithmetic_add_fusion.refs_3_.refs_0_), custom_call_target="tpu_custom_call" | custom-call | flops 1 | bytes 1 | tf_op jit(solution)/shard_map/dense_tile/pallas_call | solution.py:58
  18.6 2.1 %forward.4 = (f32[128,3584]{1,0:T(8,128)S(1)}, bf16[128,3584]{1,0:T(8,128)(2,1)S(1)}, f32[8,128]{1,0:T(8,128)S(1)}) custom-call(bf16[256,1024]{1,0:T(8,128)(2,1)S(1)} %get-tuple-element.97.refs_0_, bf16[1024,7168]{1,0:T(8,128)(2,1)S(1)} %get-tuple-element.98.refs_1_.refs_3_, f32[8,128]{1,0:T(8,128)S(1)} %get-tuple-element.99.refs_2_), custom_call_target="tpu_custom_call" | custom-call | flops 1 | bytes 1 | tf_op jit(solution)/shard_map/forward/pallas_call | solution.py:58
  20.8 2.1 %forward.5 = (f32[128,3584]{1,0:T(8,128)S(1)}, bf16[128,3584]{1,0:T(8,128)(2,1)S(1)}, f32[8,128]{1,0:T(8,128)S(1)}) custom-call(bf16[256,1024]{1,0:T(8,128)(2,1)S(1)} %get-tuple-element.97.refs_0_, bf16[1024,7168]{1,0:T(8,128)(2,1)S(1)} %get-tuple-element.98.refs_1_.refs_3_, f32[8,128]{1,0:T(8,128)S(1)} %get-tuple-element.102.refs_2_), custom_call_target="tpu_custom_call" | custom-call | flops 1 | bytes 1 | tf_op jit(solution)/shard_map/forward/pallas_call | solution.py:58
  25.8 1.6 %collective-permute-start.10 = (bf16[64,3584]{1,0:T(8,128)(2,1)S(1)}, bf16[64,3584]{1,0:T(8,128)(2,1)S(1)}, u32[]{:S(2)}, u32[]{:S(2)}) collective-permute-start(bf16[64,3584]{1,0:T(8,128)(2,1)S(1)} %get-tuple-element.113), channel_id=1, source_target_pairs={{0,16},{4,20},{8,24},{12,28},{16,0},{20,4},{24,8},{28,12},{1,17},{... | collective-permute-start | bytes 1376264 | tf_op jit(solution)/shard_map/ppermute | solution.py:385
  27.4 2.9 %collective-permute-start.9 = (bf16[2,32,1024]{2,1,0:T(8,128)(2,1)S(1)}, bf16[2,32,1024]{2,1,0:T(8,128)(2,1)S(1)}, u32[]{:S(2)}, u32[]{:S(2)}) collective-permute-start(bf16[2,32,1024]{2,1,0:T(8,128)(2,1)S(1)} %get-tuple-element.189.refs_1_), channel_id=1, source_target_pairs={{0,3},{1,2},{2,1},{3,0},{4,7},{5,6},{6,5},{7,4},{8,11},{9,10},{10,... | collective-permute-start | bytes 393224 | tf_op jit(solution)/shard_map/ppermute | solution.py:385
  31.8 4.4 %collective-permute-done.4.refs_1_ = bf16[64,3584]{1,0:T(8,128)(2,1)S(1)} collective-permute-done((bf16[64,3584]{1,0:T(8,128)(2,1)S(1)}, bf16[64,3584]{1,0:T(8,128)(2,1)S(1)}, u32[]{:S(2)}, u32[]{:S(2)}) %collective-permute-start.4) | collective-permute-done | bytes 458784 | tf_op jit(solution)/shard_map/ppermute | solution.py:385
  36.3 2.3 %collective-permute-done.10.refs_1_ = bf16[64,3584]{1,0:T(8,128)(2,1)S(1)} collective-permute-done((bf16[64,3584]{1,0:T(8,128)(2,1)S(1)}, bf16[64,3584]{1,0:T(8,128)(2,1)S(1)}, u32[]{:S(2)}, u32[]{:S(2)}) %collective-permute-start.10) | collective-permute-done | bytes 458784 | tf_op jit(solution)/shard_map/ppermute | solution.py:385
  38.7 2.7 %collective-permute-done.8.refs_3_ = bf16[2,32,1024]{2,1,0:T(8,128)(2,1)S(1)} collective-permute-done((bf16[2,32,1024]{2,1,0:T(8,128)(2,1)S(1)}, bf16[2,32,1024]{2,1,0:T(8,128)(2,1)S(1)}, u32[]{:S(2)}, u32[]{:S(2)}) %collective-permute-start.8) | collective-permute-done | bytes 131104 | tf_op jit(solution)/shard_map/ppermute | solution.py:385
  42.2 2.1 %forward.6 = (f32[128,3584]{1,0:T(8,128)S(1)}, bf16[128,3584]{1,0:T(8,128)(2,1)S(1)}, f32[8,128]{1,0:T(8,128)S(1)}) custom-call(bf16[256,1024]{1,0:T(8,128)(2,1)S(1)} %get-tuple-element.116.refs_0_, bf16[1024,7168]{1,0:T(8,128)(2,1)S(1)} %get-tuple-element.98.refs_1_.refs_3_, f32[8,128]{1,0:T(8,128)S(1)} %get-tuple-element.117.refs_2_), custom_call_target="tpu_custom_call" | custom-call | flops 1 | bytes 1 | tf_op jit(solution)/shard_map/forward/pallas_call | solution.py:58
  44.4 2.1 %forward.7 = (f32[128,3584]{1,0:T(8,128)S(1)}, bf16[128,3584]{1,0:T(8,128)(2,1)S(1)}, f32[8,128]{1,0:T(8,128)S(1)}) custom-call(bf16[256,1024]{1,0:T(8,128)(2,1)S(1)} %get-tuple-element.116.refs_0_, bf16[1024,7168]{1,0:T(8,128)(2,1)S(1)} %get-tuple-element.98.refs_1_.refs_3_, f32[8,128]{1,0:T(8,128)S(1)} %get-tuple-element.118.refs_2_), custom_call_target="tpu_custom_call" | custom-call | flops 1 | bytes 1 | tf_op jit(solution)/shard_map/forward/pallas_call | solution.py:58
  47.6 1.6 %collective-permute-start.13 = (bf16[32,3584]{1,0:T(8,128)(2,1)S(1)}, bf16[32,3584]{1,0:T(8,128)(2,1)S(1)}, u32[]{:S(2)}, u32[]{:S(2)}) collective-permute-start(bf16[32,3584]{1,0:T(8,128)(2,1)S(1)} %get-tuple-element.128), channel_id=1, source_target_pairs={{0,8},{4,12},{8,0},{12,4},{16,24},{20,28},{24,16},{28,20},{1,9},{5... | collective-permute-start | bytes 688136 | tf_op jit(solution)/shard_map/ppermute | solution.py:385
  49.7 5.0 %collective-permute-done.6.refs_1_ = bf16[32,3584]{1,0:T(8,128)(2,1)S(1)} collective-permute-done((bf16[32,3584]{1,0:T(8,128)(2,1)S(1)}, bf16[32,3584]{1,0:T(8,128)(2,1)S(1)}, u32[]{:S(2)}, u32[]{:S(2)}) %collective-permute-start.6) | collective-permute-done | bytes 229408 | tf_op jit(solution)/shard_map/ppermute | solution.py:385
  56.1 1.7 %collective-permute-start.15 = (bf16[32,3584]{1,0:T(8,128)(2,1)S(1)}, bf16[32,3584]{1,0:T(8,128)(2,1)S(1)}, u32[]{:S(2)}, u32[]{:S(2)}) collective-permute-start(bf16[32,3584]{1,0:T(8,128)(2,1)S(1)} %get-tuple-element.133.refs_0_), channel_id=1, source_target_pairs={{0,8},{4,12},{8,0},{12,4},{16,24},{20,28},{24,16},{28,20},{1,9},{5... | collective-permute-start | bytes 688136 | tf_op jit(solution)/shard_map/ppermute | solution.py:385
  59.7 4.0 %collective-permute-done.16.refs_1_ = bf16[32,3584]{1,0:T(8,128)(2,1)S(1)} collective-permute-done((bf16[32,3584]{1,0:T(8,128)(2,1)S(1)}, bf16[32,3584]{1,0:T(8,128)(2,1)S(1)}, u32[]{:S(2)}, u32[]{:S(2)}) %collective-permute-start.16) | collective-permute-done | bytes 229408 | tf_op jit(solution)/shard_map/ppermute | solution.py:385
  63.8 1.8 %collective-permute-start.19 = (bf16[64,3584]{1,0:T(8,128)(2,1)S(1)}, bf16[64,3584]{1,0:T(8,128)(2,1)S(1)}, u32[]{:S(2)}, u32[]{:S(2)}) collective-permute-start(bf16[64,3584]{1,0:T(8,128)(2,1)S(1)} %get-tuple-element.141.refs_0_), channel_id=1, source_target_pairs={{0,8},{4,12},{8,0},{12,4},{16,24},{20,28},{24,16},{28,20},{1,9},{5... | collective-permute-start | bytes 1376264 | tf_op jit(solution)/shard_map/ppermute | solution.py:385
  66.3 8.2 %collective-permute-done.14.refs_1_ = bf16[64,3584]{1,0:T(8,128)(2,1)S(1)} collective-permute-done((bf16[64,3584]{1,0:T(8,128)(2,1)S(1)}, bf16[64,3584]{1,0:T(8,128)(2,1)S(1)}, u32[]{:S(2)}, u32[]{:S(2)}) %collective-permute-start.14) | collective-permute-done | bytes 458784 | tf_op jit(solution)/shard_map/ppermute | solution.py:385
  76.3 1.8 %collective-permute-start.21 = (bf16[32,3584]{1,0:T(8,128)(2,1)S(1)}, bf16[32,3584]{1,0:T(8,128)(2,1)S(1)}, u32[]{:S(2)}, u32[]{:S(2)}) collective-permute-start(bf16[32,3584]{1,0:T(8,128)(2,1)S(1)} %get-tuple-element.150), channel_id=1, source_target_pairs={{0,8},{4,12},{8,0},{12,4},{16,24},{20,28},{24,16},{28,20},{1,9},{5... | collective-permute-start | bytes 688136 | tf_op jit(solution)/shard_map/ppermute | solution.py:385
  78.1 6.2 %collective-permute-done.19.refs_1_ = bf16[64,3584]{1,0:T(8,128)(2,1)S(1)} collective-permute-done((bf16[64,3584]{1,0:T(8,128)(2,1)S(1)}, bf16[64,3584]{1,0:T(8,128)(2,1)S(1)}, u32[]{:S(2)}, u32[]{:S(2)}) %collective-permute-start.19) | collective-permute-done | bytes 458784 | tf_op jit(solution)/shard_map/ppermute | solution.py:385
  87.9 1.7 %collective-permute-start.22 = (bf16[32,3584]{1,0:T(8,128)(2,1)S(1)}, bf16[32,3584]{1,0:T(8,128)(2,1)S(1)}, u32[]{:S(2)}, u32[]{:S(2)}) collective-permute-start(bf16[32,3584]{1,0:T(8,128)(2,1)S(1)} %get-tuple-element.153.refs_0_), channel_id=1, source_target_pairs={{0,8},{4,12},{8,0},{12,4},{16,24},{20,28},{24,16},{28,20},{1,9},{5... | collective-permute-start | bytes 688136 | tf_op jit(solution)/shard_map/ppermute | solution.py:385
  89.6 3.6 %collective-permute-done.23.refs_1_ = bf16[32,3584]{1,0:T(8,128)(2,1)S(1)} collective-permute-done((bf16[32,3584]{1,0:T(8,128)(2,1)S(1)}, bf16[32,3584]{1,0:T(8,128)(2,1)S(1)}, u32[]{:S(2)}, u32[]{:S(2)}) %collective-permute-start.23) | collective-permute-done | bytes 229408 | tf_op jit(solution)/shard_map/ppermute | solution.py:385
  93.2 1.7 %collective-permute-start.30 = (bf16[64,3584]{1,0:T(8,128)(2,1)S(1)}, bf16[64,3584]{1,0:T(8,128)(2,1)S(1)}, u32[]{:S(2)}, u32[]{:S(2)}) collective-permute-start(bf16[64,3584]{1,0:T(8,128)(2,1)S(1)} %get-tuple-element.169.refs_0_), channel_id=1, source_target_pairs={{0,8},{4,12},{8,0},{12,4},{16,24},{20,28},{24,16},{28,20},{1,9},{5... | collective-permute-start | bytes 1376264 | tf_op jit(solution)/shard_map/ppermute | solution.py:385
  97.6 2.9 %input_partial.4 = (f32[1024,256]{1,0:T(8,128)S(1)}, f32[8,128]{1,0:T(8,128)S(1)}) custom-call(s32[8]{0:T(128)S(1)} %shift-right-arithmetic_add_fusion.refs_3_.refs_0_, bf16[128,3584]{1,0:T(8,128)(2,1)S(1)} %get-tuple-element.160.refs_1_.refs_3_, bf16[128,3584]{1,0:T(8,128)(2,1)S(1)} %collective-permute-done.25.refs_2_.refs_4_, ...), custom_call_target="tpu_custom_call" | custom-call | flops 1 | bytes 1 | tf_op jit(solution)/shard_map/input_partial/pallas_call | solution.py:58
  100.6 3.0 %input_partial.5 = (f32[64,1024]{1,0:T(8,128)S(1)}, bf16[64,1024]{1,0:T(8,128)(2,1)S(1)}, bf16[64,1024]{1,0:T(8,128)(2,1)S(1)}, bf16[64,1024]{1,0:T(8,128)(2,1)S(1)}, f32[8,128]{1,0:T(8,128)S(1)}) custom-call(s32[8]{0:T(128)S(1)} %shift-right-arithmetic_add_fusion.refs_3_.refs_0_, bf16[128,3584]{1,0:T(8,128)(2,1)S(1)} %get-tuple-element.159.refs_1_.refs_3_, ...), custom_call_target="tpu_custom_call" | custom-call | flops 1 | bytes 1 | tf_op jit(solution)/shard_map/input_partial/pallas_call | solution.py:58
  106.2 2.5 %collective-permute-start.27 = (bf16[64,1024]{1,0:T(8,128)(2,1)S(1)}, bf16[64,1024]{1,0:T(8,128)(2,1)S(1)}, u32[]{:S(2)}, u32[]{:S(2)}) collective-permute-start(bf16[64,1024]{1,0:T(8,128)(2,1)S(1)} %get-tuple-element.166), channel_id=1, source_target_pairs={{0,2},{1,3},{2,0},{3,1},{4,6},{5,7},{6,4},{7,5},{8,10},{9,11},{10,... | collective-permute-start | bytes 393224 | tf_op jit(solution)/shard_map/ppermute | solution.py:385
  108.7 1.8 %collective-permute-start.28 = (bf16[64,1024]{1,0:T(8,128)(2,1)S(1)}, bf16[64,1024]{1,0:T(8,128)(2,1)S(1)}, u32[]{:S(2)}, u32[]{:S(2)}) collective-permute-start(bf16[64,1024]{1,0:T(8,128)(2,1)S(1)} %get-tuple-element.167), channel_id=1, source_target_pairs={{0,3},{1,2},{2,1},{3,0},{4,7},{5,6},{6,5},{7,4},{8,11},{9,10},{10,... | collective-permute-start | bytes 393224 | tf_op jit(solution)/shard_map/ppermute | solution.py:385
  110.6 2.7 %input_partial.6 = (f32[1024,256]{1,0:T(8,128)S(1)}, f32[8,128]{1,0:T(8,128)S(1)}) custom-call(s32[8]{0:T(128)S(1)} %shift-right-arithmetic_add_fusion.refs_3_.refs_0_, bf16[128,3584]{1,0:T(8,128)(2,1)S(1)} %get-tuple-element.173.refs_1_.refs_5_, bf16[128,3584]{1,0:T(8,128)(2,1)S(1)} %collective-permute-done.32.refs_2_.refs_6_, ...), custom_call_target="tpu_custom_call" | custom-call | flops 1 | bytes 1 | tf_op jit(solution)/shard_map/input_partial/pallas_call | solution.py:58
  113.3 3.0 %input_partial.7 = (f32[64,1024]{1,0:T(8,128)S(1)}, bf16[64,1024]{1,0:T(8,128)(2,1)S(1)}, bf16[64,1024]{1,0:T(8,128)(2,1)S(1)}, bf16[64,1024]{1,0:T(8,128)(2,1)S(1)}, f32[8,128]{1,0:T(8,128)S(1)}) custom-call(s32[8]{0:T(128)S(1)} %shift-right-arithmetic_add_fusion.refs_3_.refs_0_, bf16[128,3584]{1,0:T(8,128)(2,1)S(1)} %get-tuple-element.172.refs_1_.refs_5_, ...), custom_call_target="tpu_custom_call" | custom-call | flops 1 | bytes 1 | tf_op jit(solution)/shard_map/input_partial/pallas_call | solution.py:58
  116.4 2.5 %collective-permute-start.34 = (bf16[64,1024]{1,0:T(8,128)(2,1)S(1)}, bf16[64,1024]{1,0:T(8,128)(2,1)S(1)}, u32[]{:S(2)}, u32[]{:S(2)}) collective-permute-start(bf16[64,1024]{1,0:T(8,128)(2,1)S(1)} %get-tuple-element.179), channel_id=1, source_target_pairs={{0,2},{1,3},{2,0},{3,1},{4,6},{5,7},{6,4},{7,5},{8,10},{9,11},{10,... | collective-permute-start | bytes 393224 | tf_op jit(solution)/shard_map/ppermute | solution.py:385
  118.9 1.8 %collective-permute-start.35 = (bf16[64,1024]{1,0:T(8,128)(2,1)S(1)}, bf16[64,1024]{1,0:T(8,128)(2,1)S(1)}, u32[]{:S(2)}, u32[]{:S(2)}) collective-permute-start(bf16[64,1024]{1,0:T(8,128)(2,1)S(1)} %get-tuple-element.180), channel_id=1, source_target_pairs={{0,3},{1,2},{2,1},{3,0},{4,7},{5,6},{6,5},{7,4},{8,11},{9,10},{10,... | collective-permute-start | bytes 393224 | tf_op jit(solution)/shard_map/ppermute | solution.py:385
  120.8 5.2 %weight_gradient.2 = (bf16[1,1,448,128,128]{4,3,2,1,0:T(8,128)(2,1)}, f32[8,128]{1,0:T(8,128)S(1)}) custom-call(s32[448]{0:T(512)S(1)} %select_reduce_fusion.refs_0_, bf16[1024,256]{1,0:T(8,128)(2,1)S(1)} %get-tuple-element.181.refs_1_, bf16[1024,256]{1,0:T(8,128)(2,1)S(1)} %get-tuple-element.182.refs_2_, ...), custom_call_target="tpu_custom_call" | custom-call | flops 1 | bytes 1 | tf_op jit(solution)/shard_map/weight_gradient/pallas_call | solution.py:58
  126.0 5.5 %weight_gradient.3 = (bf16[1,1,448,128,128]{4,3,2,1,0:T(8,128)(2,1)}, f32[8,128]{1,0:T(8,128)S(1)}) custom-call(s32[448]{0:T(512)S(1)} %select_reduce_fusion.refs_0_, bf16[1024,256]{1,0:T(8,128)(2,1)S(1)} %get-tuple-element.181.refs_1_, bf16[1024,256]{1,0:T(8,128)(2,1)S(1)} %get-tuple-element.182.refs_2_, ...), custom_call_target="tpu_custom_call", output_to_operand_aliasing={{0}: (7, {})} | custom-call | flops 1 | bytes 1 | tf_op jit(solution)/shard_map/weight_gradient/pallas_call | solution.py:58
  (83 shorter events, 26.8 us)
Async XLA Ops:
  1.6 15.8 %collective-permute-start.2 = (bf16[2,32,1024]{2,1,0:T(8,128)(2,1)S(1)}, bf16[2,32,1024]{2,1,0:T(8,128)(2,1)S(1)}, u32[]{:S(2)}, u32[]{:S(2)}) collective-permute-start(bf16[2,32,1024]{2,1,0:T(8,128)(2,1)S(1)} %get-tuple-element.190.refs_1_), channel_id=1, source_target_pairs={{0,3},{1,2},{2,1},{3,0},{4,7},{5,6},{6,5},{7,4},{8,11},{9,10},{10,... | collective-permute-start | bytes 393224 | tf_op jit(solution)/shard_map/ppermute | solution.py:385
  6.7 11.1 %collective-permute-start.1 = (bf16[2,32,1024]{2,1,0:T(8,128)(2,1)S(1)}, bf16[2,32,1024]{2,1,0:T(8,128)(2,1)S(1)}, u32[]{:S(2)}, u32[]{:S(2)}) collective-permute-start(bf16[2,32,1024]{2,1,0:T(8,128)(2,1)S(1)} %get-tuple-element.190.refs_1_), channel_id=1, source_target_pairs={{0,2},{1,3},{2,0},{3,1},{4,6},{5,7},{6,4},{7,5},{8,10},{9,11},{10,... | collective-permute-start | bytes 393224 | tf_op jit(solution)/shard_map/ppermute | solution.py:385
  6.7 11.1 %collective-permute-start = (bf16[2,32,1024]{2,1,0:T(8,128)(2,1)S(1)}, bf16[2,32,1024]{2,1,0:T(8,128)(2,1)S(1)}, u32[]{:S(2)}, u32[]{:S(2)}) collective-permute-start(bf16[2,32,1024]{2,1,0:T(8,128)(2,1)S(1)} %get-tuple-element.190.refs_1_), channel_id=1, source_target_pairs={{0,1},{1,0},{2,3},{3,2},{4,5},{5,4},{6,7},{7,6},{8,9},{9,8},{10,11... | collective-permute-start | bytes 393224 | tf_op jit(solution)/shard_map/ppermute | solution.py:385
  23.7 12.5 %collective-permute-start.4 = (bf16[64,3584]{1,0:T(8,128)(2,1)S(1)}, bf16[64,3584]{1,0:T(8,128)(2,1)S(1)}, u32[]{:S(2)}, u32[]{:S(2)}) collective-permute-start(bf16[64,3584]{1,0:T(8,128)(2,1)S(1)} %get-tuple-element.105), channel_id=1, source_target_pairs={{0,8},{4,12},{8,0},{12,4},{16,24},{20,28},{24,16},{28,20},{1,9},{5... | collective-permute-start | bytes 1376264 | tf_op jit(solution)/shard_map/ppermute | solution.py:385
  25.8 12.9 %collective-permute-start.10 = (bf16[64,3584]{1,0:T(8,128)(2,1)S(1)}, bf16[64,3584]{1,0:T(8,128)(2,1)S(1)}, u32[]{:S(2)}, u32[]{:S(2)}) collective-permute-start(bf16[64,3584]{1,0:T(8,128)(2,1)S(1)} %get-tuple-element.113), channel_id=1, source_target_pairs={{0,16},{4,20},{8,24},{12,28},{16,0},{20,4},{24,8},{28,12},{1,17},{... | collective-permute-start | bytes 1376264 | tf_op jit(solution)/shard_map/ppermute | solution.py:385
  27.4 11.3 %collective-permute-start.9 = (bf16[2,32,1024]{2,1,0:T(8,128)(2,1)S(1)}, bf16[2,32,1024]{2,1,0:T(8,128)(2,1)S(1)}, u32[]{:S(2)}, u32[]{:S(2)}) collective-permute-start(bf16[2,32,1024]{2,1,0:T(8,128)(2,1)S(1)} %get-tuple-element.189.refs_1_), channel_id=1, source_target_pairs={{0,3},{1,2},{2,1},{3,0},{4,7},{5,6},{6,5},{7,4},{8,11},{9,10},{10,... | collective-permute-start | bytes 393224 | tf_op jit(solution)/shard_map/ppermute | solution.py:385
  30.3 11.1 %collective-permute-start.8 = (bf16[2,32,1024]{2,1,0:T(8,128)(2,1)S(1)}, bf16[2,32,1024]{2,1,0:T(8,128)(2,1)S(1)}, u32[]{:S(2)}, u32[]{:S(2)}) collective-permute-start(bf16[2,32,1024]{2,1,0:T(8,128)(2,1)S(1)} %get-tuple-element.189.refs_1_), channel_id=1, source_target_pairs={{0,2},{1,3},{2,0},{3,1},{4,6},{5,7},{6,4},{7,5},{8,10},{9,11},{10,... | collective-permute-start | bytes 393224 | tf_op jit(solution)/shard_map/ppermute | solution.py:385
  30.3 11.1 %collective-permute-start.7 = (bf16[2,32,1024]{2,1,0:T(8,128)(2,1)S(1)}, bf16[2,32,1024]{2,1,0:T(8,128)(2,1)S(1)}, u32[]{:S(2)}, u32[]{:S(2)}) collective-permute-start(bf16[2,32,1024]{2,1,0:T(8,128)(2,1)S(1)} %get-tuple-element.189.refs_1_), channel_id=1, source_target_pairs={{0,1},{1,0},{2,3},{3,2},{4,5},{5,4},{6,7},{7,6},{8,9},{9,8},{10,11... | collective-permute-start | bytes 393224 | tf_op jit(solution)/shard_map/ppermute | solution.py:385
  47.1 7.6 %collective-permute-start.6 = (bf16[32,3584]{1,0:T(8,128)(2,1)S(1)}, bf16[32,3584]{1,0:T(8,128)(2,1)S(1)}, u32[]{:S(2)}, u32[]{:S(2)}) collective-permute-start(bf16[32,3584]{1,0:T(8,128)(2,1)S(1)} %get-tuple-element.111), channel_id=1, source_target_pairs={{0,16},{4,20},{8,24},{12,28},{16,0},{20,4},{24,8},{28,12},{1,17},{... | collective-permute-start | bytes 688136 | tf_op jit(solution)/shard_map/ppermute | solution.py:385
  47.6 8.1 %collective-permute-start.13 = (bf16[32,3584]{1,0:T(8,128)(2,1)S(1)}, bf16[32,3584]{1,0:T(8,128)(2,1)S(1)}, u32[]{:S(2)}, u32[]{:S(2)}) collective-permute-start(bf16[32,3584]{1,0:T(8,128)(2,1)S(1)} %get-tuple-element.128), channel_id=1, source_target_pairs={{0,8},{4,12},{8,0},{12,4},{16,24},{20,28},{24,16},{28,20},{1,9},{5... | collective-permute-start | bytes 688136 | tf_op jit(solution)/shard_map/ppermute | solution.py:385
  55.1 8.6 %collective-permute-start.16 = (bf16[32,3584]{1,0:T(8,128)(2,1)S(1)}, bf16[32,3584]{1,0:T(8,128)(2,1)S(1)}, u32[]{:S(2)}, u32[]{:S(2)}) collective-permute-start(bf16[32,3584]{1,0:T(8,128)(2,1)S(1)} %get-tuple-element.134.refs_0_), channel_id=1, source_target_pairs={{0,16},{4,20},{8,24},{12,28},{16,0},{20,4},{24,8},{28,12},{1,17},{... | collective-permute-start | bytes 688136 | tf_op jit(solution)/shard_map/ppermute | solution.py:385
  56.1 9.5 %collective-permute-start.15 = (bf16[32,3584]{1,0:T(8,128)(2,1)S(1)}, bf16[32,3584]{1,0:T(8,128)(2,1)S(1)}, u32[]{:S(2)}, u32[]{:S(2)}) collective-permute-start(bf16[32,3584]{1,0:T(8,128)(2,1)S(1)} %get-tuple-element.133.refs_0_), channel_id=1, source_target_pairs={{0,8},{4,12},{8,0},{12,4},{16,24},{20,28},{24,16},{28,20},{1,9},{5... | collective-permute-start | bytes 688136 | tf_op jit(solution)/shard_map/ppermute | solution.py:385
  57.8 16.7 %collective-permute-start.14 = (bf16[64,3584]{1,0:T(8,128)(2,1)S(1)}, bf16[64,3584]{1,0:T(8,128)(2,1)S(1)}, u32[]{:S(2)}, u32[]{:S(2)}) collective-permute-start(bf16[64,3584]{1,0:T(8,128)(2,1)S(1)} %get-tuple-element.132), channel_id=1, source_target_pairs={{0,8},{4,12},{8,0},{12,4},{16,24},{20,28},{24,16},{28,20},{1,9},{5... | collective-permute-start | bytes 1376264 | tf_op jit(solution)/shard_map/ppermute | solution.py:385
  58.2 18.0 %collective-permute-start.20 = (bf16[64,3584]{1,0:T(8,128)(2,1)S(1)}, bf16[64,3584]{1,0:T(8,128)(2,1)S(1)}, u32[]{:S(2)}, u32[]{:S(2)}) collective-permute-start(bf16[64,3584]{1,0:T(8,128)(2,1)S(1)} %get-tuple-element.143), channel_id=1, source_target_pairs={{0,16},{4,20},{8,24},{12,28},{16,0},{20,4},{24,8},{28,12},{1,17},{... | collective-permute-start | bytes 1376264 | tf_op jit(solution)/shard_map/ppermute | solution.py:385
  63.8 20.6 %collective-permute-start.19 = (bf16[64,3584]{1,0:T(8,128)(2,1)S(1)}, bf16[64,3584]{1,0:T(8,128)(2,1)S(1)}, u32[]{:S(2)}, u32[]{:S(2)}) collective-permute-start(bf16[64,3584]{1,0:T(8,128)(2,1)S(1)} %get-tuple-element.141.refs_0_), channel_id=1, source_target_pairs={{0,8},{4,12},{8,0},{12,4},{16,24},{20,28},{24,16},{28,20},{1,9},{5... | collective-permute-start | bytes 1376264 | tf_op jit(solution)/shard_map/ppermute | solution.py:385
  65.6 18.9 %collective-permute-start.18 = (bf16[64,3584]{1,0:T(8,128)(2,1)S(1)}, bf16[64,3584]{1,0:T(8,128)(2,1)S(1)}, u32[]{:S(2)}, u32[]{:S(2)}) collective-permute-start(bf16[64,3584]{1,0:T(8,128)(2,1)S(1)} %get-tuple-element.140.refs_0_), channel_id=1, source_target_pairs={{0,16},{4,20},{8,24},{12,28},{16,0},{20,4},{24,8},{28,12},{1,17},{... | collective-permute-start | bytes 1376264 | tf_op jit(solution)/shard_map/ppermute | solution.py:385
  74.6 11.9 %collective-permute-start.17 = (bf16[32,3584]{1,0:T(8,128)(2,1)S(1)}, bf16[32,3584]{1,0:T(8,128)(2,1)S(1)}, u32[]{:S(2)}, u32[]{:S(2)}) collective-permute-start(bf16[32,3584]{1,0:T(8,128)(2,1)S(1)} %get-tuple-element.139), channel_id=1, source_target_pairs={{0,16},{4,20},{8,24},{12,28},{16,0},{20,4},{24,8},{28,12},{1,17},{... | collective-permute-start | bytes 688136 | tf_op jit(solution)/shard_map/ppermute | solution.py:385
  76.3 11.2 %collective-permute-start.21 = (bf16[32,3584]{1,0:T(8,128)(2,1)S(1)}, bf16[32,3584]{1,0:T(8,128)(2,1)S(1)}, u32[]{:S(2)}, u32[]{:S(2)}) collective-permute-start(bf16[32,3584]{1,0:T(8,128)(2,1)S(1)} %get-tuple-element.150), channel_id=1, source_target_pairs={{0,8},{4,12},{8,0},{12,4},{16,24},{20,28},{24,16},{28,20},{1,9},{5... | collective-permute-start | bytes 688136 | tf_op jit(solution)/shard_map/ppermute | solution.py:385
  84.4 13.2 %collective-permute-start.25 = (bf16[128,3584]{1,0:T(8,128)(2,1)S(1)}, bf16[128,3584]{1,0:T(8,128)(2,1)S(1)}, u32[]{:S(2)}, u32[]{:S(2)}) collective-permute-start(bf16[128,3584]{1,0:T(8,128)(2,1)S(1)} %get-tuple-element.160.refs_1_.refs_3_), channel_id=1, source_target_pairs={{0,4},{4,0},{8,12},{12,8},{16,20},{20,16},{24,28},{28,24},{1,5},{5... | collective-permute-start | bytes 2752520 | tf_op jit(solution)/shard_map/ppermute | solution.py:385
  84.6 16.0 %collective-permute-start.24 = (bf16[128,3584]{1,0:T(8,128)(2,1)S(1)}, bf16[128,3584]{1,0:T(8,128)(2,1)S(1)}, u32[]{:S(2)}, u32[]{:S(2)}) collective-permute-start(bf16[128,3584]{1,0:T(8,128)(2,1)S(1)} %get-tuple-element.159.refs_1_.refs_3_), channel_id=1, source_target_pairs={{0,4},{4,0},{8,12},{12,8},{16,20},{20,16},{24,28},{28,24},{1,5},{5... | collective-permute-start | bytes 2752520 | tf_op jit(solution)/shard_map/ppermute | solution.py:385
  86.9 6.2 %collective-permute-start.23 = (bf16[32,3584]{1,0:T(8,128)(2,1)S(1)}, bf16[32,3584]{1,0:T(8,128)(2,1)S(1)}, u32[]{:S(2)}, u32[]{:S(2)}) collective-permute-start(bf16[32,3584]{1,0:T(8,128)(2,1)S(1)} %get-tuple-element.154.refs_0_), channel_id=1, source_target_pairs={{0,16},{4,20},{8,24},{12,28},{16,0},{20,4},{24,8},{28,12},{1,17},{... | collective-permute-start | bytes 688136 | tf_op jit(solution)/shard_map/ppermute | solution.py:385
  87.9 8.0 %collective-permute-start.22 = (bf16[32,3584]{1,0:T(8,128)(2,1)S(1)}, bf16[32,3584]{1,0:T(8,128)(2,1)S(1)}, u32[]{:S(2)}, u32[]{:S(2)}) collective-permute-start(bf16[32,3584]{1,0:T(8,128)(2,1)S(1)} %get-tuple-element.153.refs_0_), channel_id=1, source_target_pairs={{0,8},{4,12},{8,0},{12,4},{16,24},{20,28},{24,16},{28,20},{1,9},{5... | collective-permute-start | bytes 688136 | tf_op jit(solution)/shard_map/ppermute | solution.py:385
  93.2 11.5 %collective-permute-start.30 = (bf16[64,3584]{1,0:T(8,128)(2,1)S(1)}, bf16[64,3584]{1,0:T(8,128)(2,1)S(1)}, u32[]{:S(2)}, u32[]{:S(2)}) collective-permute-start(bf16[64,3584]{1,0:T(8,128)(2,1)S(1)} %get-tuple-element.169.refs_0_), channel_id=1, source_target_pairs={{0,8},{4,12},{8,0},{12,4},{16,24},{20,28},{24,16},{28,20},{1,9},{5... | collective-permute-start | bytes 1376264 | tf_op jit(solution)/shard_map/ppermute | solution.py:385
  95.9 10.1 %collective-permute-start.29 = (bf16[64,3584]{1,0:T(8,128)(2,1)S(1)}, bf16[64,3584]{1,0:T(8,128)(2,1)S(1)}, u32[]{:S(2)}, u32[]{:S(2)}) collective-permute-start(bf16[64,3584]{1,0:T(8,128)(2,1)S(1)} %get-tuple-element.168.refs_0_), channel_id=1, source_target_pairs={{0,16},{4,20},{8,24},{12,28},{16,0},{20,4},{24,8},{28,12},{1,17},{... | collective-permute-start | bytes 1376264 | tf_op jit(solution)/shard_map/ppermute | solution.py:385
  104.8 5.8 %collective-permute-start.32 = (bf16[128,3584]{1,0:T(8,128)(2,1)S(1)}, bf16[128,3584]{1,0:T(8,128)(2,1)S(1)}, u32[]{:S(2)}, u32[]{:S(2)}) collective-permute-start(bf16[128,3584]{1,0:T(8,128)(2,1)S(1)} %get-tuple-element.173.refs_1_.refs_5_), channel_id=1, source_target_pairs={{0,4},{4,0},{8,12},{12,8},{16,20},{20,16},{24,28},{28,24},{1,5},{5... | collective-permute-start | bytes 2752520 | tf_op jit(solution)/shard_map/ppermute | solution.py:385
  106.0 7.3 %collective-permute-start.31 = (bf16[128,3584]{1,0:T(8,128)(2,1)S(1)}, bf16[128,3584]{1,0:T(8,128)(2,1)S(1)}, u32[]{:S(2)}, u32[]{:S(2)}) collective-permute-start(bf16[128,3584]{1,0:T(8,128)(2,1)S(1)} %get-tuple-element.172.refs_1_.refs_5_), channel_id=1, source_target_pairs={{0,4},{4,0},{8,12},{12,8},{16,20},{20,16},{24,28},{28,24},{1,5},{5... | collective-permute-start | bytes 2752520 | tf_op jit(solution)/shard_map/ppermute | solution.py:385
  106.1 12.8 %collective-permute-start.26 = (bf16[64,1024]{1,0:T(8,128)(2,1)S(1)}, bf16[64,1024]{1,0:T(8,128)(2,1)S(1)}, u32[]{:S(2)}, u32[]{:S(2)}) collective-permute-start(bf16[64,1024]{1,0:T(8,128)(2,1)S(1)} %get-tuple-element.165), channel_id=1, source_target_pairs={{0,1},{1,0},{2,3},{3,2},{4,5},{5,4},{6,7},{7,6},{8,9},{9,8},{10,11... | collective-permute-start | bytes 393224 | tf_op jit(solution)/shard_map/ppermute | solution.py:385
  106.2 25.3 %collective-permute-start.27 = (bf16[64,1024]{1,0:T(8,128)(2,1)S(1)}, bf16[64,1024]{1,0:T(8,128)(2,1)S(1)}, u32[]{:S(2)}, u32[]{:S(2)}) collective-permute-start(bf16[64,1024]{1,0:T(8,128)(2,1)S(1)} %get-tuple-element.166), channel_id=1, source_target_pairs={{0,2},{1,3},{2,0},{3,1},{4,6},{5,7},{6,4},{7,5},{8,10},{9,11},{10,... | collective-permute-start | bytes 393224 | tf_op jit(solution)/shard_map/ppermute | solution.py:385
  108.7 22.8 %collective-permute-start.28 = (bf16[64,1024]{1,0:T(8,128)(2,1)S(1)}, bf16[64,1024]{1,0:T(8,128)(2,1)S(1)}, u32[]{:S(2)}, u32[]{:S(2)}) collective-permute-start(bf16[64,1024]{1,0:T(8,128)(2,1)S(1)} %get-tuple-element.167), channel_id=1, source_target_pairs={{0,3},{1,2},{2,1},{3,0},{4,7},{5,6},{6,5},{7,4},{8,11},{9,10},{10,... | collective-permute-start | bytes 393224 | tf_op jit(solution)/shard_map/ppermute | solution.py:385
  116.3 15.2 %collective-permute-start.33 = (bf16[64,1024]{1,0:T(8,128)(2,1)S(1)}, bf16[64,1024]{1,0:T(8,128)(2,1)S(1)}, u32[]{:S(2)}, u32[]{:S(2)}) collective-permute-start(bf16[64,1024]{1,0:T(8,128)(2,1)S(1)} %get-tuple-element.178), channel_id=1, source_target_pairs={{0,1},{1,0},{2,3},{3,2},{4,5},{5,4},{6,7},{7,6},{8,9},{9,8},{10,11... | collective-permute-start | bytes 393224 | tf_op jit(solution)/shard_map/ppermute | solution.py:385
  116.4 15.2 %collective-permute-start.34 = (bf16[64,1024]{1,0:T(8,128)(2,1)S(1)}, bf16[64,1024]{1,0:T(8,128)(2,1)S(1)}, u32[]{:S(2)}, u32[]{:S(2)}) collective-permute-start(bf16[64,1024]{1,0:T(8,128)(2,1)S(1)} %get-tuple-element.179), channel_id=1, source_target_pairs={{0,2},{1,3},{2,0},{3,1},{4,6},{5,7},{6,4},{7,5},{8,10},{9,11},{10,... | collective-permute-start | bytes 393224 | tf_op jit(solution)/shard_map/ppermute | solution.py:385
  118.9 12.6 %collective-permute-start.35 = (bf16[64,1024]{1,0:T(8,128)(2,1)S(1)}, bf16[64,1024]{1,0:T(8,128)(2,1)S(1)}, u32[]{:S(2)}, u32[]{:S(2)}) collective-permute-start(bf16[64,1024]{1,0:T(8,128)(2,1)S(1)} %get-tuple-element.180), channel_id=1, source_target_pairs={{0,3},{1,2},{2,1},{3,0},{4,7},{5,6},{6,5},{7,4},{8,11},{9,10},{10,... | collective-permute-start | bytes 393224 | tf_op jit(solution)/shard_map/ppermute | solution.py:385
  (5 other events, 25.7 us)

commit v2 on v1

--- a/solution.py
+++ b/solution.py
@@ -37,7 +37,7 @@
     def __init__(self):
         self.turn = None
 
-    def __call__(self, kernel, name, out_shape, out_specs, in_specs, operands, scratch=(), aliases=None):
+    def __call__(self, kernel, name, out_shape, out_specs, in_specs, operands, scratch=(), limit=vmem_limit):
         homes = {id(in_vmem): pltpu.VMEM, id(anywhere): pltpu.HBM}
         in_specs, operands = list(in_specs), list(operands)
         if self.turn is not None:
@@ -61,8 +61,7 @@
             in_specs=in_specs,
             out_specs=[*out_specs, in_vmem],
             scratch_shapes=list(scratch),
-            input_output_aliases=aliases or {},
-            compiler_params=pltpu.CompilerParams(vmem_limit_bytes=vmem_limit),
+            compiler_params=pltpu.CompilerParams(vmem_limit_bytes=limit),
             cost_estimate=pl.CostEstimate(flops=1, transcendentals=0, bytes_accessed=1),
             name=name,
         )(*placed)
@@ -222,107 +221,97 @@
     )
 
 
-def input_kernel(first, groups, has_before, finished, given, place, near_ref, far_ref, w_ref, *refs):
-    half, width = near_ref.shape
+def input_kernel(groups, slabs, given, place, *refs):
+    grads = [refs[2 * c : 2 * c + 2] for c in range(slabs)]
+    w_ref = refs[2 * slabs]
+    outs = refs[2 * slabs + 1 : 2 * slabs + 1 + given]
+    turned, total, upright = refs[2 * slabs + 1 + given :]
+    half, width = grads[0][0].shape
     rows = 2 * half // groups
     tall = w_ref.shape[0]
-    before = refs[0] if has_before else None
-    outs = refs[has_before : has_before + given]
-    scratch = refs[has_before + given :]
-    turned = scratch[0]
-    total = scratch[1] if finished else outs[0]
     wide = 128 * group_of(width // 128, 4)
-    for at in range(0, width, wide):
-        here = slice(at, at + wide)
-        grad = jnp.concatenate([near_ref[:, here], far_ref[:, here]], axis=0)
-        turned[here, :] = grad.T
-    high = 128 * group_of(tall // 128, 2)
+    for c in range(slabs):
+        for at in range(0, width, wide):
+            here = slice(at, at + wide)
+            grad = jnp.concatenate([g[:, here] for g in grads[c]], axis=0)
+            turned[c * width + at : c * width + at + wide, :] = grad.T
+    high = 128 * group_of(tall // 128, 4)
     for at in range(0, tall, high):
         here = slice(at, at + high)
-        product = jnp.dot(
-            w_ref[here, first : first + width], turned[...], preferred_element_type=jnp.float32
-        )
-        total[here, :] = product + before[here, :] if has_before else product
-    if finished:
-        upright = scratch[2]
-        upright[...] = total[...].T
-        each = groups // given
-        for i in range(groups):
-            start = pl.multiple_of(place[i] * rows, rows)
-            out_ref = outs[i // each]
-            at = i % each * rows
-            out_ref[at : at + rows, :] = upright[pl.ds(start, rows), :].astype(out_ref.dtype)
-
-
-def input_partial(core, near, far, weight, first, place, before, pieces):
-    half, width = near.shape
+        total[here, :] = jnp.dot(w_ref[here, :], turned[...], preferred_element_type=jnp.float32)
+    upright[...] = total[...].T
+    each = groups // given
+    for i in range(groups):
+        start = pl.multiple_of(place[i] * rows, rows)
+        out_ref = outs[i // each]
+        at = i % each * rows
+        out_ref[at : at + rows, :] = upright[pl.ds(start, rows), :].astype(out_ref.dtype)
+
+
+def input_partial(core, grads, weight, place, pieces):
+    slabs = len(grads)
+    half, width = grads[0][0].shape
     tall = weight.shape[0]
     both = 2 * half
-    if pieces:
-        outs = [pltpu.VMEM((both // pieces, tall), jnp.float32)]
-        outs += [pltpu.VMEM((both // pieces, tall), jnp.bfloat16)] * (pieces - 1)
-    else:
-        outs = [pltpu.VMEM((tall, both), jnp.float32)]
-    has_before = before is not None
-    scratch = [pltpu.VMEM((width, both), near.dtype)]
-    if pieces:
-        scratch += [pltpu.VMEM((tall, both), jnp.float32), pltpu.VMEM((both, tall), jnp.float32)]
+    outs = [pltpu.VMEM((both // pieces, tall), jnp.float32)]
+    outs += [pltpu.VMEM((both // pieces, tall), jnp.bfloat16)] * (pieces - 1)
     return core(
-        functools.partial(
-            input_kernel, first, place.shape[0], has_before, pieces > 0, len(outs)
-        ),
+        functools.partial(input_kernel, place.shape[0], slabs, len(outs)),
         "input_partial",
         outs,
         [in_vmem] * len(outs),
-        [in_smem] + [in_vmem] * (4 if has_before else 3),
-        (place, near, far, weight) + ((before,) if has_before else ()),
-        scratch=scratch,
-    )
-
-
-def weight_kernel(row_blocks, col_blocks, first, parts, has_before, code, *refs):
+        [in_smem] + [in_vmem] * (2 * slabs + 1),
+        (place, *(g for pair in grads for g in pair), weight),
+        scratch=[
+            pltpu.VMEM((slabs * width, both), weight.dtype),
+            pltpu.VMEM((tall, both), jnp.float32),
+            pltpu.VMEM((both, tall), jnp.float32),
+        ],
+    )
+
+
+def weight_kernel(row_blocks, col_blocks, slabs, parts, code, *refs):
     turned = refs[:parts]
-    grads = refs[parts : 3 * parts]
-    out_ref, made, sem = refs[3 * parts + has_before :]
+    grads = [refs[parts * (1 + 2 * c) : parts * (3 + 2 * c)] for c in range(slabs)]
+    out_ref, made, sem = refs[parts * (1 + 2 * slabs) :]
     blk = made.shape[-1]
-    width = grads[0].shape[1]
-    here = width // blk
+    here = col_blocks // slabs
     per_step = group_of(here, 4)
     wide = per_step * blk
     high = group_of(row_blocks, 2)
-    for j in range(here // per_step):
-        grad = jnp.concatenate([g[:, j * wide : (j + 1) * wide] for g in grads], axis=0)
+    for j in range(col_blocks // per_step):
+        c, left = divmod(j * per_step, here)
+        columns = slice(left * blk, left * blk + wide)
+        grad = jnp.concatenate([g[:, columns] for g in grads[c]], axis=0)
         for r in range(0, row_blocks, high):
             rows = slice(r * blk, (r + high) * blk)
             features = jnp.concatenate([t[rows, :] for t in turned], axis=1)
             product = jnp.dot(features, grad, preferred_element_type=jnp.float32)
             for i in range(high):
-                for c in range(per_step):
-                    entry = code[(r + i) * col_blocks + first // blk + j * per_step + c]
+                for b in range(per_step):
+                    entry = code[(r + i) * col_blocks + j * per_step + b]
                     live = lax.rem(entry, 2).astype(jnp.float32)
-                    at = (j * row_blocks + r + i) * per_step + c
-                    block = product[i * blk : (i + 1) * blk, c * blk : (c + 1) * blk] * live
+                    at = (j * row_blocks + r + i) * per_step + b
+                    block = product[i * blk : (i + 1) * blk, b * blk : (b + 1) * blk] * live
                     made[at] = block.astype(made.dtype)
                     pltpu.make_async_copy(
                         made.at[at], out_ref.at[0, 0, lax.div(entry, 2)], sem
                     ).start(priority=at % 2)
-    pltpu.make_async_copy(made, out_ref.at[0, 0, pl.ds(0, made.shape[0])], sem).wait()
-
-
-def weight_gradient(core, turned, grads, code, first, row_blocks, col_blocks, blk, before):
-    parts = len(turned)
-    has_before = before is not None
-    here = row_blocks * grads[0].shape[1] // blk
+    pltpu.make_async_copy(made, out_ref.at[0, 0], sem).wait()
+
+
+def weight_gradient(core, turned, grads, code, row_blocks, col_blocks, blk, slabs):
     arrays = [*turned, *grads]
+    blocks = row_blocks * col_blocks
     [out] = core(
-        functools.partial(weight_kernel, row_blocks, col_blocks, first, parts, has_before),
+        functools.partial(weight_kernel, row_blocks, col_blocks, slabs, len(turned)),
         "weight_gradient",
-        [jax.ShapeDtypeStruct((1, 1, row_blocks * col_blocks, blk, blk), jnp.bfloat16)],
+        [jax.ShapeDtypeStruct((1, 1, blocks, blk, blk), jnp.bfloat16)],
         [anywhere],
-        [in_smem] + [in_vmem] * len(arrays) + [anywhere] * has_before,
-        (code, *arrays) + ((before,) if has_before else ()),
-        scratch=[pltpu.VMEM((here, blk, blk), jnp.bfloat16), pltpu.SemaphoreType.DMA],
-        aliases={1 + len(arrays): 0} if has_before else None,
+        [in_smem] + [in_vmem] * len(arrays),
+        (code, *arrays),
+        scratch=[pltpu.VMEM((blocks, blk, blk), jnp.bfloat16), pltpu.SemaphoreType.DMA],
+        limit=vmem_limit + 2 * blocks * blk * blk,
     )
     return out
 
@@ -433,7 +422,7 @@
     paths = [far_bits if at % 2 == 0 else far_bits[::-1] for at in range(len(units))]
     state = {}
     full, turned = {}, {}
-    activations, sums, input_grads = {}, {}, {}
+    activations, input_grads = {}, {}
 
     def begin(k, c, path):
         if c == 0:
@@ -456,16 +445,14 @@
         state[k, c] = (near, swap(near, "row", n_row, ([1] + path)[at]))
 
     def finish(k, c, path):
-        last = c + 1 == slabs
-        cut = (n_col if direct else 1) * last
-        found = input_partial(
-            core, *state[k, c], weight, c * width, place, sums.get((k, c - 1)), cut
-        )
-        sums[k, c] = found[0]
-        if last and direct:
+        if c + 1 < slabs:
+            return
+        grads = [state[k, c] for c in range(slabs)]
+        found = input_partial(core, grads, weight, place, n_col if direct else 1)
+        if direct:
             input_grads[k] = [found[0]]
             input_grads[k] += [swap(found[m], "col", n_col, m) for m in range(1, n_col)]
-        elif last:
+        else:
             total = found[0].reshape(n_col, col_groups * sizes[k], tall)
             total = lax.psum_scatter(total, "col", scatter_dimension=0, tiled=True)[0]
             input_grads[k] = [total]
@@ -486,19 +473,16 @@
                 [(starts[k], c * width) for k, c in units],
                 grad_act.shape,
             )
-    weight_grad = None
-    for c in range(slabs):
-        weight_grad = weight_gradient(
-            core,
-            [turned[k] for k in range(parts)],
-            [g for k in range(parts) for g in state[k, c]],
-            code,
-            c * width,
-            row_blocks,
-            col_blocks,
-            blk,
-            weight_grad,
-        )
+    weight_grad = weight_gradient(
+        core,
+        [turned[k] for k in range(parts)],
+        [g for c in range(slabs) for k in range(parts) for g in state[k, c]],
+        code,
+        row_blocks,
+        col_blocks,
+        blk,
+        slabs,
+    )
     input_grad = total_input(
         core, [input_grads[k] for k in range(parts)], col_groups, starts, sizes
     )

time: 132 us -> 132 us (level)
  waiting for transfers between devices: 41.9 us -> 46.8 us
  Pallas kernels: 45.1 us -> 40.9 us
    ppermute x36, waiting for transfers between devices: 41.9 us -> 46.8 us  [swap(): return lax.ppermute(array, axis, [(i, i ^ bit) for i in range(size)])]
    pallas_call x35 -> x32, Pallas kernels: 45.1 us -> 40.9 us  [__call__(): pl.pallas_call(body, out_shape=[*out_shape, pltpu.VMEM((8, 128), jnp.floa...]
  transfers between devices with their start and end apart: 36 -> 36, of which waited for: 14 -> 15; matrix products, arithmetic and copies ran while one was open for 1% -> 1% of each run, Pallas kernels for 29% -> 26%
where the time goes in v2:
time: 132 us
  waiting for transfers between devices  46.8 us (35%)
  Pallas kernels  40.9 us (31%)
  starting transfers between devices  39.9 us (30%)
  between operations  1.61 us (1%)
  other arithmetic  1.56 us (1%)
    ppermute x36, waiting for transfers between devices, swap(): return lax.ppermute(array, axis, [(i, i ^ bit) for i in range(size)])  46.8 us
    pallas_call x32, Pallas kernels, __call__(): pl.pallas_call(body, out_shape=[*out_shape, pltpu.VMEM((8, 128), jnp.floa...  40.9 us
    ppermute x36, starting transfers between devices, swap(): return lax.ppermute(array, axis, [(i, i ^ bit) for i in range(size)])  39.9 us
  transfers between devices with their start and end apart: 36, of which 15 were waited for; matrix products, arithmetic and copies ran while one was open for 1% of the time, Pallas kernels for 26%

profile of v2, /device:TPU:0, one launch (start us, length us, event | category | flops | bytes accessed | tf_op | source)
XLA Modules:
  0.0 131.8 jit_solution(6898343375452759638)
XLA Ops:
  1.6 5.1 %collective-permute-start.2 = (bf16[2,32,1024]{2,1,0:T(8,128)(2,1)S(1)}, bf16[2,32,1024]{2,1,0:T(8,128)(2,1)S(1)}, u32[]{:S(2)}, u32[]{:S(2)}) collective-permute-start(bf16[2,32,1024]{2,1,0:T(8,128)(2,1)S(1)} %get-tuple-element.178.refs_1_), channel_id=1, source_target_pairs={{0,3},{1,2},{2,1},{3,0},{4,7},{5,6},{6,5},{7,4},{8,11},{9,10},{10,... | collective-permute-start | bytes 393224 | tf_op jit(solution)/shard_map/ppermute | solution.py:374
  9.6 7.2 %dense_tile.1 = (bf16[1024,7168]{1,0:T(8,128)(2,1)S(1)}, f32[8,128]{1,0:T(8,128)S(1)}) custom-call(s32[448]{0:T(512)S(1)} %select_reduce_fusion.refs_0_, bf16[1,1,448,128,128]{4,3,2,1,0:T(8,128)(2,1)} %refs_1_.1, s32[8]{0:T(128)S(1)} %broadcast_xor_fusion.refs_2_.refs_0_, s32[8]{0:T(128)S(1)} %shift-right-arithmetic_add_fusion.refs_3_.refs_0_), custom_call_target="tpu_custom_call" | custom-call | flops 1 | bytes 1 | tf_op jit(solution)/shard_map/dense_tile/pallas_call | solution.py:58
  18.6 2.1 %forward.4 = (f32[128,3584]{1,0:T(8,128)S(1)}, bf16[128,3584]{1,0:T(8,128)(2,1)S(1)}, f32[8,128]{1,0:T(8,128)S(1)}) custom-call(bf16[256,1024]{1,0:T(8,128)(2,1)S(1)} %get-tuple-element.91.refs_0_, bf16[1024,7168]{1,0:T(8,128)(2,1)S(1)} %get-tuple-element.92.refs_1_.refs_5_, f32[8,128]{1,0:T(8,128)S(1)} %get-tuple-element.93.refs_2_), custom_call_target="tpu_custom_call" | custom-call | flops 1 | bytes 1 | tf_op jit(solution)/shard_map/forward/pallas_call | solution.py:58
  20.8 2.1 %forward.5 = (f32[128,3584]{1,0:T(8,128)S(1)}, bf16[128,3584]{1,0:T(8,128)(2,1)S(1)}, f32[8,128]{1,0:T(8,128)S(1)}) custom-call(bf16[256,1024]{1,0:T(8,128)(2,1)S(1)} %get-tuple-element.91.refs_0_, bf16[1024,7168]{1,0:T(8,128)(2,1)S(1)} %get-tuple-element.92.refs_1_.refs_5_, f32[8,128]{1,0:T(8,128)S(1)} %get-tuple-element.96.refs_2_), custom_call_target="tpu_custom_call" | custom-call | flops 1 | bytes 1 | tf_op jit(solution)/shard_map/forward/pallas_call | solution.py:58
  23.7 1.6 %collective-permute-start.4 = (bf16[64,3584]{1,0:T(8,128)(2,1)S(1)}, bf16[64,3584]{1,0:T(8,128)(2,1)S(1)}, u32[]{:S(2)}, u32[]{:S(2)}) collective-permute-start(bf16[64,3584]{1,0:T(8,128)(2,1)S(1)} %get-tuple-element.99), channel_id=1, source_target_pairs={{0,8},{4,12},{8,0},{12,4},{16,24},{20,28},{24,16},{28,20},{1,9},{5... | collective-permute-start | bytes 1376264 | tf_op jit(solution)/shard_map/ppermute | solution.py:374
  25.8 1.6 %collective-permute-start.10 = (bf16[64,3584]{1,0:T(8,128)(2,1)S(1)}, bf16[64,3584]{1,0:T(8,128)(2,1)S(1)}, u32[]{:S(2)}, u32[]{:S(2)}) collective-permute-start(bf16[64,3584]{1,0:T(8,128)(2,1)S(1)} %get-tuple-element.107), channel_id=1, source_target_pairs={{0,16},{4,20},{8,24},{12,28},{16,0},{20,4},{24,8},{28,12},{1,17},{... | collective-permute-start | bytes 1376264 | tf_op jit(solution)/shard_map/ppermute | solution.py:374
  27.4 3.2 %collective-permute-start.9 = (bf16[2,32,1024]{2,1,0:T(8,128)(2,1)S(1)}, bf16[2,32,1024]{2,1,0:T(8,128)(2,1)S(1)}, u32[]{:S(2)}, u32[]{:S(2)}) collective-permute-start(bf16[2,32,1024]{2,1,0:T(8,128)(2,1)S(1)} %get-tuple-element.177.refs_1_), channel_id=1, source_target_pairs={{0,3},{1,2},{2,1},{3,0},{4,7},{5,6},{6,5},{7,4},{8,11},{9,10},{10,... | collective-permute-start | bytes 393224 | tf_op jit(solution)/shard_map/ppermute | solution.py:374
  31.8 4.4 %collective-permute-done.4.refs_1_ = bf16[64,3584]{1,0:T(8,128)(2,1)S(1)} collective-permute-done((bf16[64,3584]{1,0:T(8,128)(2,1)S(1)}, bf16[64,3584]{1,0:T(8,128)(2,1)S(1)}, u32[]{:S(2)}, u32[]{:S(2)}) %collective-permute-start.4) | collective-permute-done | bytes 458784 | tf_op jit(solution)/shard_map/ppermute | solution.py:374
  36.3 2.3 %collective-permute-done.10.refs_1_ = bf16[64,3584]{1,0:T(8,128)(2,1)S(1)} collective-permute-done((bf16[64,3584]{1,0:T(8,128)(2,1)S(1)}, bf16[64,3584]{1,0:T(8,128)(2,1)S(1)}, u32[]{:S(2)}, u32[]{:S(2)}) %collective-permute-start.10) | collective-permute-done | bytes 458784 | tf_op jit(solution)/shard_map/ppermute | solution.py:374
  38.7 2.7 %collective-permute-done.8.refs_3_ = bf16[2,32,1024]{2,1,0:T(8,128)(2,1)S(1)} collective-permute-done((bf16[2,32,1024]{2,1,0:T(8,128)(2,1)S(1)}, bf16[2,32,1024]{2,1,0:T(8,128)(2,1)S(1)}, u32[]{:S(2)}, u32[]{:S(2)}) %collective-permute-start.8) | collective-permute-done | bytes 131104 | tf_op jit(solution)/shard_map/ppermute | solution.py:374
  42.2 2.1 %forward.6 = (f32[128,3584]{1,0:T(8,128)S(1)}, bf16[128,3584]{1,0:T(8,128)(2,1)S(1)}, f32[8,128]{1,0:T(8,128)S(1)}) custom-call(bf16[256,1024]{1,0:T(8,128)(2,1)S(1)} %get-tuple-element.110.refs_0_, bf16[1024,7168]{1,0:T(8,128)(2,1)S(1)} %get-tuple-element.92.refs_1_.refs_5_, f32[8,128]{1,0:T(8,128)S(1)} %get-tuple-element.111.refs_2_), custom_call_target="tpu_custom_call" | custom-call | flops 1 | bytes 1 | tf_op jit(solution)/shard_map/forward/pallas_call | solution.py:58
  44.4 2.1 %forward.7 = (f32[128,3584]{1,0:T(8,128)S(1)}, bf16[128,3584]{1,0:T(8,128)(2,1)S(1)}, f32[8,128]{1,0:T(8,128)S(1)}) custom-call(bf16[256,1024]{1,0:T(8,128)(2,1)S(1)} %get-tuple-element.110.refs_0_, bf16[1024,7168]{1,0:T(8,128)(2,1)S(1)} %get-tuple-element.92.refs_1_.refs_5_, f32[8,128]{1,0:T(8,128)S(1)} %get-tuple-element.112.refs_2_), custom_call_target="tpu_custom_call" | custom-call | flops 1 | bytes 1 | tf_op jit(solution)/shard_map/forward/pallas_call | solution.py:58
  49.4 5.3 %collective-permute-done.6.refs_1_ = bf16[32,3584]{1,0:T(8,128)(2,1)S(1)} collective-permute-done((bf16[32,3584]{1,0:T(8,128)(2,1)S(1)}, bf16[32,3584]{1,0:T(8,128)(2,1)S(1)}, u32[]{:S(2)}, u32[]{:S(2)}) %collective-permute-start.6) | collective-permute-done | bytes 229408 | tf_op jit(solution)/shard_map/ppermute | solution.py:374
  56.2 1.4 %collective-permute-start.15 = (bf16[32,3584]{1,0:T(8,128)(2,1)S(1)}, bf16[32,3584]{1,0:T(8,128)(2,1)S(1)}, u32[]{:S(2)}, u32[]{:S(2)}) collective-permute-start(bf16[32,3584]{1,0:T(8,128)(2,1)S(1)} %get-tuple-element.127.refs_0_), channel_id=1, source_target_pairs={{0,8},{4,12},{8,0},{12,4},{16,24},{20,28},{24,16},{28,20},{1,9},{5... | collective-permute-start | bytes 688136 | tf_op jit(solution)/shard_map/ppermute | solution.py:374
  58.3 1.4 %collective-permute-start.20 = (bf16[64,3584]{1,0:T(8,128)(2,1)S(1)}, bf16[64,3584]{1,0:T(8,128)(2,1)S(1)}, u32[]{:S(2)}, u32[]{:S(2)}) collective-permute-start(bf16[64,3584]{1,0:T(8,128)(2,1)S(1)} %get-tuple-element.137), channel_id=1, source_target_pairs={{0,16},{4,20},{8,24},{12,28},{16,0},{20,4},{24,8},{28,12},{1,17},{... | collective-permute-start | bytes 1376264 | tf_op jit(solution)/shard_map/ppermute | solution.py:374
  59.7 4.0 %collective-permute-done.16.refs_1_ = bf16[32,3584]{1,0:T(8,128)(2,1)S(1)} collective-permute-done((bf16[32,3584]{1,0:T(8,128)(2,1)S(1)}, bf16[32,3584]{1,0:T(8,128)(2,1)S(1)}, u32[]{:S(2)}, u32[]{:S(2)}) %collective-permute-start.16) | collective-permute-done | bytes 229408 | tf_op jit(solution)/shard_map/ppermute | solution.py:374
  63.8 1.5 %collective-permute-start.19 = (bf16[64,3584]{1,0:T(8,128)(2,1)S(1)}, bf16[64,3584]{1,0:T(8,128)(2,1)S(1)}, u32[]{:S(2)}, u32[]{:S(2)}) collective-permute-start(bf16[64,3584]{1,0:T(8,128)(2,1)S(1)} %get-tuple-element.135.refs_0_), channel_id=1, source_target_pairs={{0,8},{4,12},{8,0},{12,4},{16,24},{20,28},{24,16},{28,20},{1,9},{5... | collective-permute-start | bytes 1376264 | tf_op jit(solution)/shard_map/ppermute | solution.py:374
  66.3 8.3 %collective-permute-done.14.refs_1_ = bf16[64,3584]{1,0:T(8,128)(2,1)S(1)} collective-permute-done((bf16[64,3584]{1,0:T(8,128)(2,1)S(1)}, bf16[64,3584]{1,0:T(8,128)(2,1)S(1)}, u32[]{:S(2)}, u32[]{:S(2)}) %collective-permute-start.14) | collective-permute-done | bytes 458784 | tf_op jit(solution)/shard_map/ppermute | solution.py:374
  74.7 1.5 %collective-permute-start.17 = (bf16[32,3584]{1,0:T(8,128)(2,1)S(1)}, bf16[32,3584]{1,0:T(8,128)(2,1)S(1)}, u32[]{:S(2)}, u32[]{:S(2)}) collective-permute-start(bf16[32,3584]{1,0:T(8,128)(2,1)S(1)} %get-tuple-element.133), channel_id=1, source_target_pairs={{0,16},{4,20},{8,24},{12,28},{16,0},{20,4},{24,8},{28,12},{1,17},{... | collective-permute-start | bytes 688136 | tf_op jit(solution)/shard_map/ppermute | solution.py:374
  76.3 1.5 %collective-permute-start.21 = (bf16[32,3584]{1,0:T(8,128)(2,1)S(1)}, bf16[32,3584]{1,0:T(8,128)(2,1)S(1)}, u32[]{:S(2)}, u32[]{:S(2)}) collective-permute-start(bf16[32,3584]{1,0:T(8,128)(2,1)S(1)} %get-tuple-element.144), channel_id=1, source_target_pairs={{0,8},{4,12},{8,0},{12,4},{16,24},{20,28},{24,16},{28,20},{1,9},{5... | collective-permute-start | bytes 688136 | tf_op jit(solution)/shard_map/ppermute | solution.py:374
  77.8 6.6 %collective-permute-done.19.refs_1_ = bf16[64,3584]{1,0:T(8,128)(2,1)S(1)} collective-permute-done((bf16[64,3584]{1,0:T(8,128)(2,1)S(1)}, bf16[64,3584]{1,0:T(8,128)(2,1)S(1)}, u32[]{:S(2)}, u32[]{:S(2)}) %collective-permute-start.19) | collective-permute-done | bytes 458784 | tf_op jit(solution)/shard_map/ppermute | solution.py:374
  85.2 1.3 %collective-permute-done.17.refs_1_ = bf16[32,3584]{1,0:T(8,128)(2,1)S(1)} collective-permute-done((bf16[32,3584]{1,0:T(8,128)(2,1)S(1)}, bf16[32,3584]{1,0:T(8,128)(2,1)S(1)}, u32[]{:S(2)}, u32[]{:S(2)}) %collective-permute-start.17) | collective-permute-done | bytes 229408 | tf_op jit(solution)/shard_map/ppermute | solution.py:374
  88.0 1.4 %collective-permute-start.22 = (bf16[32,3584]{1,0:T(8,128)(2,1)S(1)}, bf16[32,3584]{1,0:T(8,128)(2,1)S(1)}, u32[]{:S(2)}, u32[]{:S(2)}) collective-permute-start(bf16[32,3584]{1,0:T(8,128)(2,1)S(1)} %get-tuple-element.147.refs_0_), channel_id=1, source_target_pairs={{0,8},{4,12},{8,0},{12,4},{16,24},{20,28},{24,16},{28,20},{1,9},{5... | collective-permute-start | bytes 688136 | tf_op jit(solution)/shard_map/ppermute | solution.py:374
  89.3 3.9 %collective-permute-done.23.refs_1_ = bf16[32,3584]{1,0:T(8,128)(2,1)S(1)} collective-permute-done((bf16[32,3584]{1,0:T(8,128)(2,1)S(1)}, bf16[32,3584]{1,0:T(8,128)(2,1)S(1)}, u32[]{:S(2)}, u32[]{:S(2)}) %collective-permute-start.23) | collective-permute-done | bytes 229408 | tf_op jit(solution)/shard_map/ppermute | solution.py:374
  93.2 1.4 %collective-permute-start.29 = (bf16[64,3584]{1,0:T(8,128)(2,1)S(1)}, bf16[64,3584]{1,0:T(8,128)(2,1)S(1)}, u32[]{:S(2)}, u32[]{:S(2)}) collective-permute-start(bf16[64,3584]{1,0:T(8,128)(2,1)S(1)} %get-tuple-element.160.refs_0_), channel_id=1, source_target_pairs={{0,8},{4,12},{8,0},{12,4},{16,24},{20,28},{24,16},{28,20},{1,9},{5... | collective-permute-start | bytes 1376264 | tf_op jit(solution)/shard_map/ppermute | solution.py:374
  97.3 5.0 %input_partial.2 = (f32[64,1024]{1,0:T(8,128)S(1)}, bf16[64,1024]{1,0:T(8,128)(2,1)S(1)}, bf16[64,1024]{1,0:T(8,128)(2,1)S(1)}, bf16[64,1024]{1,0:T(8,128)(2,1)S(1)}, f32[8,128]{1,0:T(8,128)S(1)}) custom-call(s32[8]{0:T(128)S(1)} %shift-right-arithmetic_add_fusion.refs_3_.refs_0_, bf16[128,3584]{1,0:T(8,128)(2,1)S(1)} %get-tuple-element.153.refs_1_.refs_3_, ...), custom_call_target="tpu_custom_call" | custom-call | flops 1 | bytes 1 | tf_op jit(solution)/shard_map/input_partial/pallas_call | solution.py:58
  102.3 2.4 %collective-permute-done.29.refs_1_ = bf16[64,3584]{1,0:T(8,128)(2,1)S(1)} collective-permute-done((bf16[64,3584]{1,0:T(8,128)(2,1)S(1)}, bf16[64,3584]{1,0:T(8,128)(2,1)S(1)}, u32[]{:S(2)}, u32[]{:S(2)}) %collective-permute-start.29) | collective-permute-done | bytes 458784 | tf_op jit(solution)/shard_map/ppermute | solution.py:374
  106.9 2.8 %collective-permute-start.27 = (bf16[64,1024]{1,0:T(8,128)(2,1)S(1)}, bf16[64,1024]{1,0:T(8,128)(2,1)S(1)}, u32[]{:S(2)}, u32[]{:S(2)}) collective-permute-start(bf16[64,1024]{1,0:T(8,128)(2,1)S(1)} %get-tuple-element.158), channel_id=1, source_target_pairs={{0,2},{1,3},{2,0},{3,1},{4,6},{5,7},{6,4},{7,5},{8,10},{9,11},{10,... | collective-permute-start | bytes 393224 | tf_op jit(solution)/shard_map/ppermute | solution.py:374
  110.8 4.8 %input_partial.3 = (f32[64,1024]{1,0:T(8,128)S(1)}, bf16[64,1024]{1,0:T(8,128)(2,1)S(1)}, bf16[64,1024]{1,0:T(8,128)(2,1)S(1)}, bf16[64,1024]{1,0:T(8,128)(2,1)S(1)}, f32[8,128]{1,0:T(8,128)S(1)}) custom-call(s32[8]{0:T(128)S(1)} %shift-right-arithmetic_add_fusion.refs_3_.refs_0_, bf16[128,3584]{1,0:T(8,128)(2,1)S(1)} %get-tuple-element.162.refs_1_.refs_5_, ...), custom_call_target="tpu_custom_call" | custom-call | flops 1 | bytes 1 | tf_op jit(solution)/shard_map/input_partial/pallas_call | solution.py:58
  115.7 3.2 %collective-permute-start.34 = (bf16[64,1024]{1,0:T(8,128)(2,1)S(1)}, bf16[64,1024]{1,0:T(8,128)(2,1)S(1)}, u32[]{:S(2)}, u32[]{:S(2)}) collective-permute-start(bf16[64,1024]{1,0:T(8,128)(2,1)S(1)} %get-tuple-element.169), channel_id=1, source_target_pairs={{0,2},{1,3},{2,0},{3,1},{4,6},{5,7},{6,4},{7,5},{8,10},{9,11},{10,... | collective-permute-start | bytes 393224 | tf_op jit(solution)/shard_map/ppermute | solution.py:374
  120.1 9.1 %weight_gradient.1 = (bf16[1,1,448,128,128]{4,3,2,1,0:T(8,128)(2,1)}, f32[8,128]{1,0:T(8,128)S(1)}) custom-call(s32[448]{0:T(512)S(1)} %select_reduce_fusion.refs_0_, bf16[1024,256]{1,0:T(8,128)(2,1)S(1)} %get-tuple-element.171.refs_1_, bf16[1024,256]{1,0:T(8,128)(2,1)S(1)} %get-tuple-element.172.refs_2_, ...), custom_call_target="tpu_custom_call" | custom-call | flops 1 | bytes 1 | tf_op jit(solution)/shard_map/weight_gradient/pallas_call | solution.py:58
  129.2 1.8 %collective-permute-done.34.refs_6_ = bf16[64,1024]{1,0:T(8,128)(2,1)S(1)} collective-permute-done((bf16[64,1024]{1,0:T(8,128)(2,1)S(1)}, bf16[64,1024]{1,0:T(8,128)(2,1)S(1)}, u32[]{:S(2)}, u32[]{:S(2)}) %collective-permute-start.34) | collective-permute-done | bytes 131104 | tf_op jit(solution)/shard_map/ppermute | solution.py:374
  (80 shorter events, 25.1 us)
Async XLA Ops:
  1.6 15.2 %collective-permute-start.2 = (bf16[2,32,1024]{2,1,0:T(8,128)(2,1)S(1)}, bf16[2,32,1024]{2,1,0:T(8,128)(2,1)S(1)}, u32[]{:S(2)}, u32[]{:S(2)}) collective-permute-start(bf16[2,32,1024]{2,1,0:T(8,128)(2,1)S(1)} %get-tuple-element.178.refs_1_), channel_id=1, source_target_pairs={{0,3},{1,2},{2,1},{3,0},{4,7},{5,6},{6,5},{7,4},{8,11},{9,10},{10,... | collective-permute-start | bytes 393224 | tf_op jit(solution)/shard_map/ppermute | solution.py:374
  6.7 11.1 %collective-permute-start.1 = (bf16[2,32,1024]{2,1,0:T(8,128)(2,1)S(1)}, bf16[2,32,1024]{2,1,0:T(8,128)(2,1)S(1)}, u32[]{:S(2)}, u32[]{:S(2)}) collective-permute-start(bf16[2,32,1024]{2,1,0:T(8,128)(2,1)S(1)} %get-tuple-element.178.refs_1_), channel_id=1, source_target_pairs={{0,2},{1,3},{2,0},{3,1},{4,6},{5,7},{6,4},{7,5},{8,10},{9,11},{10,... | collective-permute-start | bytes 393224 | tf_op jit(solution)/shard_map/ppermute | solution.py:374
  6.7 11.1 %collective-permute-start = (bf16[2,32,1024]{2,1,0:T(8,128)(2,1)S(1)}, bf16[2,32,1024]{2,1,0:T(8,128)(2,1)S(1)}, u32[]{:S(2)}, u32[]{:S(2)}) collective-permute-start(bf16[2,32,1024]{2,1,0:T(8,128)(2,1)S(1)} %get-tuple-element.178.refs_1_), channel_id=1, source_target_pairs={{0,1},{1,0},{2,3},{3,2},{4,5},{5,4},{6,7},{7,6},{8,9},{9,8},{10,11... | collective-permute-start | bytes 393224 | tf_op jit(solution)/shard_map/ppermute | solution.py:374
  23.7 12.5 %collective-permute-start.4 = (bf16[64,3584]{1,0:T(8,128)(2,1)S(1)}, bf16[64,3584]{1,0:T(8,128)(2,1)S(1)}, u32[]{:S(2)}, u32[]{:S(2)}) collective-permute-start(bf16[64,3584]{1,0:T(8,128)(2,1)S(1)} %get-tuple-element.99), channel_id=1, source_target_pairs={{0,8},{4,12},{8,0},{12,4},{16,24},{20,28},{24,16},{28,20},{1,9},{5... | collective-permute-start | bytes 1376264 | tf_op jit(solution)/shard_map/ppermute | solution.py:374
  25.8 12.9 %collective-permute-start.10 = (bf16[64,3584]{1,0:T(8,128)(2,1)S(1)}, bf16[64,3584]{1,0:T(8,128)(2,1)S(1)}, u32[]{:S(2)}, u32[]{:S(2)}) collective-permute-start(bf16[64,3584]{1,0:T(8,128)(2,1)S(1)} %get-tuple-element.107), channel_id=1, source_target_pairs={{0,16},{4,20},{8,24},{12,28},{16,0},{20,4},{24,8},{28,12},{1,17},{... | collective-permute-start | bytes 1376264 | tf_op jit(solution)/shard_map/ppermute | solution.py:374
  27.4 11.3 %collective-permute-start.9 = (bf16[2,32,1024]{2,1,0:T(8,128)(2,1)S(1)}, bf16[2,32,1024]{2,1,0:T(8,128)(2,1)S(1)}, u32[]{:S(2)}, u32[]{:S(2)}) collective-permute-start(bf16[2,32,1024]{2,1,0:T(8,128)(2,1)S(1)} %get-tuple-element.177.refs_1_), channel_id=1, source_target_pairs={{0,3},{1,2},{2,1},{3,0},{4,7},{5,6},{6,5},{7,4},{8,11},{9,10},{10,... | collective-permute-start | bytes 393224 | tf_op jit(solution)/shard_map/ppermute | solution.py:374
  30.5 10.9 %collective-permute-start.8 = (bf16[2,32,1024]{2,1,0:T(8,128)(2,1)S(1)}, bf16[2,32,1024]{2,1,0:T(8,128)(2,1)S(1)}, u32[]{:S(2)}, u32[]{:S(2)}) collective-permute-start(bf16[2,32,1024]{2,1,0:T(8,128)(2,1)S(1)} %get-tuple-element.177.refs_1_), channel_id=1, source_target_pairs={{0,2},{1,3},{2,0},{3,1},{4,6},{5,7},{6,4},{7,5},{8,10},{9,11},{10,... | collective-permute-start | bytes 393224 | tf_op jit(solution)/shard_map/ppermute | solution.py:374
  30.5 10.9 %collective-permute-start.7 = (bf16[2,32,1024]{2,1,0:T(8,128)(2,1)S(1)}, bf16[2,32,1024]{2,1,0:T(8,128)(2,1)S(1)}, u32[]{:S(2)}, u32[]{:S(2)}) collective-permute-start(bf16[2,32,1024]{2,1,0:T(8,128)(2,1)S(1)} %get-tuple-element.177.refs_1_), channel_id=1, source_target_pairs={{0,1},{1,0},{2,3},{3,2},{4,5},{5,4},{6,7},{7,6},{8,9},{9,8},{10,11... | collective-permute-start | bytes 393224 | tf_op jit(solution)/shard_map/ppermute | solution.py:374
  47.1 7.6 %collective-permute-start.6 = (bf16[32,3584]{1,0:T(8,128)(2,1)S(1)}, bf16[32,3584]{1,0:T(8,128)(2,1)S(1)}, u32[]{:S(2)}, u32[]{:S(2)}) collective-permute-start(bf16[32,3584]{1,0:T(8,128)(2,1)S(1)} %get-tuple-element.105), channel_id=1, source_target_pairs={{0,16},{4,20},{8,24},{12,28},{16,0},{20,4},{24,8},{28,12},{1,17},{... | collective-permute-start | bytes 688136 | tf_op jit(solution)/shard_map/ppermute | solution.py:374
  47.7 8.1 %collective-permute-start.13 = (bf16[32,3584]{1,0:T(8,128)(2,1)S(1)}, bf16[32,3584]{1,0:T(8,128)(2,1)S(1)}, u32[]{:S(2)}, u32[]{:S(2)}) collective-permute-start(bf16[32,3584]{1,0:T(8,128)(2,1)S(1)} %get-tuple-element.122), channel_id=1, source_target_pairs={{0,8},{4,12},{8,0},{12,4},{16,24},{20,28},{24,16},{28,20},{1,9},{5... | collective-permute-start | bytes 688136 | tf_op jit(solution)/shard_map/ppermute | solution.py:374
  55.1 8.6 %collective-permute-start.16 = (bf16[32,3584]{1,0:T(8,128)(2,1)S(1)}, bf16[32,3584]{1,0:T(8,128)(2,1)S(1)}, u32[]{:S(2)}, u32[]{:S(2)}) collective-permute-start(bf16[32,3584]{1,0:T(8,128)(2,1)S(1)} %get-tuple-element.128.refs_0_), channel_id=1, source_target_pairs={{0,16},{4,20},{8,24},{12,28},{16,0},{20,4},{24,8},{28,12},{1,17},{... | collective-permute-start | bytes 688136 | tf_op jit(solution)/shard_map/ppermute | solution.py:374
  56.2 9.1 %collective-permute-start.15 = (bf16[32,3584]{1,0:T(8,128)(2,1)S(1)}, bf16[32,3584]{1,0:T(8,128)(2,1)S(1)}, u32[]{:S(2)}, u32[]{:S(2)}) collective-permute-start(bf16[32,3584]{1,0:T(8,128)(2,1)S(1)} %get-tuple-element.127.refs_0_), channel_id=1, source_target_pairs={{0,8},{4,12},{8,0},{12,4},{16,24},{20,28},{24,16},{28,20},{1,9},{5... | collective-permute-start | bytes 688136 | tf_op jit(solution)/shard_map/ppermute | solution.py:374
  57.5 17.1 %collective-permute-start.14 = (bf16[64,3584]{1,0:T(8,128)(2,1)S(1)}, bf16[64,3584]{1,0:T(8,128)(2,1)S(1)}, u32[]{:S(2)}, u32[]{:S(2)}) collective-permute-start(bf16[64,3584]{1,0:T(8,128)(2,1)S(1)} %get-tuple-element.126), channel_id=1, source_target_pairs={{0,8},{4,12},{8,0},{12,4},{16,24},{20,28},{24,16},{28,20},{1,9},{5... | collective-permute-start | bytes 1376264 | tf_op jit(solution)/shard_map/ppermute | solution.py:374
  58.3 18.0 %collective-permute-start.20 = (bf16[64,3584]{1,0:T(8,128)(2,1)S(1)}, bf16[64,3584]{1,0:T(8,128)(2,1)S(1)}, u32[]{:S(2)}, u32[]{:S(2)}) collective-permute-start(bf16[64,3584]{1,0:T(8,128)(2,1)S(1)} %get-tuple-element.137), channel_id=1, source_target_pairs={{0,16},{4,20},{8,24},{12,28},{16,0},{20,4},{24,8},{28,12},{1,17},{... | collective-permute-start | bytes 1376264 | tf_op jit(solution)/shard_map/ppermute | solution.py:374
  63.8 20.7 %collective-permute-start.19 = (bf16[64,3584]{1,0:T(8,128)(2,1)S(1)}, bf16[64,3584]{1,0:T(8,128)(2,1)S(1)}, u32[]{:S(2)}, u32[]{:S(2)}) collective-permute-start(bf16[64,3584]{1,0:T(8,128)(2,1)S(1)} %get-tuple-element.135.refs_0_), channel_id=1, source_target_pairs={{0,8},{4,12},{8,0},{12,4},{16,24},{20,28},{24,16},{28,20},{1,9},{5... | collective-permute-start | bytes 1376264 | tf_op jit(solution)/shard_map/ppermute | solution.py:374
  65.3 19.2 %collective-permute-start.18 = (bf16[64,3584]{1,0:T(8,128)(2,1)S(1)}, bf16[64,3584]{1,0:T(8,128)(2,1)S(1)}, u32[]{:S(2)}, u32[]{:S(2)}) collective-permute-start(bf16[64,3584]{1,0:T(8,128)(2,1)S(1)} %get-tuple-element.134.refs_0_), channel_id=1, source_target_pairs={{0,16},{4,20},{8,24},{12,28},{16,0},{20,4},{24,8},{28,12},{1,17},{... | collective-permute-start | bytes 1376264 | tf_op jit(solution)/shard_map/ppermute | solution.py:374
  74.7 11.8 %collective-permute-start.17 = (bf16[32,3584]{1,0:T(8,128)(2,1)S(1)}, bf16[32,3584]{1,0:T(8,128)(2,1)S(1)}, u32[]{:S(2)}, u32[]{:S(2)}) collective-permute-start(bf16[32,3584]{1,0:T(8,128)(2,1)S(1)} %get-tuple-element.133), channel_id=1, source_target_pairs={{0,16},{4,20},{8,24},{12,28},{16,0},{20,4},{24,8},{28,12},{1,17},{... | collective-permute-start | bytes 688136 | tf_op jit(solution)/shard_map/ppermute | solution.py:374
  76.3 11.2 %collective-permute-start.21 = (bf16[32,3584]{1,0:T(8,128)(2,1)S(1)}, bf16[32,3584]{1,0:T(8,128)(2,1)S(1)}, u32[]{:S(2)}, u32[]{:S(2)}) collective-permute-start(bf16[32,3584]{1,0:T(8,128)(2,1)S(1)} %get-tuple-element.144), channel_id=1, source_target_pairs={{0,8},{4,12},{8,0},{12,4},{16,24},{20,28},{24,16},{28,20},{1,9},{5... | collective-permute-start | bytes 688136 | tf_op jit(solution)/shard_map/ppermute | solution.py:374
  84.6 12.7 %collective-permute-start.25 = (bf16[128,3584]{1,0:T(8,128)(2,1)S(1)}, bf16[128,3584]{1,0:T(8,128)(2,1)S(1)}, u32[]{:S(2)}, u32[]{:S(2)}) collective-permute-start(bf16[128,3584]{1,0:T(8,128)(2,1)S(1)} %get-tuple-element.154.refs_3_.refs_7_), channel_id=1, source_target_pairs={{0,4},{4,0},{8,12},{12,8},{16,20},{20,16},{24,28},{28,24},{1,5},{5... | collective-permute-start | bytes 2752520 | tf_op jit(solution)/shard_map/ppermute | solution.py:374
  84.7 12.6 %collective-permute-start.24 = (bf16[128,3584]{1,0:T(8,128)(2,1)S(1)}, bf16[128,3584]{1,0:T(8,128)(2,1)S(1)}, u32[]{:S(2)}, u32[]{:S(2)}) collective-permute-start(bf16[128,3584]{1,0:T(8,128)(2,1)S(1)} %get-tuple-element.153.refs_1_.refs_3_), channel_id=1, source_target_pairs={{0,4},{4,0},{8,12},{12,8},{16,20},{20,16},{24,28},{28,24},{1,5},{5... | collective-permute-start | bytes 2752520 | tf_op jit(solution)/shard_map/ppermute | solution.py:374
  86.9 6.3 %collective-permute-start.23 = (bf16[32,3584]{1,0:T(8,128)(2,1)S(1)}, bf16[32,3584]{1,0:T(8,128)(2,1)S(1)}, u32[]{:S(2)}, u32[]{:S(2)}) collective-permute-start(bf16[32,3584]{1,0:T(8,128)(2,1)S(1)} %get-tuple-element.148.refs_0_), channel_id=1, source_target_pairs={{0,16},{4,20},{8,24},{12,28},{16,0},{20,4},{24,8},{28,12},{1,17},{... | collective-permute-start | bytes 688136 | tf_op jit(solution)/shard_map/ppermute | solution.py:374
  88.0 7.9 %collective-permute-start.22 = (bf16[32,3584]{1,0:T(8,128)(2,1)S(1)}, bf16[32,3584]{1,0:T(8,128)(2,1)S(1)}, u32[]{:S(2)}, u32[]{:S(2)}) collective-permute-start(bf16[32,3584]{1,0:T(8,128)(2,1)S(1)} %get-tuple-element.147.refs_0_), channel_id=1, source_target_pairs={{0,8},{4,12},{8,0},{12,4},{16,24},{20,28},{24,16},{28,20},{1,9},{5... | collective-permute-start | bytes 688136 | tf_op jit(solution)/shard_map/ppermute | solution.py:374
  93.2 11.4 %collective-permute-start.29 = (bf16[64,3584]{1,0:T(8,128)(2,1)S(1)}, bf16[64,3584]{1,0:T(8,128)(2,1)S(1)}, u32[]{:S(2)}, u32[]{:S(2)}) collective-permute-start(bf16[64,3584]{1,0:T(8,128)(2,1)S(1)} %get-tuple-element.160.refs_0_), channel_id=1, source_target_pairs={{0,8},{4,12},{8,0},{12,4},{16,24},{20,28},{24,16},{28,20},{1,9},{5... | collective-permute-start | bytes 1376264 | tf_op jit(solution)/shard_map/ppermute | solution.py:374
  95.9 9.8 %collective-permute-start.31 = (bf16[64,3584]{1,0:T(8,128)(2,1)S(1)}, bf16[64,3584]{1,0:T(8,128)(2,1)S(1)}, u32[]{:S(2)}, u32[]{:S(2)}) collective-permute-start(bf16[64,3584]{1,0:T(8,128)(2,1)S(1)} %get-tuple-element.163.refs_0_), channel_id=1, source_target_pairs={{0,16},{4,20},{8,24},{12,28},{16,0},{20,4},{24,8},{28,12},{1,17},{... | collective-permute-start | bytes 1376264 | tf_op jit(solution)/shard_map/ppermute | solution.py:374
  105.8 5.0 %collective-permute-start.32 = (bf16[128,3584]{1,0:T(8,128)(2,1)S(1)}, bf16[128,3584]{1,0:T(8,128)(2,1)S(1)}, u32[]{:S(2)}, u32[]{:S(2)}) collective-permute-start(bf16[128,3584]{1,0:T(8,128)(2,1)S(1)} %get-tuple-element.165.refs_3_.refs_9_), channel_id=1, source_target_pairs={{0,4},{4,0},{8,12},{12,8},{16,20},{20,16},{24,28},{28,24},{1,5},{5... | collective-permute-start | bytes 2752520 | tf_op jit(solution)/shard_map/ppermute | solution.py:374
  105.9 4.9 %collective-permute-start.30 = (bf16[128,3584]{1,0:T(8,128)(2,1)S(1)}, bf16[128,3584]{1,0:T(8,128)(2,1)S(1)}, u32[]{:S(2)}, u32[]{:S(2)}) collective-permute-start(bf16[128,3584]{1,0:T(8,128)(2,1)S(1)} %get-tuple-element.162.refs_1_.refs_5_), channel_id=1, source_target_pairs={{0,4},{4,0},{8,12},{12,8},{16,20},{20,16},{24,28},{28,24},{1,5},{5... | collective-permute-start | bytes 2752520 | tf_op jit(solution)/shard_map/ppermute | solution.py:374
  106.4 12.5 %collective-permute-start.26 = (bf16[64,1024]{1,0:T(8,128)(2,1)S(1)}, bf16[64,1024]{1,0:T(8,128)(2,1)S(1)}, u32[]{:S(2)}, u32[]{:S(2)}) collective-permute-start(bf16[64,1024]{1,0:T(8,128)(2,1)S(1)} %get-tuple-element.157), channel_id=1, source_target_pairs={{0,1},{1,0},{2,3},{3,2},{4,5},{5,4},{6,7},{7,6},{8,9},{9,8},{10,11... | collective-permute-start | bytes 393224 | tf_op jit(solution)/shard_map/ppermute | solution.py:374
  106.9 22.3 %collective-permute-start.27 = (bf16[64,1024]{1,0:T(8,128)(2,1)S(1)}, bf16[64,1024]{1,0:T(8,128)(2,1)S(1)}, u32[]{:S(2)}, u32[]{:S(2)}) collective-permute-start(bf16[64,1024]{1,0:T(8,128)(2,1)S(1)} %get-tuple-element.158), channel_id=1, source_target_pairs={{0,2},{1,3},{2,0},{3,1},{4,6},{5,7},{6,4},{7,5},{8,10},{9,11},{10,... | collective-permute-start | bytes 393224 | tf_op jit(solution)/shard_map/ppermute | solution.py:374
  109.6 19.6 %collective-permute-start.28 = (bf16[64,1024]{1,0:T(8,128)(2,1)S(1)}, bf16[64,1024]{1,0:T(8,128)(2,1)S(1)}, u32[]{:S(2)}, u32[]{:S(2)}) collective-permute-start(bf16[64,1024]{1,0:T(8,128)(2,1)S(1)} %get-tuple-element.159), channel_id=1, source_target_pairs={{0,3},{1,2},{2,1},{3,0},{4,7},{5,6},{6,5},{7,4},{8,11},{9,10},{10,... | collective-permute-start | bytes 393224 | tf_op jit(solution)/shard_map/ppermute | solution.py:374
  115.6 13.6 %collective-permute-start.33 = (bf16[64,1024]{1,0:T(8,128)(2,1)S(1)}, bf16[64,1024]{1,0:T(8,128)(2,1)S(1)}, u32[]{:S(2)}, u32[]{:S(2)}) collective-permute-start(bf16[64,1024]{1,0:T(8,128)(2,1)S(1)} %get-tuple-element.168), channel_id=1, source_target_pairs={{0,1},{1,0},{2,3},{3,2},{4,5},{5,4},{6,7},{7,6},{8,9},{9,8},{10,11... | collective-permute-start | bytes 393224 | tf_op jit(solution)/shard_map/ppermute | solution.py:374
  115.7 15.3 %collective-permute-start.34 = (bf16[64,1024]{1,0:T(8,128)(2,1)S(1)}, bf16[64,1024]{1,0:T(8,128)(2,1)S(1)}, u32[]{:S(2)}, u32[]{:S(2)}) collective-permute-start(bf16[64,1024]{1,0:T(8,128)(2,1)S(1)} %get-tuple-element.169), channel_id=1, source_target_pairs={{0,2},{1,3},{2,0},{3,1},{4,6},{5,7},{6,4},{7,5},{8,10},{9,11},{10,... | collective-permute-start | bytes 393224 | tf_op jit(solution)/shard_map/ppermute | solution.py:374
  118.9 12.1 %collective-permute-start.35 = (bf16[64,1024]{1,0:T(8,128)(2,1)S(1)}, bf16[64,1024]{1,0:T(8,128)(2,1)S(1)}, u32[]{:S(2)}, u32[]{:S(2)}) collective-permute-start(bf16[64,1024]{1,0:T(8,128)(2,1)S(1)} %get-tuple-element.170), channel_id=1, source_target_pairs={{0,3},{1,2},{2,1},{3,0},{4,7},{5,6},{6,5},{7,4},{8,11},{9,10},{10,... | collective-permute-start | bytes 393224 | tf_op jit(solution)/shard_map/ppermute | solution.py:374
  (5 other events, 18.2 us)

commit v3 on v2

--- a/solution.py
+++ b/solution.py
@@ -346,7 +346,7 @@
     out_ref = refs[-1]
     own = sum(sizes)
     for k, (start, rows) in enumerate(zip(starts, sizes)):
-        found = refs[k * many : (k + 1) * many]
+        found = refs[sum(many[:k]) : sum(many[: k + 1])]
         for j in range(each):
             here = slice(j * rows, (j + 1) * rows)
             total = found[0][here, :]
@@ -360,7 +360,7 @@
     arrays = [x for part in found for x in part]
     shape = (each * sum(sizes), arrays[0].shape[1])
     [out] = core(
-        functools.partial(total_kernel, each, len(found[0]), starts, sizes),
+        functools.partial(total_kernel, each, [len(part) for part in found], starts, sizes),
         "total_input",
         [jax.ShapeDtypeStruct(shape, jnp.bfloat16)],
         [pl.BlockSpec(shape, lambda: (0, 0))],
@@ -448,8 +448,15 @@
         if c + 1 < slabs:
             return
         grads = [state[k, c] for c in range(slabs)]
-        found = input_partial(core, grads, weight, place, n_col if direct else 1)
-        if direct:
+        halved = n_col == 4 and k + 1 < parts
+        spots = place.reshape(n_col, -1)[jnp.array([0, 2, 1, 3])].reshape(-1) if halved else place
+        found = input_partial(
+            core, grads, weight, spots, 2 if halved else n_col if direct else 1
+        )
+        if halved:
+            keep, send = add_step(core, found[0], swap(found[1], "col", n_col, 1), [2], 2)
+            input_grads[k] = [keep, swap(send, "col", n_col, 2)]
+        elif direct:
             input_grads[k] = [found[0]]
             input_grads[k] += [swap(found[m], "col", n_col, m) for m in range(1, n_col)]
         else:

time: 132 us -> 157 us (1.19)
  local copies, waits for them, and re-layouts: 1 us -> 17 us
  Pallas kernels: 40.9 us -> 46.6 us
  waiting for transfers between devices: 46.8 us -> 50.2 us
    unnamed x2 -> x26, local copies, waits for them, and re-layouts: 0.01 us -> 15.2 us
    pallas_call x32 -> x33, Pallas kernels: 40.9 us -> 46.6 us  [__call__(): pl.pallas_call(body, out_shape=[*out_shape, pltpu.VMEM((8, 128), jnp.floa...]
    ppermute x36 -> x35, waiting for transfers between devices: 46.8 us -> 50.2 us  [swap(): return lax.ppermute(array, axis, [(i, i ^ bit) for i in range(size)])]
    ppermute x36 -> x35, starting transfers between devices: 39.9 us -> 40.1 us  [swap(): return lax.ppermute(array, axis, [(i, i ^ bit) for i in range(size)])]
  transfers between devices with their start and end apart: 36 -> 35, of which waited for: 15 -> 15; matrix products, arithmetic and copies ran while one was open for 1% -> 1% of each run, Pallas kernels for 26% -> 25%
where the time goes in v3:
time: 157 us
  waiting for transfers between devices  50.2 us (32%)
  Pallas kernels  46.6 us (30%)
  starting transfers between devices  40.1 us (26%)
  local copies, waits for them, and re-layouts  17 us (11%)
  between operations  1.71 us (1%)
  other arithmetic  1.57 us (1%)
    ppermute x35, waiting for transfers between devices, swap(): return lax.ppermute(array, axis, [(i, i ^ bit) for i in range(size)])  50.2 us
    pallas_call x33, Pallas kernels, __call__(): pl.pallas_call(body, out_shape=[*out_shape, pltpu.VMEM((8, 128), jnp.floa...  46.6 us
    ppermute x35, starting transfers between devices, swap(): return lax.ppermute(array, axis, [(i, i ^ bit) for i in range(size)])  40.1 us
    unnamed x26, local copies, waits for them, and re-layouts  15.2 us
  transfers between devices with their start and end apart: 35, of which 15 were waited for; matrix products, arithmetic and copies ran while one was open for 1% of the time, Pallas kernels for 25%

profile of v3, /device:TPU:0, one launch (start us, length us, event | category | flops | bytes accessed | tf_op | source)
XLA Modules:
  0.0 157.1 jit_solution(10073430172826028432)
XLA Ops:
  1.6 5.1 %collective-permute-start.2 = (bf16[2,32,1024]{2,1,0:T(8,128)(2,1)S(1)}, bf16[2,32,1024]{2,1,0:T(8,128)(2,1)S(1)}, u32[]{:S(2)}, u32[]{:S(2)}) collective-permute-start(bf16[2,32,1024]{2,1,0:T(8,128)(2,1)S(1)} %get-tuple-element.180.refs_1_), channel_id=1, source_target_pairs={{0,3},{1,2},{2,1},{3,0},{4,7},{5,6},{6,5},{7,4},{8,11},{9,10},{10,... | collective-permute-start | bytes 393224 | tf_op jit(solution)/shard_map/ppermute | solution.py:374
  9.6 7.8 %dense_tile.1 = (bf16[1024,7168]{1,0:T(8,128)(2,1)S(1)}, f32[8,128]{1,0:T(8,128)S(1)}) custom-call(s32[448]{0:T(512)S(1)} %select_reduce_fusion.refs_0_, bf16[1,1,448,128,128]{4,3,2,1,0:T(8,128)(2,1)} %refs_1_.1, s32[8]{0:T(128)S(1)} %broadcast_xor_fusion.refs_2_.refs_0_, s32[8]{0:T(128)S(1)} %shift-right-arithmetic_add_fusion.refs_3_.refs_0_), custom_call_target="tpu_custom_call" | custom-call | flops 1 | bytes 1 | tf_op jit(solution)/shard_map/dense_tile/pallas_call | solution.py:58
  18.6 2.1 %forward.4 = (f32[128,3584]{1,0:T(8,128)S(1)}, bf16[128,3584]{1,0:T(8,128)(2,1)S(1)}, f32[8,128]{1,0:T(8,128)S(1)}) custom-call(bf16[256,1024]{1,0:T(8,128)(2,1)S(1)} %get-tuple-element.92.refs_0_, bf16[1024,7168]{1,0:T(8,128)(2,1)S(1)} %get-tuple-element.93.refs_1_.refs_5_, f32[8,128]{1,0:T(8,128)S(1)} %get-tuple-element.94.refs_2_), custom_call_target="tpu_custom_call" | custom-call | flops 1 | bytes 1 | tf_op jit(solution)/shard_map/forward/pallas_call | solution.py:58
  20.7 2.1 %forward.5 = (f32[128,3584]{1,0:T(8,128)S(1)}, bf16[128,3584]{1,0:T(8,128)(2,1)S(1)}, f32[8,128]{1,0:T(8,128)S(1)}) custom-call(bf16[256,1024]{1,0:T(8,128)(2,1)S(1)} %get-tuple-element.92.refs_0_, bf16[1024,7168]{1,0:T(8,128)(2,1)S(1)} %get-tuple-element.93.refs_1_.refs_5_, f32[8,128]{1,0:T(8,128)S(1)} %get-tuple-element.97.refs_2_), custom_call_target="tpu_custom_call" | custom-call | flops 1 | bytes 1 | tf_op jit(solution)/shard_map/forward/pallas_call | solution.py:58
  27.3 3.2 %collective-permute-start.9 = (bf16[2,32,1024]{2,1,0:T(8,128)(2,1)S(1)}, bf16[2,32,1024]{2,1,0:T(8,128)(2,1)S(1)}, u32[]{:S(2)}, u32[]{:S(2)}) collective-permute-start(bf16[2,32,1024]{2,1,0:T(8,128)(2,1)S(1)} %get-tuple-element.179.refs_1_), channel_id=1, source_target_pairs={{0,3},{1,2},{2,1},{3,0},{4,7},{5,6},{6,5},{7,4},{8,11},{9,10},{10,... | collective-permute-start | bytes 393224 | tf_op jit(solution)/shard_map/ppermute | solution.py:374
  31.7 4.4 %collective-permute-done.4.refs_1_ = bf16[64,3584]{1,0:T(8,128)(2,1)S(1)} collective-permute-done((bf16[64,3584]{1,0:T(8,128)(2,1)S(1)}, bf16[64,3584]{1,0:T(8,128)(2,1)S(1)}, u32[]{:S(2)}, u32[]{:S(2)}) %collective-permute-start.4) | collective-permute-done | bytes 458784 | tf_op jit(solution)/shard_map/ppermute | solution.py:374
  36.2 2.3 %collective-permute-done.10.refs_1_ = bf16[64,3584]{1,0:T(8,128)(2,1)S(1)} collective-permute-done((bf16[64,3584]{1,0:T(8,128)(2,1)S(1)}, bf16[64,3584]{1,0:T(8,128)(2,1)S(1)}, u32[]{:S(2)}, u32[]{:S(2)}) %collective-permute-start.10) | collective-permute-done | bytes 458784 | tf_op jit(solution)/shard_map/ppermute | solution.py:374
  38.6 2.6 %collective-permute-done.8.refs_3_ = bf16[2,32,1024]{2,1,0:T(8,128)(2,1)S(1)} collective-permute-done((bf16[2,32,1024]{2,1,0:T(8,128)(2,1)S(1)}, bf16[2,32,1024]{2,1,0:T(8,128)(2,1)S(1)}, u32[]{:S(2)}, u32[]{:S(2)}) %collective-permute-start.8) | collective-permute-done | bytes 131104 | tf_op jit(solution)/shard_map/ppermute | solution.py:374
  42.0 2.1 %forward.6 = (f32[128,3584]{1,0:T(8,128)S(1)}, bf16[128,3584]{1,0:T(8,128)(2,1)S(1)}, f32[8,128]{1,0:T(8,128)S(1)}) custom-call(bf16[256,1024]{1,0:T(8,128)(2,1)S(1)} %get-tuple-element.111.refs_0_, bf16[1024,7168]{1,0:T(8,128)(2,1)S(1)} %get-tuple-element.93.refs_1_.refs_5_, f32[8,128]{1,0:T(8,128)S(1)} %get-tuple-element.112.refs_2_), custom_call_target="tpu_custom_call" | custom-call | flops 1 | bytes 1 | tf_op jit(solution)/shard_map/forward/pallas_call | solution.py:58
  44.2 2.1 %forward.7 = (f32[128,3584]{1,0:T(8,128)S(1)}, bf16[128,3584]{1,0:T(8,128)(2,1)S(1)}, f32[8,128]{1,0:T(8,128)S(1)}) custom-call(bf16[256,1024]{1,0:T(8,128)(2,1)S(1)} %get-tuple-element.111.refs_0_, bf16[1024,7168]{1,0:T(8,128)(2,1)S(1)} %get-tuple-element.93.refs_1_.refs_5_, f32[8,128]{1,0:T(8,128)S(1)} %get-tuple-element.113.refs_2_), custom_call_target="tpu_custom_call" | custom-call | flops 1 | bytes 1 | tf_op jit(solution)/shard_map/forward/pallas_call | solution.py:58
  47.2 2.0 %collective-permute-start.13 = (bf16[32,3584]{1,0:T(8,128)(2,1)S(1)}, bf16[32,3584]{1,0:T(8,128)(2,1)S(1)}, u32[]{:S(2)}, u32[]{:S(2)}) collective-permute-start(bf16[32,3584]{1,0:T(8,128)(2,1)S(1)} %get-tuple-element.123), channel_id=1, source_target_pairs={{0,8},{4,12},{8,0},{12,4},{16,24},{20,28},{24,16},{28,20},{1,9},{5... | collective-permute-start | bytes 688136 | tf_op jit(solution)/shard_map/ppermute | solution.py:374
  49.6 4.8 %collective-permute-done.6.refs_1_ = bf16[32,3584]{1,0:T(8,128)(2,1)S(1)} collective-permute-done((bf16[32,3584]{1,0:T(8,128)(2,1)S(1)}, bf16[32,3584]{1,0:T(8,128)(2,1)S(1)}, u32[]{:S(2)}, u32[]{:S(2)}) %collective-permute-start.6) | collective-permute-done | bytes 229408 | tf_op jit(solution)/shard_map/ppermute | solution.py:374
  56.3 2.0 %collective-permute-start.15 = (bf16[32,3584]{1,0:T(8,128)(2,1)S(1)}, bf16[32,3584]{1,0:T(8,128)(2,1)S(1)}, u32[]{:S(2)}, u32[]{:S(2)}) collective-permute-start(bf16[32,3584]{1,0:T(8,128)(2,1)S(1)} %get-tuple-element.128.refs_0_), channel_id=1, source_target_pairs={{0,8},{4,12},{8,0},{12,4},{16,24},{20,28},{24,16},{28,20},{1,9},{5... | collective-permute-start | bytes 688136 | tf_op jit(solution)/shard_map/ppermute | solution.py:374
  60.0 3.4 %collective-permute-done.16.refs_1_ = bf16[32,3584]{1,0:T(8,128)(2,1)S(1)} collective-permute-done((bf16[32,3584]{1,0:T(8,128)(2,1)S(1)}, bf16[32,3584]{1,0:T(8,128)(2,1)S(1)}, u32[]{:S(2)}, u32[]{:S(2)}) %collective-permute-start.16) | collective-permute-done | bytes 229408 | tf_op jit(solution)/shard_map/ppermute | solution.py:374
  63.5 2.1 %collective-permute-start.19 = (bf16[64,3584]{1,0:T(8,128)(2,1)S(1)}, bf16[64,3584]{1,0:T(8,128)(2,1)S(1)}, u32[]{:S(2)}, u32[]{:S(2)}) collective-permute-start(bf16[64,3584]{1,0:T(8,128)(2,1)S(1)} %get-tuple-element.136.refs_0_), channel_id=1, source_target_pairs={{0,8},{4,12},{8,0},{12,4},{16,24},{20,28},{24,16},{28,20},{1,9},{5... | collective-permute-start | bytes 1376264 | tf_op jit(solution)/shard_map/ppermute | solution.py:374
  66.6 8.1 %collective-permute-done.14.refs_1_ = bf16[64,3584]{1,0:T(8,128)(2,1)S(1)} collective-permute-done((bf16[64,3584]{1,0:T(8,128)(2,1)S(1)}, bf16[64,3584]{1,0:T(8,128)(2,1)S(1)}, u32[]{:S(2)}, u32[]{:S(2)}) %collective-permute-start.14) | collective-permute-done | bytes 458784 | tf_op jit(solution)/shard_map/ppermute | solution.py:374
  74.9 7.8 %collective-permute-done.19.refs_1_ = bf16[64,3584]{1,0:T(8,128)(2,1)S(1)} collective-permute-done((bf16[64,3584]{1,0:T(8,128)(2,1)S(1)}, bf16[64,3584]{1,0:T(8,128)(2,1)S(1)}, u32[]{:S(2)}, u32[]{:S(2)}) %collective-permute-start.19) | collective-permute-done | bytes 458784 | tf_op jit(solution)/shard_map/ppermute | solution.py:374
  83.5 1.7 %collective-permute-start.17 = (bf16[32,3584]{1,0:T(8,128)(2,1)S(1)}, bf16[32,3584]{1,0:T(8,128)(2,1)S(1)}, u32[]{:S(2)}, u32[]{:S(2)}) collective-permute-start(bf16[32,3584]{1,0:T(8,128)(2,1)S(1)} %get-tuple-element.134), channel_id=1, source_target_pairs={{0,16},{4,20},{8,24},{12,28},{16,0},{20,4},{24,8},{28,12},{1,17},{... | collective-permute-start | bytes 688136 | tf_op jit(solution)/shard_map/ppermute | solution.py:374
  85.1 1.7 %collective-permute-start.21 = (bf16[32,3584]{1,0:T(8,128)(2,1)S(1)}, bf16[32,3584]{1,0:T(8,128)(2,1)S(1)}, u32[]{:S(2)}, u32[]{:S(2)}) collective-permute-start(bf16[32,3584]{1,0:T(8,128)(2,1)S(1)} %get-tuple-element.145), channel_id=1, source_target_pairs={{0,8},{4,12},{8,0},{12,4},{16,24},{20,28},{24,16},{28,20},{1,9},{5... | collective-permute-start | bytes 688136 | tf_op jit(solution)/shard_map/ppermute | solution.py:374
  86.9 4.2 %collective-permute-done.17.refs_1_ = bf16[32,3584]{1,0:T(8,128)(2,1)S(1)} collective-permute-done((bf16[32,3584]{1,0:T(8,128)(2,1)S(1)}, bf16[32,3584]{1,0:T(8,128)(2,1)S(1)}, u32[]{:S(2)}, u32[]{:S(2)}) %collective-permute-start.17) | collective-permute-done | bytes 229408 | tf_op jit(solution)/shard_map/ppermute | solution.py:374
  92.1 1.7 %collective-permute-start.23 = (bf16[32,3584]{1,0:T(8,128)(2,1)S(1)}, bf16[32,3584]{1,0:T(8,128)(2,1)S(1)}, u32[]{:S(2)}, u32[]{:S(2)}) collective-permute-start(bf16[32,3584]{1,0:T(8,128)(2,1)S(1)} %get-tuple-element.149.refs_0_), channel_id=1, source_target_pairs={{0,16},{4,20},{8,24},{12,28},{16,0},{20,4},{24,8},{28,12},{1,17},{... | collective-permute-start | bytes 688136 | tf_op jit(solution)/shard_map/ppermute | solution.py:374
  94.9 1.7 %collective-permute-start.22 = (bf16[32,3584]{1,0:T(8,128)(2,1)S(1)}, bf16[32,3584]{1,0:T(8,128)(2,1)S(1)}, u32[]{:S(2)}, u32[]{:S(2)}) collective-permute-start(bf16[32,3584]{1,0:T(8,128)(2,1)S(1)} %get-tuple-element.148.refs_0_), channel_id=1, source_target_pairs={{0,8},{4,12},{8,0},{12,4},{16,24},{20,28},{24,16},{28,20},{1,9},{5... | collective-permute-start | bytes 688136 | tf_op jit(solution)/shard_map/ppermute | solution.py:374
  96.6 2.2 %collective-permute-done.23.refs_1_ = bf16[32,3584]{1,0:T(8,128)(2,1)S(1)} collective-permute-done((bf16[32,3584]{1,0:T(8,128)(2,1)S(1)}, bf16[32,3584]{1,0:T(8,128)(2,1)S(1)}, u32[]{:S(2)}, u32[]{:S(2)}) %collective-permute-start.23) | collective-permute-done | bytes 229408 | tf_op jit(solution)/shard_map/ppermute | solution.py:374
  99.7 1.7 %collective-permute-start.28 = (bf16[64,3584]{1,0:T(8,128)(2,1)}, bf16[64,3584]{1,0:T(8,128)(2,1)}, u32[]{:S(2)}, u32[]{:S(2)}) collective-permute-start(bf16[64,3584]{1,0:T(8,128)(2,1)} %get-tuple-element.162.refs_0_), channel_id=1, source_target_pairs={{0,8},{4,12},{8,0},{12,4},{16,24},{20,28},{24,16},{28,20},{1,9},{5... | collective-permute-start | bytes 1376264 | tf_op jit(solution)/shard_map/ppermute | solution.py:374
  108.5 5.2 %copy-done.1 = bf16[1024,7168]{1,0:T(8,128)(2,1)S(1)} copy-done((bf16[1024,7168]{1,0:T(8,128)(2,1)S(1)}, bf16[1024,7168]{1,0:T(8,128)(2,1)}, u32[]{:S(2)}) %copy-start.1) | copy-done | bytes 14680088
  113.6 5.6 %input_partial.2 = (f32[128,1024]{1,0:T(8,128)S(1)}, bf16[128,1024]{1,0:T(8,128)(2,1)S(1)}, f32[8,128]{1,0:T(8,128)S(1)}) custom-call(s32[8]{0:T(128)S(1)} %reshape.39.refs_0_, bf16[128,3584]{1,0:T(8,128)(2,1)S(1)} %get-tuple-element.154.refs_1_.refs_3_, bf16[128,3584]{1,0:T(8,128)(2,1)} %collective-permute-done.24.refs_2_.refs_4_, ...), custom_call_target="tpu_custom_call" | custom-call | flops 1 | bytes 1 | tf_op jit(solution)/shard_map/input_partial/pallas_call | solution.py:58
  119.3 6.4 %collective-permute-done.26.refs_1_ = bf16[128,1024]{1,0:T(8,128)(2,1)S(1)} collective-permute-done((bf16[128,1024]{1,0:T(8,128)(2,1)S(1)}, bf16[128,1024]{1,0:T(8,128)(2,1)S(1)}, u32[]{:S(2)}, u32[]{:S(2)}) %collective-permute-start.26) | collective-permute-done | bytes 262176 | tf_op jit(solution)/shard_map/ppermute | solution.py:374
  132.1 5.2 %copy-done.2 = bf16[1024,7168]{1,0:T(8,128)(2,1)S(1)} copy-done((bf16[1024,7168]{1,0:T(8,128)(2,1)S(1)}, bf16[1024,7168]{1,0:T(8,128)(2,1)}, u32[]{:S(2)}) %copy-start.2) | copy-done | bytes 14680088
  137.3 4.8 %input_partial.3 = (f32[64,1024]{1,0:T(8,128)S(1)}, bf16[64,1024]{1,0:T(8,128)(2,1)S(1)}, bf16[64,1024]{1,0:T(8,128)(2,1)S(1)}, bf16[64,1024]{1,0:T(8,128)(2,1)S(1)}, f32[8,128]{1,0:T(8,128)S(1)}) custom-call(s32[8]{0:T(128)S(1)} %shift-right-arithmetic_add_fusion.refs_3_.refs_0_, bf16[128,3584]{1,0:T(8,128)(2,1)S(1)} %get-tuple-element.164.refs_1_.refs_5_, ...), custom_call_target="tpu_custom_call" | custom-call | flops 1 | bytes 1 | tf_op jit(solution)/shard_map/input_partial/pallas_call | solution.py:58
  142.1 2.4 %collective-permute-start.33 = (bf16[64,1024]{1,0:T(8,128)(2,1)S(1)}, bf16[64,1024]{1,0:T(8,128)(2,1)S(1)}, u32[]{:S(2)}, u32[]{:S(2)}) collective-permute-start(bf16[64,1024]{1,0:T(8,128)(2,1)S(1)} %get-tuple-element.171), channel_id=1, source_target_pairs={{0,2},{1,3},{2,0},{3,1},{4,6},{5,7},{6,4},{7,5},{8,10},{9,11},{10,... | collective-permute-start | bytes 393224 | tf_op jit(solution)/shard_map/ppermute | solution.py:374
  144.6 2.0 %collective-permute-start.34 = (bf16[64,1024]{1,0:T(8,128)(2,1)S(1)}, bf16[64,1024]{1,0:T(8,128)(2,1)S(1)}, u32[]{:S(2)}, u32[]{:S(2)}) collective-permute-start(bf16[64,1024]{1,0:T(8,128)(2,1)S(1)} %get-tuple-element.172), channel_id=1, source_target_pairs={{0,3},{1,2},{2,1},{3,0},{4,7},{5,6},{6,5},{7,4},{8,11},{9,10},{10,... | collective-permute-start | bytes 393224 | tf_op jit(solution)/shard_map/ppermute | solution.py:374
  146.5 9.7 %weight_gradient.1 = (bf16[1,1,448,128,128]{4,3,2,1,0:T(8,128)(2,1)}, f32[8,128]{1,0:T(8,128)S(1)}) custom-call(s32[448]{0:T(512)S(1)} %select_reduce_fusion.refs_0_, bf16[1024,256]{1,0:T(8,128)(2,1)S(1)} %get-tuple-element.173.refs_1_, bf16[1024,256]{1,0:T(8,128)(2,1)S(1)} %copy-done.5, bf16[128,3584]{1,0:T(8,128)(2,1)S(1)} %get-tuple-element.154.refs_1_.refs_3_, ...), custom_call_target="tpu_custom_call" | custom-call | flops 1 | bytes 1 | tf_op jit(solution)/shard_map/weight_gradient/pallas_call | solution.py:58
  (107 shorter events, 35.3 us)
Async XLA Ops:
  1.6 15.8 %collective-permute-start.2 = (bf16[2,32,1024]{2,1,0:T(8,128)(2,1)S(1)}, bf16[2,32,1024]{2,1,0:T(8,128)(2,1)S(1)}, u32[]{:S(2)}, u32[]{:S(2)}) collective-permute-start(bf16[2,32,1024]{2,1,0:T(8,128)(2,1)S(1)} %get-tuple-element.180.refs_1_), channel_id=1, source_target_pairs={{0,3},{1,2},{2,1},{3,0},{4,7},{5,6},{6,5},{7,4},{8,11},{9,10},{10,... | collective-permute-start | bytes 393224 | tf_op jit(solution)/shard_map/ppermute | solution.py:374
  6.7 11.1 %collective-permute-start.1 = (bf16[2,32,1024]{2,1,0:T(8,128)(2,1)S(1)}, bf16[2,32,1024]{2,1,0:T(8,128)(2,1)S(1)}, u32[]{:S(2)}, u32[]{:S(2)}) collective-permute-start(bf16[2,32,1024]{2,1,0:T(8,128)(2,1)S(1)} %get-tuple-element.180.refs_1_), channel_id=1, source_target_pairs={{0,2},{1,3},{2,0},{3,1},{4,6},{5,7},{6,4},{7,5},{8,10},{9,11},{10,... | collective-permute-start | bytes 393224 | tf_op jit(solution)/shard_map/ppermute | solution.py:374
  6.7 11.1 %collective-permute-start = (bf16[2,32,1024]{2,1,0:T(8,128)(2,1)S(1)}, bf16[2,32,1024]{2,1,0:T(8,128)(2,1)S(1)}, u32[]{:S(2)}, u32[]{:S(2)}) collective-permute-start(bf16[2,32,1024]{2,1,0:T(8,128)(2,1)S(1)} %get-tuple-element.180.refs_1_), channel_id=1, source_target_pairs={{0,1},{1,0},{2,3},{3,2},{4,5},{5,4},{6,7},{7,6},{8,9},{9,8},{10,11... | collective-permute-start | bytes 393224 | tf_op jit(solution)/shard_map/ppermute | solution.py:374
  23.6 12.5 %collective-permute-start.4 = (bf16[64,3584]{1,0:T(8,128)(2,1)S(1)}, bf16[64,3584]{1,0:T(8,128)(2,1)S(1)}, u32[]{:S(2)}, u32[]{:S(2)}) collective-permute-start(bf16[64,3584]{1,0:T(8,128)(2,1)S(1)} %get-tuple-element.100), channel_id=1, source_target_pairs={{0,8},{4,12},{8,0},{12,4},{16,24},{20,28},{24,16},{28,20},{1,9},{5... | collective-permute-start | bytes 1376264 | tf_op jit(solution)/shard_map/ppermute | solution.py:374
  25.7 12.9 %collective-permute-start.10 = (bf16[64,3584]{1,0:T(8,128)(2,1)S(1)}, bf16[64,3584]{1,0:T(8,128)(2,1)S(1)}, u32[]{:S(2)}, u32[]{:S(2)}) collective-permute-start(bf16[64,3584]{1,0:T(8,128)(2,1)S(1)} %get-tuple-element.108), channel_id=1, source_target_pairs={{0,16},{4,20},{8,24},{12,28},{16,0},{20,4},{24,8},{28,12},{1,17},{... | collective-permute-start | bytes 1376264 | tf_op jit(solution)/shard_map/ppermute | solution.py:374
  27.3 11.3 %collective-permute-start.9 = (bf16[2,32,1024]{2,1,0:T(8,128)(2,1)S(1)}, bf16[2,32,1024]{2,1,0:T(8,128)(2,1)S(1)}, u32[]{:S(2)}, u32[]{:S(2)}) collective-permute-start(bf16[2,32,1024]{2,1,0:T(8,128)(2,1)S(1)} %get-tuple-element.179.refs_1_), channel_id=1, source_target_pairs={{0,3},{1,2},{2,1},{3,0},{4,7},{5,6},{6,5},{7,4},{8,11},{9,10},{10,... | collective-permute-start | bytes 393224 | tf_op jit(solution)/shard_map/ppermute | solution.py:374
  30.5 10.8 %collective-permute-start.8 = (bf16[2,32,1024]{2,1,0:T(8,128)(2,1)S(1)}, bf16[2,32,1024]{2,1,0:T(8,128)(2,1)S(1)}, u32[]{:S(2)}, u32[]{:S(2)}) collective-permute-start(bf16[2,32,1024]{2,1,0:T(8,128)(2,1)S(1)} %get-tuple-element.179.refs_1_), channel_id=1, source_target_pairs={{0,2},{1,3},{2,0},{3,1},{4,6},{5,7},{6,4},{7,5},{8,10},{9,11},{10,... | collective-permute-start | bytes 393224 | tf_op jit(solution)/shard_map/ppermute | solution.py:374
  30.5 10.8 %collective-permute-start.7 = (bf16[2,32,1024]{2,1,0:T(8,128)(2,1)S(1)}, bf16[2,32,1024]{2,1,0:T(8,128)(2,1)S(1)}, u32[]{:S(2)}, u32[]{:S(2)}) collective-permute-start(bf16[2,32,1024]{2,1,0:T(8,128)(2,1)S(1)} %get-tuple-element.179.refs_1_), channel_id=1, source_target_pairs={{0,1},{1,0},{2,3},{3,2},{4,5},{5,4},{6,7},{7,6},{8,9},{9,8},{10,11... | collective-permute-start | bytes 393224 | tf_op jit(solution)/shard_map/ppermute | solution.py:374
  44.1 5.1 %collective-permute-start.12 = (bf16[128,3584]{1,0:T(8,128)(2,1)S(1)}, bf16[128,3584]{1,0:T(8,128)(2,1)S(1)}, u32[]{:S(2)}, u32[]{:S(2)}) collective-permute-start(bf16[128,3584]{1,0:T(8,128)(2,1)S(1)} %get-tuple-element.117), channel_id=1, source_target_pairs={{0,4},{4,0},{8,12},{12,8},{16,20},{20,16},{24,28},{28,24},{1,5},{5... | collective-permute-start | bytes 2752520 | tf_op jit(solution)/shard_map/ppermute | solution.py:374
  46.3 3.1 %collective-permute-start.11 = (bf16[128,3584]{1,0:T(8,128)(2,1)S(1)}, bf16[128,3584]{1,0:T(8,128)(2,1)S(1)}, u32[]{:S(2)}, u32[]{:S(2)}) collective-permute-start(bf16[128,3584]{1,0:T(8,128)(2,1)S(1)} %get-tuple-element.115), channel_id=1, source_target_pairs={{0,4},{4,0},{8,12},{12,8},{16,20},{20,16},{24,28},{28,24},{1,5},{5... | collective-permute-start | bytes 2752520 | tf_op jit(solution)/shard_map/ppermute | solution.py:374
  46.8 7.6 %collective-permute-start.6 = (bf16[32,3584]{1,0:T(8,128)(2,1)S(1)}, bf16[32,3584]{1,0:T(8,128)(2,1)S(1)}, u32[]{:S(2)}, u32[]{:S(2)}) collective-permute-start(bf16[32,3584]{1,0:T(8,128)(2,1)S(1)} %get-tuple-element.106), channel_id=1, source_target_pairs={{0,16},{4,20},{8,24},{12,28},{16,0},{20,4},{24,8},{28,12},{1,17},{... | collective-permute-start | bytes 688136 | tf_op jit(solution)/shard_map/ppermute | solution.py:374
  47.2 8.1 %collective-permute-start.13 = (bf16[32,3584]{1,0:T(8,128)(2,1)S(1)}, bf16[32,3584]{1,0:T(8,128)(2,1)S(1)}, u32[]{:S(2)}, u32[]{:S(2)}) collective-permute-start(bf16[32,3584]{1,0:T(8,128)(2,1)S(1)} %get-tuple-element.123), channel_id=1, source_target_pairs={{0,8},{4,12},{8,0},{12,4},{16,24},{20,28},{24,16},{28,20},{1,9},{5... | collective-permute-start | bytes 688136 | tf_op jit(solution)/shard_map/ppermute | solution.py:374
  54.8 8.6 %collective-permute-start.16 = (bf16[32,3584]{1,0:T(8,128)(2,1)S(1)}, bf16[32,3584]{1,0:T(8,128)(2,1)S(1)}, u32[]{:S(2)}, u32[]{:S(2)}) collective-permute-start(bf16[32,3584]{1,0:T(8,128)(2,1)S(1)} %get-tuple-element.129.refs_0_), channel_id=1, source_target_pairs={{0,16},{4,20},{8,24},{12,28},{16,0},{20,4},{24,8},{28,12},{1,17},{... | collective-permute-start | bytes 688136 | tf_op jit(solution)/shard_map/ppermute | solution.py:374
  56.3 9.2 %collective-permute-start.15 = (bf16[32,3584]{1,0:T(8,128)(2,1)S(1)}, bf16[32,3584]{1,0:T(8,128)(2,1)S(1)}, u32[]{:S(2)}, u32[]{:S(2)}) collective-permute-start(bf16[32,3584]{1,0:T(8,128)(2,1)S(1)} %get-tuple-element.128.refs_0_), channel_id=1, source_target_pairs={{0,8},{4,12},{8,0},{12,4},{16,24},{20,28},{24,16},{28,20},{1,9},{5... | collective-permute-start | bytes 688136 | tf_op jit(solution)/shard_map/ppermute | solution.py:374
  58.3 16.4 %collective-permute-start.14 = (bf16[64,3584]{1,0:T(8,128)(2,1)S(1)}, bf16[64,3584]{1,0:T(8,128)(2,1)S(1)}, u32[]{:S(2)}, u32[]{:S(2)}) collective-permute-start(bf16[64,3584]{1,0:T(8,128)(2,1)S(1)} %get-tuple-element.127), channel_id=1, source_target_pairs={{0,8},{4,12},{8,0},{12,4},{16,24},{20,28},{24,16},{28,20},{1,9},{5... | collective-permute-start | bytes 1376264 | tf_op jit(solution)/shard_map/ppermute | solution.py:374
  58.4 16.4 %collective-permute-start.20 = (bf16[64,3584]{1,0:T(8,128)(2,1)S(1)}, bf16[64,3584]{1,0:T(8,128)(2,1)S(1)}, u32[]{:S(2)}, u32[]{:S(2)}) collective-permute-start(bf16[64,3584]{1,0:T(8,128)(2,1)S(1)} %get-tuple-element.138), channel_id=1, source_target_pairs={{0,16},{4,20},{8,24},{12,28},{16,0},{20,4},{24,8},{28,12},{1,17},{... | collective-permute-start | bytes 1376264 | tf_op jit(solution)/shard_map/ppermute | solution.py:374
  63.5 19.3 %collective-permute-start.19 = (bf16[64,3584]{1,0:T(8,128)(2,1)S(1)}, bf16[64,3584]{1,0:T(8,128)(2,1)S(1)}, u32[]{:S(2)}, u32[]{:S(2)}) collective-permute-start(bf16[64,3584]{1,0:T(8,128)(2,1)S(1)} %get-tuple-element.136.refs_0_), channel_id=1, source_target_pairs={{0,8},{4,12},{8,0},{12,4},{16,24},{20,28},{24,16},{28,20},{1,9},{5... | collective-permute-start | bytes 1376264 | tf_op jit(solution)/shard_map/ppermute | solution.py:374
  65.6 17.2 %collective-permute-start.18 = (bf16[64,3584]{1,0:T(8,128)(2,1)S(1)}, bf16[64,3584]{1,0:T(8,128)(2,1)S(1)}, u32[]{:S(2)}, u32[]{:S(2)}) collective-permute-start(bf16[64,3584]{1,0:T(8,128)(2,1)S(1)} %get-tuple-element.135.refs_0_), channel_id=1, source_target_pairs={{0,16},{4,20},{8,24},{12,28},{16,0},{20,4},{24,8},{28,12},{1,17},{... | collective-permute-start | bytes 1376264 | tf_op jit(solution)/shard_map/ppermute | solution.py:374
  82.9 25.6 %collective-permute-start.25 = (bf16[128,3584]{1,0:T(8,128)(2,1)S(1)}, bf16[128,3584]{1,0:T(8,128)(2,1)S(1)}, u32[]{:S(2)}, u32[]{:S(2)}) collective-permute-start(bf16[128,3584]{1,0:T(8,128)(2,1)S(1)} %get-tuple-element.155.refs_3_.refs_7_), channel_id=1, source_target_pairs={{0,4},{4,0},{8,12},{12,8},{16,20},{20,16},{24,28},{28,24},{1,5},{5... | collective-permute-start | bytes 2752520 | tf_op jit(solution)/shard_map/ppermute | solution.py:374
  83.0 25.5 %collective-permute-start.24 = (bf16[128,3584]{1,0:T(8,128)(2,1)S(1)}, bf16[128,3584]{1,0:T(8,128)(2,1)}, u32[]{:S(2)}, u32[]{:S(2)}) collective-permute-start(bf16[128,3584]{1,0:T(8,128)(2,1)S(1)} %get-tuple-element.154.refs_1_.refs_3_), channel_id=1, source_target_pairs={{0,4},{4,0},{8,12},{12,8},{16,20},{20,16},{24,28},{28,24},{1,5},{5... | collective-permute-start | bytes 2752520 | tf_op jit(solution)/shard_map/ppermute | solution.py:374
  83.5 7.6 %collective-permute-start.17 = (bf16[32,3584]{1,0:T(8,128)(2,1)S(1)}, bf16[32,3584]{1,0:T(8,128)(2,1)S(1)}, u32[]{:S(2)}, u32[]{:S(2)}) collective-permute-start(bf16[32,3584]{1,0:T(8,128)(2,1)S(1)} %get-tuple-element.134), channel_id=1, source_target_pairs={{0,16},{4,20},{8,24},{12,28},{16,0},{20,4},{24,8},{28,12},{1,17},{... | collective-permute-start | bytes 688136 | tf_op jit(solution)/shard_map/ppermute | solution.py:374
  85.1 8.7 %collective-permute-start.21 = (bf16[32,3584]{1,0:T(8,128)(2,1)S(1)}, bf16[32,3584]{1,0:T(8,128)(2,1)S(1)}, u32[]{:S(2)}, u32[]{:S(2)}) collective-permute-start(bf16[32,3584]{1,0:T(8,128)(2,1)S(1)} %get-tuple-element.145), channel_id=1, source_target_pairs={{0,8},{4,12},{8,0},{12,4},{16,24},{20,28},{24,16},{28,20},{1,9},{5... | collective-permute-start | bytes 688136 | tf_op jit(solution)/shard_map/ppermute | solution.py:374
  92.1 6.7 %collective-permute-start.23 = (bf16[32,3584]{1,0:T(8,128)(2,1)S(1)}, bf16[32,3584]{1,0:T(8,128)(2,1)S(1)}, u32[]{:S(2)}, u32[]{:S(2)}) collective-permute-start(bf16[32,3584]{1,0:T(8,128)(2,1)S(1)} %get-tuple-element.149.refs_0_), channel_id=1, source_target_pairs={{0,16},{4,20},{8,24},{12,28},{16,0},{20,4},{24,8},{28,12},{1,17},{... | collective-permute-start | bytes 688136 | tf_op jit(solution)/shard_map/ppermute | solution.py:374
  94.9 6.9 %collective-permute-start.22 = (bf16[32,3584]{1,0:T(8,128)(2,1)S(1)}, bf16[32,3584]{1,0:T(8,128)(2,1)S(1)}, u32[]{:S(2)}, u32[]{:S(2)}) collective-permute-start(bf16[32,3584]{1,0:T(8,128)(2,1)S(1)} %get-tuple-element.148.refs_0_), channel_id=1, source_target_pairs={{0,8},{4,12},{8,0},{12,4},{16,24},{20,28},{24,16},{28,20},{1,9},{5... | collective-permute-start | bytes 688136 | tf_op jit(solution)/shard_map/ppermute | solution.py:374
  99.7 26.1 %collective-permute-start.28 = (bf16[64,3584]{1,0:T(8,128)(2,1)}, bf16[64,3584]{1,0:T(8,128)(2,1)}, u32[]{:S(2)}, u32[]{:S(2)}) collective-permute-start(bf16[64,3584]{1,0:T(8,128)(2,1)} %get-tuple-element.162.refs_0_), channel_id=1, source_target_pairs={{0,8},{4,12},{8,0},{12,4},{16,24},{20,28},{24,16},{28,20},{1,9},{5... | collective-permute-start | bytes 1376264 | tf_op jit(solution)/shard_map/ppermute | solution.py:374
  102.7 24.4 %collective-permute-start.30 = (bf16[64,3584]{1,0:T(8,128)(2,1)}, bf16[64,3584]{1,0:T(8,128)(2,1)}, u32[]{:S(2)}, u32[]{:S(2)}) collective-permute-start(bf16[64,3584]{1,0:T(8,128)(2,1)} %get-tuple-element.165.refs_0_), channel_id=1, source_target_pairs={{0,16},{4,20},{8,24},{12,28},{16,0},{20,4},{24,8},{28,12},{1,17},{... | collective-permute-start | bytes 1376264 | tf_op jit(solution)/shard_map/ppermute | solution.py:374
  119.3 6.4 %collective-permute-start.26 = (bf16[128,1024]{1,0:T(8,128)(2,1)S(1)}, bf16[128,1024]{1,0:T(8,128)(2,1)S(1)}, u32[]{:S(2)}, u32[]{:S(2)}) collective-permute-start(bf16[128,1024]{1,0:T(8,128)(2,1)S(1)} %get-tuple-element.158), channel_id=1, source_target_pairs={{0,1},{1,0},{2,3},{3,2},{4,5},{5,4},{6,7},{7,6},{8,9},{9,8},{10,11... | collective-permute-start | bytes 786440 | tf_op jit(solution)/shard_map/ppermute | solution.py:374
  128.3 3.8 %collective-permute-start.29 = (bf16[128,3584]{1,0:T(8,128)(2,1)S(1)}, bf16[128,3584]{1,0:T(8,128)(2,1)S(1)}, u32[]{:S(2)}, u32[]{:S(2)}) collective-permute-start(bf16[128,3584]{1,0:T(8,128)(2,1)S(1)} %get-tuple-element.164.refs_1_.refs_5_), channel_id=1, source_target_pairs={{0,4},{4,0},{8,12},{12,8},{16,20},{20,16},{24,28},{28,24},{1,5},{5... | collective-permute-start | bytes 2752520 | tf_op jit(solution)/shard_map/ppermute | solution.py:374
  128.8 27.4 %collective-permute-start.27 = (bf16[64,1024]{1,0:T(8,128)(2,1)S(1)}, bf16[64,1024]{1,0:T(8,128)(2,1)S(1)}, u32[]{:S(2)}, u32[]{:S(2)}) collective-permute-start(bf16[64,1024]{1,0:T(8,128)(2,1)S(1)} %get-tuple-element.161), channel_id=1, source_target_pairs={{0,2},{1,3},{2,0},{3,1},{4,6},{5,7},{6,4},{7,5},{8,10},{9,11},{10,... | collective-permute-start | bytes 393224 | tf_op jit(solution)/shard_map/ppermute | solution.py:374
  142.1 14.2 %collective-permute-start.32 = (bf16[64,1024]{1,0:T(8,128)(2,1)S(1)}, bf16[64,1024]{1,0:T(8,128)(2,1)S(1)}, u32[]{:S(2)}, u32[]{:S(2)}) collective-permute-start(bf16[64,1024]{1,0:T(8,128)(2,1)S(1)} %get-tuple-element.170), channel_id=1, source_target_pairs={{0,1},{1,0},{2,3},{3,2},{4,5},{5,4},{6,7},{7,6},{8,9},{9,8},{10,11... | collective-permute-start | bytes 393224 | tf_op jit(solution)/shard_map/ppermute | solution.py:374
  142.1 14.1 %collective-permute-start.33 = (bf16[64,1024]{1,0:T(8,128)(2,1)S(1)}, bf16[64,1024]{1,0:T(8,128)(2,1)S(1)}, u32[]{:S(2)}, u32[]{:S(2)}) collective-permute-start(bf16[64,1024]{1,0:T(8,128)(2,1)S(1)} %get-tuple-element.171), channel_id=1, source_target_pairs={{0,2},{1,3},{2,0},{3,1},{4,6},{5,7},{6,4},{7,5},{8,10},{9,11},{10,... | collective-permute-start | bytes 393224 | tf_op jit(solution)/shard_map/ppermute | solution.py:374
  144.6 11.7 %collective-permute-start.34 = (bf16[64,1024]{1,0:T(8,128)(2,1)S(1)}, bf16[64,1024]{1,0:T(8,128)(2,1)S(1)}, u32[]{:S(2)}, u32[]{:S(2)}) collective-permute-start(bf16[64,1024]{1,0:T(8,128)(2,1)S(1)} %get-tuple-element.172), channel_id=1, source_target_pairs={{0,3},{1,2},{2,1},{3,0},{4,7},{5,6},{6,5},{7,4},{8,11},{9,10},{10,... | collective-permute-start | bytes 393224 | tf_op jit(solution)/shard_map/ppermute | solution.py:374
  (16 other events, 79.2 us)
